TPU v7x, 32 devices: a whole 2x2x4 slice. The times are simulated.
32 devices in a mesh: dp: 8 (over y, x, core), fsdp: 4 (over z).
Axes of the slice: x: 2, y: 2, z: 4, core: 2. Of those that a mesh axis runs over, the one named last changes fastest.
Arguments:
- tokens: bfloat16 [32, 1024, 768], P(('dp', 'fsdp')), may hold values from -6 to 6
- w_qkv: bfloat16 [768, 2304], P(('dp', 'fsdp')), may hold values from -0.21875 to 0.21875
- b_qkv: bfloat16 [2304], P(('dp', 'fsdp')), may hold values from -2 to 2
- conv_kv: bfloat16 [5, 1536], P(None, ('dp', 'fsdp')), may hold values from -0.19921875 to 0.59765625
- w_out: bfloat16 [768, 768], P(None, ('dp', 'fsdp')), may hold values from -1.75 to 1.75
- b_out: bfloat16 [768], P(('dp', 'fsdp')), may hold values from -2 to 2
- gain_one: bfloat16 [768], P(('dp', 'fsdp')), may hold values from 0.5 to 1.5
- shift_one: bfloat16 [768], P(('dp', 'fsdp')), may hold values from -2 to 2
- w_up: bfloat16 [768, 3072], P(('dp', 'fsdp')), may hold values from -0.21875 to 0.21875
- b_up: bfloat16 [3072], P(('dp', 'fsdp')), may hold values from -2 to 2
- w_down: bfloat16 [3072, 768], P(None, ('dp', 'fsdp')), may hold values from -0.109375 to 0.109375
- b_down: bfloat16 [768], P(('dp', 'fsdp')), may hold values from -2 to 2
- gain_two: bfloat16 [768], P(('dp', 'fsdp')), may hold values from 0.5 to 1.5
- shift_two: bfloat16 [768], P(('dp', 'fsdp')), may hold values from -2 to 2
- positions: int32 [32, 160], P(('dp', 'fsdp')), may hold values from 0 to 1024, as said below
- cotangent: bfloat16 [32, 160, 768], P(('dp', 'fsdp')), may hold values from -6 to 6
Outputs:
- layer_out: bfloat16 [32, 1024, 768], P(('dp', 'fsdp'))
- grad_tokens: float32 [32, 1024, 768], P(('dp', 'fsdp'))
- grad_qkv: float32 [768, 2304], P(('dp', 'fsdp'))
- grad_qkvbias: float32 [2304], P(('dp', 'fsdp'))
- grad_conv: float32 [5, 1536], P(None, ('dp', 'fsdp'))
- grad_wout: float32 [768, 768], P(None, ('dp', 'fsdp'))
- grad_bout: float32 [768], P(('dp', 'fsdp'))
- grad_gainone: float32 [768], P(('dp', 'fsdp'))
- grad_shiftone: float32 [768], P(('dp', 'fsdp'))
- grad_wup: float32 [768, 3072], P(('dp', 'fsdp'))
- grad_bup: float32 [3072], P(('dp', 'fsdp'))
- grad_wdown: float32 [3072, 768], P(None, ('dp', 'fsdp'))
- grad_bdown: float32 [768], P(('dp', 'fsdp'))
- grad_gaintwo: float32 [768], P(('dp', 'fsdp'))
- grad_shifttwo: float32 [768], P(('dp', 'fsdp'))
Inputs may be any that keep to these rules, and one draw needn't show every extreme that they name: Each row lists distinct token positions of its item in no particular order, followed by the value 1024 in its unused slots; a row holds at least 120 positions, and some row holds 160.
All inputs are finite; a program needn't handle non-finite values.
Results may differ from a plain program's by a relative error of at most 0.013.
Values may be sent and summed in bfloat16 or wider, within the bound.
A program may use at most 256 MiB of HBM per device.

v0:
```python
import jax
import jax.numpy as jnp
from jax import lax
from jax.sharding import PartitionSpec as P

D = 768
HEADS = 12
HEAD_DIM = 64
SEQ = 1024
WIN = 128
POOL_WIN = 512
STRIDE = 4
KERNEL = 5


def layer_norm(values, norm_gain, norm_shift):
    average = jnp.mean(values, axis=-1, keepdims=True)
    centred = values - average
    variance = jnp.mean(centred * centred, axis=-1, keepdims=True)
    return centred * lax.rsqrt(variance + 1e-05) * norm_gain + norm_shift


def norm_back(values, norm_gain, norm_shift, incoming):
    unused, pullback = jax.vjp(layer_norm, values, norm_gain, norm_shift)
    return pullback(incoming)


def window_mask(first_row, block_rows):
    near_half = WIN // 2
    far_half = POOL_WIN // 2
    query_pos = first_row + jnp.arange(block_rows, dtype=jnp.int32)
    key_pos = first_row - near_half + jnp.arange(block_rows + 2 * near_half, dtype=jnp.int32)
    nearby = (
        (jnp.abs(query_pos[:, None] - key_pos[None, :]) <= near_half)
        & (key_pos[None, :] >= 0)
        & (key_pos[None, :] < SEQ)
    )
    pool_slot = (
        first_row // STRIDE
        - far_half // STRIDE
        + jnp.arange((block_rows + 2 * far_half) // STRIDE, dtype=jnp.int32)
    )
    distant = (
        (jnp.abs(query_pos[:, None] - STRIDE * pool_slot[None, :]) <= far_half)
        & (pool_slot[None, :] >= 0)
        & (pool_slot[None, :] < SEQ // STRIDE)
    )
    return jnp.concatenate([nearby, distant], axis=1)


def pool_window(values, taps):
    half_kernel = KERNEL // 2
    padded = jnp.pad(values, ((half_kernel, half_kernel), (0, 0)))
    pool_count = SEQ // STRIDE
    summed = jnp.zeros((pool_count, values.shape[1]), jnp.float32)
    for tap_index in range(KERNEL):
        summed = (
            summed + taps[tap_index] * padded[tap_index : tap_index + STRIDE * pool_count : STRIDE]
        )
    return summed


def block_operands(first_row, block_rows, kv_pad, pooled_pad):
    near_span = block_rows + 2 * (WIN // 2)
    far_span = (block_rows + 2 * (POOL_WIN // 2)) // STRIDE
    nearby = kv_pad[first_row : first_row + near_span]
    distant = pooled_pad[first_row // STRIDE : first_row // STRIDE + far_span]
    keys_all = jnp.concatenate([nearby[:, :D], distant[:, :D]], 0).reshape(-1, HEADS, HEAD_DIM)
    values_all = jnp.concatenate([nearby[:, D:], distant[:, D:]], 0).reshape(-1, HEADS, HEAD_DIM)
    return (keys_all, values_all)


def block_scores(first_row, heads_q, keys_all):
    scores = jnp.einsum(
        "qhd,khd->hqk", heads_q, keys_all, preferred_element_type=jnp.float32
    ) * HEAD_DIM ** (-0.5)
    allowed = window_mask(first_row, heads_q.shape[0])
    return jnp.where(allowed[None], scores, -1e30)


def feed_back(
    incoming, pre_two, first_low, hidden_pre, active, up_all, down_all, gain_second, shift_second
):
    d_pre_two, grad_gaintwo, grad_shifttwo = norm_back(pre_two, gain_second, shift_second, incoming)
    d_branch = d_pre_two.astype(jnp.bfloat16)
    grad_wdown = jnp.einsum("sf,sd->fd", active, d_branch, preferred_element_type=jnp.float32)
    grad_bdown = jnp.sum(d_branch.astype(jnp.float32), axis=0)
    d_active = jnp.einsum("sd,fd->sf", d_branch, down_all, preferred_element_type=jnp.float32)
    unused, gelu_pull = jax.vjp(jax.nn.gelu, hidden_pre)
    d_hidden = gelu_pull(d_active)[0].astype(jnp.bfloat16)
    grad_wup = jnp.einsum("sd,sf->df", first_low, d_hidden, preferred_element_type=jnp.float32)
    grad_bup = jnp.sum(d_hidden.astype(jnp.float32), axis=0)
    d_first = d_pre_two + jnp.einsum(
        "sf,df->sd", d_hidden, up_all, preferred_element_type=jnp.float32
    )
    return (d_first, (grad_wup, grad_bup, grad_wdown, grad_bdown, grad_gaintwo, grad_shifttwo))


def shards(
    tokens,
    w_qkv,
    b_qkv,
    conv_kv,
    w_out,
    b_out,
    gain_one,
    shift_one,
    w_up,
    b_up,
    w_down,
    b_down,
    gain_two,
    shift_two,
    positions,
    cotangent,
):
    attn_set = (
        lax.all_gather(w_qkv, ("dp", "fsdp"), axis=0, tiled=True),
        lax.all_gather(b_qkv, ("dp", "fsdp"), axis=0, tiled=True),
        lax.all_gather(conv_kv, ("dp", "fsdp"), axis=1, tiled=True),
        lax.all_gather(w_out, ("dp", "fsdp"), axis=1, tiled=True),
        lax.all_gather(b_out, ("dp", "fsdp"), axis=0, tiled=True),
        lax.all_gather(gain_one, ("dp", "fsdp"), axis=0, tiled=True),
        lax.all_gather(shift_one, ("dp", "fsdp"), axis=0, tiled=True),
    )
    feed_set = (
        lax.all_gather(w_up, ("dp", "fsdp"), axis=0, tiled=True),
        lax.all_gather(b_up, ("dp", "fsdp"), axis=0, tiled=True),
        lax.all_gather(w_down, ("dp", "fsdp"), axis=1, tiled=True),
        lax.all_gather(b_down, ("dp", "fsdp"), axis=0, tiled=True),
        lax.all_gather(gain_two, ("dp", "fsdp"), axis=0, tiled=True),
        lax.all_gather(shift_two, ("dp", "fsdp"), axis=0, tiled=True),
    )
    qkv_all, qkv_bias, conv_all, out_all, out_bias, gain_first, shift_first = attn_set
    up_all, up_bias, down_all, down_bias, gain_second, shift_second = feed_set
    sequence = tokens[0]
    near_half = WIN // 2
    far_half = POOL_WIN // 2 // STRIDE
    block_rows = min(512, SEQ)
    starts = list(range(0, SEQ, block_rows))
    scale = HEAD_DIM ** (-0.5)
    projected = jnp.dot(sequence, qkv_all, preferred_element_type=jnp.float32) + qkv_bias.astype(
        jnp.float32
    )
    mixed_low = projected.astype(jnp.bfloat16)
    kv_float = mixed_low[:, D:].astype(jnp.float32)
    pooled_low = pool_window(kv_float, conv_all.astype(jnp.float32)).astype(jnp.bfloat16)
    kv_pad = jnp.pad(mixed_low[:, D:], ((near_half, near_half), (0, 0)))
    pooled_pad = jnp.pad(pooled_low, ((far_half, far_half), (0, 0)))
    queries = mixed_low[:, :D].reshape(SEQ, HEADS, HEAD_DIM)
    contexts = []
    log_totals = []
    for first_row in starts:
        keys_all, values_all = block_operands(first_row, block_rows, kv_pad, pooled_pad)
        masked = block_scores(first_row, queries[first_row : first_row + block_rows], keys_all)
        row_peak = jnp.max(masked, axis=-1, keepdims=True)
        exponent = jnp.exp(masked - row_peak)
        summed = jnp.sum(exponent, axis=-1, keepdims=True)
        attn_probs = (exponent / summed).astype(jnp.bfloat16)
        contexts.append(
            jnp.einsum(
                "hqk,khd->qhd", attn_probs, values_all, preferred_element_type=jnp.float32
            ).reshape(block_rows, D)
        )
        log_totals.append(row_peak + jnp.log(summed))
    context_low = jnp.concatenate(contexts, 0).astype(jnp.bfloat16)
    pre_one = (
        sequence.astype(jnp.float32)
        + jnp.dot(context_low, out_all, preferred_element_type=jnp.float32)
        + out_bias.astype(jnp.float32)
    )
    first_low = layer_norm(
        pre_one, gain_first.astype(jnp.float32), shift_first.astype(jnp.float32)
    ).astype(jnp.bfloat16)
    hidden_pre = jnp.dot(first_low, up_all, preferred_element_type=jnp.float32) + up_bias.astype(
        jnp.float32
    )
    active = jax.nn.gelu(hidden_pre).astype(jnp.bfloat16)
    pre_two = (
        first_low.astype(jnp.float32)
        + jnp.dot(active, down_all, preferred_element_type=jnp.float32)
        + down_bias.astype(jnp.float32)
    )
    layer_out = layer_norm(
        pre_two, gain_second.astype(jnp.float32), shift_second.astype(jnp.float32)
    ).astype(jnp.bfloat16)
    attn_back = (
        lax.all_gather(w_qkv, ("dp", "fsdp"), axis=0, tiled=True),
        lax.all_gather(b_qkv, ("dp", "fsdp"), axis=0, tiled=True),
        lax.all_gather(conv_kv, ("dp", "fsdp"), axis=1, tiled=True),
        lax.all_gather(w_out, ("dp", "fsdp"), axis=1, tiled=True),
        lax.all_gather(b_out, ("dp", "fsdp"), axis=0, tiled=True),
        lax.all_gather(gain_one, ("dp", "fsdp"), axis=0, tiled=True),
        lax.all_gather(shift_one, ("dp", "fsdp"), axis=0, tiled=True),
    )
    feed_again = (
        lax.all_gather(w_up, ("dp", "fsdp"), axis=0, tiled=True),
        lax.all_gather(b_up, ("dp", "fsdp"), axis=0, tiled=True),
        lax.all_gather(w_down, ("dp", "fsdp"), axis=1, tiled=True),
        lax.all_gather(b_down, ("dp", "fsdp"), axis=0, tiled=True),
        lax.all_gather(gain_two, ("dp", "fsdp"), axis=0, tiled=True),
        lax.all_gather(shift_two, ("dp", "fsdp"), axis=0, tiled=True),
    )
    qkv_back, unused_bias, conv_back, out_back, unused_outb, gainone_back, shiftone_back = attn_back
    up_back, unused_upb, down_back, unused_downb, gaintwo_back, shifttwo_back = feed_again
    gainone_f = gainone_back.astype(jnp.float32)
    shiftone_f = shiftone_back.astype(jnp.float32)
    present = positions[0] < SEQ
    clipped = jnp.minimum(positions[0], SEQ - 1)
    picked = cotangent[0].astype(jnp.float32) * present[:, None].astype(jnp.float32)
    grad_dense = jnp.zeros((SEQ, D), jnp.float32).at[clipped].add(picked)
    d_first, feed_grads = feed_back(
        grad_dense,
        pre_two,
        first_low,
        hidden_pre,
        active,
        up_back,
        down_back,
        gaintwo_back.astype(jnp.float32),
        shifttwo_back.astype(jnp.float32),
    )
    d_pre_one, grad_gainone, grad_shiftone = norm_back(pre_one, gainone_f, shiftone_f, d_first)
    feed_shards = (
        lax.psum_scatter(feed_grads[0], ("dp", "fsdp"), scatter_dimension=0, tiled=True),
        lax.psum_scatter(feed_grads[1], ("dp", "fsdp"), scatter_dimension=0, tiled=True),
        lax.psum_scatter(feed_grads[2], ("dp", "fsdp"), scatter_dimension=1, tiled=True),
        lax.psum_scatter(feed_grads[3], ("dp", "fsdp"), scatter_dimension=0, tiled=True),
        lax.psum_scatter(feed_grads[4], ("dp", "fsdp"), scatter_dimension=0, tiled=True),
        lax.psum_scatter(feed_grads[5], ("dp", "fsdp"), scatter_dimension=0, tiled=True),
    )
    d_attn = d_pre_one.astype(jnp.bfloat16)
    grad_wout = jnp.einsum("sc,sd->cd", context_low, d_attn, preferred_element_type=jnp.float32)
    grad_bout = jnp.sum(d_attn.astype(jnp.float32), axis=0)
    d_context = (
        jnp.einsum("sd,cd->sc", d_attn, out_back, preferred_element_type=jnp.float32)
        .astype(jnp.bfloat16)
        .reshape(SEQ, HEADS, HEAD_DIM)
    )
    kv_grad_pad = jnp.zeros((SEQ + 2 * near_half, 2 * D), jnp.float32)
    pooled_grad_pad = jnp.zeros((SEQ // STRIDE + 2 * far_half, 2 * D), jnp.float32)
    query_grads = []
    near_span = block_rows + 2 * near_half
    far_span = (block_rows + 2 * (POOL_WIN // 2)) // STRIDE
    for number, first_row in enumerate(starts):
        keys_all, values_all = block_operands(first_row, block_rows, kv_pad, pooled_pad)
        block_q = queries[first_row : first_row + block_rows]
        block_dc = d_context[first_row : first_row + block_rows]
        masked = block_scores(first_row, block_q, keys_all)
        attn_probs = jnp.exp(masked - log_totals[number])
        d_probs = jnp.einsum(
            "qhd,khd->hqk", block_dc, values_all, preferred_element_type=jnp.float32
        )
        row_dot = jnp.sum(attn_probs * d_probs, axis=-1, keepdims=True)
        d_scores = (attn_probs * (d_probs - row_dot)).astype(jnp.bfloat16)
        query_grads.append(
            jnp.einsum(
                "hqk,khd->qhd", d_scores, keys_all, preferred_element_type=jnp.float32
            ).reshape(block_rows, D)
            * scale
        )
        d_keys = (
            jnp.einsum(
                "hqk,qhd->khd", d_scores, block_q, preferred_element_type=jnp.float32
            ).reshape(-1, D)
            * scale
        )
        d_values = jnp.einsum(
            "hqk,qhd->khd",
            attn_probs.astype(jnp.bfloat16),
            block_dc,
            preferred_element_type=jnp.float32,
        ).reshape(-1, D)
        d_kv = jnp.concatenate([d_keys, d_values], axis=1)
        kv_grad_pad = kv_grad_pad.at[first_row : first_row + near_span].add(d_kv[:near_span])
        pooled_grad_pad = pooled_grad_pad.at[
            first_row // STRIDE : first_row // STRIDE + far_span
        ].add(d_kv[near_span:])
    pooled_grad = pooled_grad_pad[far_half : far_half + SEQ // STRIDE]
    half_kernel = KERNEL // 2
    pool_count = SEQ // STRIDE
    padded_kv = jnp.pad(kv_float, ((half_kernel, half_kernel), (0, 0)))
    taps_f = conv_back.astype(jnp.float32)
    grad_padded = jnp.zeros((SEQ + 2 * half_kernel, 2 * D), jnp.float32)
    tap_grads = []
    for tap_index in range(KERNEL):
        grad_padded = grad_padded.at[tap_index : tap_index + STRIDE * pool_count : STRIDE].add(
            taps_f[tap_index] * pooled_grad
        )
        tap_grads.append(
            jnp.sum(
                pooled_grad * padded_kv[tap_index : tap_index + STRIDE * pool_count : STRIDE],
                axis=0,
            )
        )
    grad_conv = jnp.stack(tap_grads, axis=0)
    kv_grad = (
        kv_grad_pad[near_half : near_half + SEQ] + grad_padded[half_kernel : half_kernel + SEQ]
    )
    d_projected = jnp.concatenate([jnp.concatenate(query_grads, 0), kv_grad], axis=1).astype(
        jnp.bfloat16
    )
    grad_qkv = jnp.einsum("sd,se->de", sequence, d_projected, preferred_element_type=jnp.float32)
    grad_qkvbias = jnp.sum(d_projected.astype(jnp.float32), axis=0)
    grad_tokens = d_pre_one + jnp.einsum(
        "se,de->sd", d_projected, qkv_back, preferred_element_type=jnp.float32
    )
    attn_terms = (
        grad_qkv,
        grad_qkvbias,
        grad_conv,
        grad_wout,
        grad_bout,
        grad_gainone,
        grad_shiftone,
    )
    attn_shards = (
        lax.psum_scatter(attn_terms[0], ("dp", "fsdp"), scatter_dimension=0, tiled=True),
        lax.psum_scatter(attn_terms[1], ("dp", "fsdp"), scatter_dimension=0, tiled=True),
        lax.psum_scatter(attn_terms[2], ("dp", "fsdp"), scatter_dimension=1, tiled=True),
        lax.psum_scatter(attn_terms[3], ("dp", "fsdp"), scatter_dimension=1, tiled=True),
        lax.psum_scatter(attn_terms[4], ("dp", "fsdp"), scatter_dimension=0, tiled=True),
        lax.psum_scatter(attn_terms[5], ("dp", "fsdp"), scatter_dimension=0, tiled=True),
        lax.psum_scatter(attn_terms[6], ("dp", "fsdp"), scatter_dimension=0, tiled=True),
    )
    return (
        layer_out[None],
        grad_tokens[None],
        attn_shards[0],
        attn_shards[1],
        attn_shards[2],
        attn_shards[3],
        attn_shards[4],
        attn_shards[5],
        attn_shards[6],
        feed_shards[0],
        feed_shards[1],
        feed_shards[2],
        feed_shards[3],
        feed_shards[4],
        feed_shards[5],
    )


def solution(mesh):
    placed = (
        P(("dp", "fsdp"), None, None),
        P(("dp", "fsdp"), None),
        P(("dp", "fsdp")),
        P(None, ("dp", "fsdp")),
        P(None, ("dp", "fsdp")),
        P(("dp", "fsdp")),
        P(("dp", "fsdp")),
        P(("dp", "fsdp")),
        P(("dp", "fsdp"), None),
        P(("dp", "fsdp")),
        P(None, ("dp", "fsdp")),
        P(("dp", "fsdp")),
        P(("dp", "fsdp")),
        P(("dp", "fsdp")),
        P(("dp", "fsdp"), None),
        P(("dp", "fsdp"), None, None),
    )
    return jax.shard_map(
        shards,
        mesh=mesh,
        in_specs=placed,
        out_specs=(
            P(("dp", "fsdp"), None, None),
            P(("dp", "fsdp"), None, None),
            P(("dp", "fsdp"), None),
            P(("dp", "fsdp")),
            P(None, ("dp", "fsdp")),
            P(None, ("dp", "fsdp")),
            P(("dp", "fsdp")),
            P(("dp", "fsdp")),
            P(("dp", "fsdp")),
            P(("dp", "fsdp"), None),
            P(("dp", "fsdp")),
            P(None, ("dp", "fsdp")),
            P(("dp", "fsdp")),
            P(("dp", "fsdp")),
            P(("dp", "fsdp")),
        ),
        check_vma=False,
    )
```

profile of v0, /device:TPU:0, one launch (start us, length us, event | category | flops | bytes accessed | tf_op | source)
XLA Modules:
  0.0 1079.1 jit_solution(17551161271776870353)
XLA Ops:
  23.7 42.8 %all-reduce.22 = (bf16[768]{0:T(1024)(128)(2,1)S(1)}, bf16[2304]{0:T(1024)(128)(2,1)S(1)}, bf16[768]{0:T(1024)(128)(2,1)S(1)}, bf16[768]{0:T(1024)(128)(2,1)S(1)...) all-reduce(bf16[768]{0:T(1024)(128)(2,1)S(1)} %dynamic-update-slice, ...), channel_id=1, replica_groups=mesh['dp'=8,'fsdp'=4] {'dp','fsdp'}, use_global_device_ids=true, to_apply=%add.6 | all-reduce | flops 9984 | bytes 39936
  68.4 66.8 %all-gather = bf16[32,48,5]{1,2,0:T(8,128)(2,1)S(1)} all-gather(bf16[1,48,5]{1,2,0:T(8,128)(2,1)} %bitcast.134), channel_id=1, replica_groups=mesh['dp'=8,'fsdp'=4] {'dp','fsdp'}, dimensions={0}, use_global_device_ids=true | all-gather | bytes 15840 | tf_op jit(solution)/shard_map/all_gather | solution.py:120
  245.1 12.4 %fusion.45 = bf16[12,64,512]{2,1,0:T(8,128)(2,1)} fusion(bf16[896,12,64]{0,2,1:T(8,128)(2,1)S(1)} %bitcast.119, f32[12,512]{1,0:T(8,128)S(1)} %fusion, f32[12,512]{1,0:T(8,128)S(1)} %get-tuple-element.177, f32[12,512,896]{2,1,0:T(8,128)} %copy-done, pred[512,896]{1,0:T(8,128)(4,1)S(1)} %copy-done.27), kind=kOutput, calls=%fused_computation.114 | convolution fusion | flops 732561408 | bytes 24690688 | tf_op jit(solution)/shard_map/hqk,khd->qhd/dot_general | solution.py:161
  257.4 11.8 %fusion.44 = bf16[12,64,512]{2,1,0:T(8,128)(2,1)} fusion(bf16[896,12,64]{0,2,1:T(8,128)(2,1)S(1)} %bitcast.121, f32[12,512]{1,0:T(8,128)S(1)} %fusion.1, f32[12,512]{1,0:T(8,128)S(1)} %get-tuple-element.175, f32[12,512,896]{2,1,0:T(8,128)} %copy-done.1, pred[512,896]{1,0:T(8,128)(4,1)S(1)} %copy-done.30), kind=kOutput, calls=%fused_computation.113 | convolution fusion | flops 732561408 | bytes 24690688 | tf_op jit(solution)/shard_map/hqk,khd->qhd/dot_general | solution.py:161
  274.4 10.6 fusion.97
  285.0 10.1 fusion.95
  305.4 15.3 %convert_reduce_fusion = (f32[3072]{0:T(1024)}, bf16[1024,3072]{1,0:T(8,128)(2,1)}) fusion(f32[1024,3072]{1,0:T(8,128)S(1)} %copy-done.19, f32[3072]{0:T(1024)S(1)} %copy-done.72, bf16[1024,768]{0,1:T(8,128)(2,1)S(1)} %get-tuple-element.155, bf16[3072,768]{0,1:T(8,128)(2,1)S(1)} %copy-done.85), kind=kOutput, calls=%fused_computation.31 | convolution fusion | flops 4904186880 | bytes 25190400 | tf_op jit(solution)/shard_map/sd,fd->sf/dot_general | solution.py:88
  320.7 10.8 %multiply_reduce_fusion.3 = (f32[768]{0:T(1024)}, f32[1024]{0:T(1024)S(1)}, f32[768]{0:T(1024)}, f32[1024,768]{0,1:T(8,128)S(1)}) fusion(f32[1024,768]{0,1:T(8,128)S(1)} %get-tuple-element.180, f32[1024]{0:T(1024)S(1)} %fusion.71, f32[1024]{0:T(1024)S(1)} %broadcast_multiply_fusion.1, f32[768]{0:T(1024)S(1)} %convert_element_type.128, ...), kind=kOutput, calls=%fused_computation.62 | convolution fusion | flops 4839699456 | bytes 20472832 | tf_op jit(solution)/shard_map/sf,df->sd/dot_general | solution.py:93
  348.0 16.5 %multiply_reduce_fusion = (f32[12,512]{1,0:T(8,128)}, f32[12,512,896]{2,1,0:T(8,128)}) fusion(f32[12,512]{1,0:T(8,128)S(1)} %log_add_fusion, f32[12,512,896]{2,1,0:T(8,128)} %copy-done.1, pred[512,896]{1,0:T(8,128)(4,1)S(1)} %copy-done.31, bf16[512,12,64]{0,2,1:T(8,128)(2,1)} %bitcast.128, bf16[896,12,64]{0,2,1:T(8,128)(2,1)} %bitcast.120), kind=kOutput, calls=%fused_computation.7 | convolution fusion | flops 732162048 | bytes 46710784 | tf_op jit(solution)/shard_map/qhd,khd->hqk/dot_general | solution.py:251
  364.6 20.6 %multiply_convert_fusion = bf16[12,512,896]{2,1,0:T(8,128)(2,1)} fusion(f32[12,512,896]{2,1,0:T(8,128)} %get-tuple-element.187, f32[12,512]{1,0:T(8,128)} %get-tuple-element.186, f32[12,512]{1,0:T(8,128)} %copy-done.55, f32[12,512,896]{2,1,0:T(8,128)} %copy-done.1, pred[512,896]{1,0:T(8,128)(4,1)} %pad_add_fusion.1), kind=kLoop, calls=%fused_computation.6 | loop fusion | flops 33030144 | bytes 55558144 | tf_op jit(solution)/shard_map/convert_element_type | solution.py:255
  385.1 9.4 multiply_convert_fusion.3
  411.4 16.2 %multiply_reduce_fusion.1 = (f32[12,512]{1,0:T(8,128)S(1)}, f32[12,512,896]{2,1,0:T(8,128)}) fusion(f32[12,512]{1,0:T(8,128)} %log_add_fusion.1, f32[12,512,896]{2,1,0:T(8,128)} %copy-done, pred[512,896]{1,0:T(8,128)(4,1)} %pad_add_fusion, bf16[512,12,64]{0,2,1:T(8,128)(2,1)} %bitcast.126, bf16[896,12,64]{0,2,1:T(8,128)(2,1)} %bitcast.118), kind=kOutput, calls=%fused_computation.10 | convolution fusion | flops 732162048 | bytes 46710784 | tf_op jit(solution)/shard_map/qhd,khd->hqk/dot_general | solution.py:251
  435.7 15.1 %multiply_convert_fusion.1 = bf16[12,512,896]{2,1,0:T(8,128)(2,1)S(1)} fusion(f32[12,512,896]{2,1,0:T(8,128)} %get-tuple-element.185, f32[12,512]{1,0:T(8,128)S(1)} %get-tuple-element.184, f32[12,512]{1,0:T(8,128)S(1)} %copy-done.54, f32[12,512,896]{2,1,0:T(8,128)} %copy-done, pred[512,896]{1,0:T(8,128)(4,1)S(1)} %copy-done.29), kind=kLoop, calls=%fused_computation.9 | loop fusion | flops 33030144 | bytes 55558144 | tf_op jit(solution)/shard_map/convert_element_type | solution.py:255
  471.0 9.0 multiply_convert_fusion.4
  495.6 9.0 scatter_custom_fusion.2
  543.4 11.5 %convolution_bitcast_fusion = f32[768,2304]{0,1:T(8,128)} fusion(bf16[1,1024,768]{2,1,0:T(8,128)(2,1)S(1)} %copy-done.41, bf16[1024,1536]{1,0:T(8,128)(2,1)S(1)} %fusion.21, bf16[512,768]{1,0:T(8,128)(2,1)S(1)} %copy-done.38, bf16[512,768]{1,0:T(8,128)(2,1)S(1)} %copy.108), kind=kOutput, calls=%fused_computation.45 | convolution fusion | flops 3638034432 | bytes 13369344 | tf_op jit(solution)/shard_map/sd,se->de/dot_general | solution.py:303
  565.0 10.5 fusion.96
  576.9 10.8 %fusion.89 = f32[3072,768]{0,1:T(8,128)} fusion(bf16[1024,768]{0,1:T(8,128)(2,1)S(1)} %copy-done.43, f32[1024,3072]{1,0:T(8,128)} %fusion.97, f32[3072]{0:T(1024)S(1)} %copy-done.73), kind=kOutput, calls=%fused_computation.199 | convolution fusion | flops 4863295488 | bytes 23605248 | tf_op jit(solution)/shard_map/sf,sd->fd/dot_general | solution.py:86
  592.7 9.1 add_bitcast_fusion
  607.7 39.0 %all-reduce.21 = (f32[2304]{0:T(1024)S(1)}, f32[768]{0:T(1024)S(1)}, f32[768]{0:T(1024)S(1)}, f32[768]{0:T(1024)S(1)}, f32[3072]{0:T(1024)S(1)}, /*index=5*/f32[...) all-reduce(f32[2304]{0:T(1024)S(1)} %convert_reduce_fusion.1, ...), channel_id=3, replica_groups=mesh['dp'=8,'fsdp'=4] {'dp','fsdp'}, use_global_device_ids=true, to_apply=%region_22.23.clone | all-reduce | flops 9984 | bytes 79872
  652.8 10.8 reduce-scatter.10.cloned.1.call-done
  663.5 125.4 %reduce-scatter.16.cloned.1.call-done = f32[24,2304]{1,0:T(8,128)} async-done(((f32[768,2304]{1,0:T(8,128)}), f32[24,2304]{1,0:T(8,128)}) %reduce-scatter.16.cloned.1.call-update) | async-done | bytes 221200
  788.9 141.4 %reduce-scatter.12.cloned.1.call-done = f32[24,3072]{1,0:T(8,128)} async-done(((f32[768,3072]{1,0:T(8,128)}), f32[24,3072]{1,0:T(8,128)}) %reduce-scatter.12.cloned.1.call-update) | async-done | bytes 294928 | tf_op jit(solution)/shard_map/reduce_scatter | solution.py:225
  930.3 142.1 %reduce-scatter.14.cloned.1.call-done = f32[3072,24]{0,1:T(8,128)} async-done(((f32[3072,768]{0,1:T(8,128)}), f32[3072,24]{0,1:T(8,128)}) %reduce-scatter.14.cloned.1.call-update) | async-done | bytes 294928 | tf_op jit(solution)/shard_map/reduce_scatter | solution.py:227
  (364 shorter events, 286.9 us)
Async XLA Ops:
  7.2 130.8 %copy-start.56 = (bf16[1,160,768]{2,1,0:T(8,128)(2,1)S(1)}, bf16[1,160,768]{2,1,0:T(8,128)(2,1)}, u32[]{:S(2)}) copy-start(bf16[1,160,768]{2,1,0:T(8,128)(2,1)} %param.39) | copy-start | bytes 737284
  7.2 139.4 %all-gather.6.cloned.1.call-start = ((), (), s32[]{:S(2)}) async-start(), calls=%async_computation.5 | async-start | bytes 3649536 | tf_op jit(solution)/shard_map/all_gather | solution.py:118
  7.9 261.4 %all-gather.8.cloned.1.call-start = ((), (), s32[]{:S(2)}) async-start(), calls=%async_computation.6 | async-start | bytes 1216512 | tf_op jit(solution)/shard_map/all_gather | solution.py:121
  8.7 265.8 %all-gather.10.cloned.1.call-start = ((), (), s32[]{:S(2)}) async-start(), calls=%async_computation.7 | async-start | bytes 4866048 | tf_op jit(solution)/shard_map/all_gather | solution.py:127
  9.4 275.6 %all-gather.12.cloned.1.call-start = ((), (), s32[]{:S(2)}) async-start(), calls=%async_computation.8 | async-start | bytes 4866048 | tf_op jit(solution)/shard_map/all_gather | solution.py:129
  10.0 641.4 %reduce-scatter.18.cloned.1.call-start = ((), (), s32[]{:S(2)}) async-start(), calls=%async_computation.13 | async-start | bytes 811008
  67.2 264.3 %copy-start.47 = (f32[768]{0:T(1024)}, f32[768]{0:T(1024)S(1)}, u32[]{:S(2)}) copy-start(f32[768]{0:T(1024)S(1)} %convert_element_type.128) | copy-start | bytes 9220
  67.2 217.8 %copy-start.51 = (f32[768]{0:T(1024)}, f32[768]{0:T(1024)S(1)}, u32[]{:S(2)}) copy-start(f32[768]{0:T(1024)S(1)} %convert_element_type.129) | copy-start | bytes 9220
  135.4 67.8 %copy-start.57 = (f32[1536]{0:T(1024)}, f32[1536]{0:T(1024)S(1)}, u32[]{:S(2)}) copy-start(f32[1536]{0:T(1024)S(1)} %get-tuple-element.134) | copy-start | bytes 18436
  135.4 67.8 %copy-start.59 = (f32[1536]{0:T(1024)}, f32[1536]{0:T(1024)S(1)}, u32[]{:S(2)}) copy-start(f32[1536]{0:T(1024)S(1)} %get-tuple-element.135) | copy-start | bytes 18436
  135.4 67.8 %copy-start.61 = (f32[1536]{0:T(1024)}, f32[1536]{0:T(1024)S(1)}, u32[]{:S(2)}) copy-start(f32[1536]{0:T(1024)S(1)} %get-tuple-element.136) | copy-start | bytes 18436
  135.4 67.8 %copy-start.63 = (f32[1536]{0:T(1024)}, f32[1536]{0:T(1024)S(1)}, u32[]{:S(2)}) copy-start(f32[1536]{0:T(1024)S(1)} %get-tuple-element.137) | copy-start | bytes 18436
  135.4 67.8 %copy-start.65 = (f32[1536]{0:T(1024)}, f32[1536]{0:T(1024)S(1)}, u32[]{:S(2)}) copy-start(f32[1536]{0:T(1024)S(1)} %get-tuple-element.133) | copy-start | bytes 18436
  273.0 47.7 %copy-start.3 = (f32[1024,768]{0,1:T(8,128)}, f32[1024,768]{0,1:T(8,128)S(1)}, u32[]{:S(2)}) copy-start(f32[1024,768]{0,1:T(8,128)S(1)} %get-tuple-element.180) | copy-start | bytes 9437188
  273.0 58.5 %copy-start.45 = (f32[1024]{0:T(1024)}, f32[1024]{0:T(1024)S(1)}, u32[]{:S(2)}) copy-start(f32[1024]{0:T(1024)S(1)} %broadcast_multiply_fusion.1) | copy-start | bytes 12292
  273.4 58.1 %copy-start.49 = (f32[1024]{0:T(1024)}, f32[1024]{0:T(1024)S(1)}, u32[]{:S(2)}) copy-start(f32[1024]{0:T(1024)S(1)} %fusion.71) | copy-start | bytes 12292
  274.4 73.7 %copy-start.55 = (f32[12,512]{1,0:T(8,128)}, f32[12,512]{1,0:T(8,128)S(1)}, u32[]{:S(2)}) copy-start(f32[12,512]{1,0:T(8,128)S(1)} %log_add_fusion) | copy-start | bytes 73732
  364.6 38.1 %slice-start.2 = ((s8[22020096]{0:T(1024)(128)(4,1)}), s8[4194304]{0:T(1024)(128)(4,1)S(1)}, s32[]{:S(2)}) async-start(s8[22020096]{0:T(1024)(128)(4,1)} %bitcast.104), calls=%async_computation.16 | async-start | bytes 8388608
  364.6 38.1 %slice-start.3 = ((s8[22020096]{0:T(1024)(128)(4,1)}), s8[1048576]{0:T(1024)(128)(4,1)S(1)}, s32[]{:S(2)}) async-start(s8[22020096]{0:T(1024)(128)(4,1)} %bitcast.104), calls=%async_computation.17 | async-start | bytes 2097152
  466.4 197.2 %reduce-scatter.10.cloned.1.call-start = ((), (), s32[]{:S(2)}) async-start(), calls=%async_computation.9 | async-start | bytes 2433024 | tf_op jit(solution)/shard_map/reduce_scatter | solution.py:321
  470.9 318.0 %reduce-scatter.16.cloned.1.call-start = ((), (), s32[]{:S(2)}) async-start(), calls=%async_computation.12 | async-start | bytes 7299072
  482.6 59.1 %copy-start.39 = (bf16[512,768]{1,0:T(8,128)(2,1)}, bf16[512,768]{1,0:T(8,128)(2,1)S(1)}, u32[]{:S(2)}) copy-start(bf16[512,768]{1,0:T(8,128)(2,1)S(1)} %copy.108) | copy-start | bytes 2359300
  563.1 367.2 %reduce-scatter.12.cloned.1.call-start = ((), (), s32[]{:S(2)}) async-start(), calls=%async_computation.10 | async-start | bytes 9732096 | tf_op jit(solution)/shard_map/reduce_scatter | solution.py:225
  575.5 496.9 %reduce-scatter.14.cloned.1.call-start = ((), (), s32[]{:S(2)}) async-start(), calls=%async_computation.11 | async-start | bytes 9732096 | tf_op jit(solution)/shard_map/reduce_scatter | solution.py:227
  (85 other events, 610.4 us)
Sparse Core Ops, SparseCore 0:
  10.8 63.2 all-gather.5
  77.0 53.0 all-gather.7
  132.8 62.5 all-gather.9
  198.0 62.3 all-gather.11
  466.5 92.9 reduce-scatter.17
  565.1 98.3 reduce-scatter.9
  670.7 118.1 reduce-scatter.15
  795.4 134.8 reduce-scatter.11
  937.8 134.5 reduce-scatter.13
where the time goes:
time: 1090 us; the launch traced here: 1080 us
  waiting for transfers between devices  422 us (39%)
  matrix products  219 us (20%)
  blocking collectives  149 us (14%)
  other arithmetic  146 us (13%)
  local copies, waits for them, and re-layouts  128 us (12%)
  between operations  15.2 us (1%)
    reduce_scatter x1, waiting for transfers between devices, shards(): lax.psum_scatter(feed_grads[2], ('dp', 'fsdp'), scatter_dimension=1, tile...  142 us
    reduce_scatter x1, waiting for transfers between devices, shards(): lax.psum_scatter(feed_grads[0], ('dp', 'fsdp'), scatter_dimension=0, tile...  141 us
    unnamed x11, waiting for transfers between devices  128 us
    unnamed x2, blocking collectives  81.9 us
    all_gather x1, blocking collectives, shards(): lax.all_gather(conv_kv, ('dp', 'fsdp'), axis=1, tiled=True)  66.8 us
    unnamed x230, local copies, waits for them, and re-layouts  53.3 us
    scatter-add x5, other arithmetic, shards(): grad_padded.at[tap_index:tap_index + STRIDE * pool_count:STRIDE]  41.8 us
    slice x5, local copies, waits for them, and re-layouts, pool_window(): padded[tap_index:tap_index + STRIDE * pool_count:STRIDE]  38.5 us
  transfers between devices with their start and end apart: 9, of which 4 were waited for; matrix products, arithmetic and copies ran while one was open for 28% of the time, Pallas kernels for 0%

commit v1 on v0

v1 whole, which is shorter than its diff:
```python
import functools
import jax
import jax.numpy as jnp
from jax import lax
from jax.experimental import pallas as pl
from jax.experimental.pallas import tpu as pltpu
from jax.sharding import PartitionSpec as P

F32 = jnp.float32
BF = jnp.bfloat16
EPS = 1e-5
NT = (((1,), (1,)), ((), ()))
TN = (((0,), (0,)), ((), ()))


def mm(a, b):
    return jnp.dot(a, b, preferred_element_type=F32)


def mm_nt(a, b):
    return lax.dot_general(a, b, NT, preferred_element_type=F32)


def mm_tn(a, b):
    return lax.dot_general(a, b, TN, preferred_element_type=F32)


def norm_stats(values):
    average = jnp.mean(values, axis=-1, keepdims=True)
    centred = values - average
    variance = jnp.mean(centred * centred, axis=-1, keepdims=True)
    rate = lax.rsqrt(variance + EPS)
    return centred * rate, rate


def norm_back(xhat, rate, gain, dy):
    e = dy * gain
    mean_e = jnp.mean(e, axis=-1, keepdims=True)
    mean_ex = jnp.mean(e * xhat, axis=-1, keepdims=True)
    return rate * (e - mean_e - xhat * mean_ex)


def colsum(v):
    return jnp.sum(v, axis=0, keepdims=True)


def gelu_both(u):
    c = 0.7978845608028654
    u2 = u * u
    t = jnp.tanh(u * (c + (c * 0.044715) * u2))
    half = 0.5 + 0.5 * t
    value = u * half
    slope = half + (0.5 * u) * (1.0 - t * t) * (c + (3.0 * c * 0.044715) * u2)
    return value, slope


def head_split(x, scale):
    lane = lax.broadcasted_iota(jnp.int32, x.shape, 1)
    low = jnp.where(lane < 64, scale, 0.0).astype(BF)
    high = jnp.where(lane < 64, 0.0, scale).astype(BF)
    return jnp.concatenate([x * low, x * high], axis=0)


def head_join(r):
    return jnp.concatenate([r[:64, :128], r[64:, 128:]], axis=0)


def window(b):
    ns = pl.multiple_of(jnp.clip(b * 128 - 64, 0, 1024 - 256), 64)
    ps = pl.multiple_of(jnp.clip(b * 32 - 64, 0, 256 - 160), 32)
    col = b * 128 + (lax.broadcasted_iota(jnp.int32, (256, 256), 1) & 127)
    row = ns + lax.broadcasted_iota(jnp.int32, (256, 256), 0)
    near = jnp.abs(row - col) <= 64
    colp = b * 128 + (lax.broadcasted_iota(jnp.int32, (160, 256), 1) & 127)
    rowp = 4 * (ps + lax.broadcasted_iota(jnp.int32, (160, 256), 0))
    far = jnp.abs(rowp - colp) <= 256
    return ns, ps, near, far


def fwd_group(g, tok, w, bqkv, conv, qkv, pkv, kvf, ctx, lse):
    for r in range(2):
        rows = pl.ds(512 * r, 512)
        low = (mm(tok[rows, :], w[g]) + bqkv[g]).astype(BF)
        qkv[g, rows, :] = low
        for cpart in range(4):
            kvf[cpart, pl.ds(8 + 512 * r, 512), :] = low[:, 256 + 128 * cpart:384 + 128 * cpart].astype(F32)
    for cpart in range(4):
        cols = pl.ds(128 * cpart, 128)
        total = jnp.zeros((256, 128), F32)
        for t in range(5):
            total = total + conv[g, pl.ds(t, 1), cols] * kvf[cpart, pl.ds(6 + t, 256, stride=4), :]
        pkv[g, :, cols] = total.astype(BF)

    def block(b, carry):
        ns, ps, near, far = window(b)
        rows = pl.ds(pl.multiple_of(b * 128, 128), 128)
        for pr in range(2):
            qm = head_split(qkv[g, rows, 128 * pr:128 * pr + 128], 0.125)
            kn = qkv[g, pl.ds(ns, 256), 256 + 128 * pr:384 + 128 * pr]
            kp = pkv[g, pl.ds(ps, 160), 128 * pr:128 * pr + 128]
            sn = jnp.where(near, mm_nt(kn, qm), -1e30)
            sp = jnp.where(far, mm_nt(kp, qm), -1e30)
            peak = jnp.maximum(jnp.max(sn, axis=0, keepdims=True), jnp.max(sp, axis=0, keepdims=True))
            en = jnp.exp(sn - peak)
            ep = jnp.exp(sp - peak)
            total = jnp.sum(en, axis=0, keepdims=True) + jnp.sum(ep, axis=0, keepdims=True)
            vn = qkv[g, pl.ds(ns, 256), 512 + 128 * pr:640 + 128 * pr]
            vp = pkv[g, pl.ds(ps, 160), 256 + 128 * pr:384 + 128 * pr]
            out = mm_tn(vn, en.astype(BF)) + mm_tn(vp, ep.astype(BF))
            out = out * pl.reciprocal(total)
            ctx[rows, 256 * g + 128 * pr:256 * g + 128 * pr + 128] = head_join(out).T.astype(BF)
            lse[(g * 2 + pr) * 8 + b] = peak + jnp.log(total)
        return carry

    lax.fori_loop(0, 8, block, 0)


def fwd_kernel(tok, w, bqkv, conv, vec, bup, pos, cot,
               out, dpre, gff, gsm, gbup, qkv, pkv, ctx, lse,
               kvf, first, act, gp, dh, dbr, tr, stage, sems):
    pre = dpre
    kvf[:, 0:8, :] = jnp.zeros((4, 8, 128), F32)
    kvf[:, 1032:1040, :] = jnp.zeros((4, 8, 128), F32)
    for g in range(3):
        fwd_group(g, tok, w, bqkv, conv, qkv, pkv, kvf, ctx, lse)
    b_out, gain1, shift1, b_down, gain2, shift2 = [vec[pl.ds(i, 1), :] for i in range(6)]
    sums = [jnp.zeros((1, 768), F32) for _ in range(5)]
    gbup[...] = jnp.zeros_like(gbup)
    T = 256
    for tile in range(1024 // T):
        rows = pl.ds(tile * T, T)
        pre_one = tok[rows, :].astype(F32) + mm_nt(ctx[rows, :], w[3]) + b_out
        pre[rows, :] = pre_one
        xhat, rate = norm_stats(pre_one)
        first[rows, :] = (xhat * gain1 + shift1).astype(BF)
    for tile in range(1024 // T):
        rows = pl.ds(tile * T, T)
        fl = first[rows, :]
        acc = fl.astype(F32) + b_down
        for j in range(4):
            value, slope = gelu_both(mm(fl, w[4 + j]) + bup[j])
            low = value.astype(BF)
            act[j, rows, :] = low
            gp[j] = slope
            acc = acc + mm_nt(low, w[8 + j])
        xhat, rate = norm_stats(acc)
        out[rows, :] = (xhat * gain2 + shift2).astype(BF)
        row = tile * T + lax.broadcasted_iota(jnp.int32, (T, 160), 0)
        dy = mm((row == pos[...]).astype(BF), cot[...])
        sums[3] = sums[3] + colsum(dy * xhat)
        sums[4] = sums[4] + colsum(dy)
        dacc = norm_back(xhat, rate, gain2, dy)
        db = dacc.astype(BF)
        dbr[rows, :] = db
        sums[2] = sums[2] + colsum(db.astype(F32))
        for j in range(4):
            low = (mm(db, w[8 + j]) * gp[j]).astype(BF)
            dh[j, rows, :] = low
            gbup[j] += colsum(low.astype(F32))
            dacc = dacc + mm_nt(low, w[4 + j])
        xhat, rate = norm_stats(pre[rows, :])
        sums[0] = sums[0] + colsum(dacc * xhat)
        sums[1] = sums[1] + colsum(dacc)
        dpre[rows, :] = norm_back(xhat, rate, gain1, dacc)
    for i in range(5):
        gsm[pl.ds(i, 1), :] = sums[i]
    sent = [None, None]
    for j in range(8):
        if j % 4 == 0:
            tr[...] = (first if j < 4 else dbr)[...].T
        if sent[j % 2] is not None:
            sent[j % 2].wait()
        stage[j % 2] = mm(tr[...], (dh if j < 4 else act)[j % 4]).astype(BF)
        sent[j % 2] = pltpu.make_async_copy(stage.at[j % 2], gff.at[j], sems.at[j % 2])
        sent[j % 2].start()
    sent[0].wait()
    sent[1].wait()


VM = pl.BlockSpec(memory_space=pltpu.VMEM)


def fwd_call(tok, w, bqkv, conv, vec, bup, pos, cot):
    s = jax.ShapeDtypeStruct
    return pl.pallas_call(
        fwd_kernel,
        in_specs=[VM] * 8,
        out_specs=[VM] * 2 + [pl.BlockSpec(memory_space=pl.ANY)] + [VM] * 6,
        out_shape=[
            s((1024, 768), BF), s((1024, 768), F32), s((8, 768, 768), BF), s((8, 768), F32), s((4, 1, 768), F32),
            s((3, 1024, 768), BF), s((3, 256, 512), BF), s((1024, 768), BF), s((48, 1, 256), F32),
        ],
        scratch_shapes=[
            pltpu.VMEM((4, 1040, 128), F32), pltpu.VMEM((1024, 768), BF),
            pltpu.VMEM((4, 1024, 768), BF), pltpu.VMEM((4, 256, 768), F32), pltpu.VMEM((4, 1024, 768), BF),
            pltpu.VMEM((1024, 768), BF), pltpu.VMEM((768, 1024), BF), pltpu.VMEM((2, 768, 768), BF),
            pltpu.SemaphoreType.DMA((2,)),
        ],
        compiler_params=pltpu.CompilerParams(vmem_limit_bytes=64 * 1024 * 1024 - 1024*512),
        name="forward",
    )(tok, w, bqkv, conv, vec, bup, pos, cot)


def bwd_group(g, tokt, w, conv, qkv, pkv, dctx, lse, kvf, dq, dk, dv, dpk, dpv, dproj, gqkv, gconv, gbias):
    dk[...] = jnp.zeros_like(dk)
    dv[...] = jnp.zeros_like(dv)
    dpk[...] = jnp.zeros_like(dpk)
    dpv[...] = jnp.zeros_like(dpv)

    def block(b, carry):
        ns, ps, near, far = window(b)
        rows = pl.ds(pl.multiple_of(b * 128, 128), 128)
        nr, prow = pl.ds(ns, 256), pl.ds(ps, 160)
        for pr in range(2):
            ln = pl.ds(128 * pr, 128)
            qm = head_split(qkv[g, rows, 128 * pr:128 * pr + 128], 0.125)
            dm = head_split(dctx[rows, 256 * g + 128 * pr:256 * g + 128 * pr + 128], 1.0)
            kn = qkv[g, nr, 256 + 128 * pr:384 + 128 * pr]
            kp = pkv[g, prow, 128 * pr:128 * pr + 128]
            vn = qkv[g, nr, 512 + 128 * pr:640 + 128 * pr]
            vp = pkv[g, prow, 256 + 128 * pr:384 + 128 * pr]
            ls = lse[(g * 2 + pr) * 8 + b]
            pn = jnp.exp(jnp.where(near, mm_nt(kn, qm), -1e30) - ls)
            pp = jnp.exp(jnp.where(far, mm_nt(kp, qm), -1e30) - ls)
            dn = mm_nt(vn, dm)
            dp = mm_nt(vp, dm)
            rd = jnp.sum(pn * dn, axis=0, keepdims=True) + jnp.sum(pp * dp, axis=0, keepdims=True)
            sn = (pn * (dn - rd)).astype(BF)
            sp = (pp * (dp - rd)).astype(BF)
            dk[nr, ln] += mm(sn, qm)
            dpk[prow, ln] += mm(sp, qm)
            dv[nr, ln] += mm(pn.astype(BF), dm)
            dpv[prow, ln] += mm(pp.astype(BF), dm)
            r = mm_tn(kn, sn) + mm_tn(kp, sp)
            dproj[g, rows, ln] = (head_join(r).T * 0.125).astype(BF)
        return carry

    lax.fori_loop(0, 8, block, 0)
    for cpart in range(4):
        kvf[cpart, 8:1032, :] = qkv[g, :, 256 + 128 * cpart:384 + 128 * cpart].astype(F32)
    for cpart in range(4):
        cols = pl.ds(128 * cpart, 128)
        src = dpk if cpart < 2 else dpv
        dst = dk if cpart < 2 else dv
        c2 = pl.ds(128 * (cpart % 2), 128)
        dpool = src[:, c2]
        for t in range(5):
            gconv[g, pl.ds(t, 1), cols] = colsum(dpool * kvf[cpart, pl.ds(6 + t, 256, stride=4), :])
        kvf[cpart, 0:8, :] = jnp.zeros((8, 128), F32)
        kvf[cpart, 1032:1040, :] = jnp.zeros((8, 128), F32)
        kvf[cpart, 8:1032, :] = dst[:, c2]
        for t in range(5):
            at = pl.ds(6 + t, 256, stride=4)
            kvf[cpart, at, :] += conv[g, pl.ds(t, 1), cols] * dpool
        dproj[g, :, 256 + 128 * cpart:384 + 128 * cpart] = kvf[cpart, 8:1032, :].astype(BF)
        kvf[cpart, 0:8, :] = jnp.zeros((8, 128), F32)
        kvf[cpart, 1032:1040, :] = jnp.zeros((8, 128), F32)
    gqkv[g] = mm(tokt[...], dproj[g]).astype(BF)
    gbias[g] = colsum(dproj[g].astype(F32))


def bwd_kernel(tok, w, conv, dpre, qkv, pkv, ctx, lse,
               gtok, gat, gconv, gbias, gbout,
               kvf, dk, dv, dpk, dpv, dctx, dproj, tr):
    kvf[:, 0:8, :] = jnp.zeros((4, 8, 128), F32)
    kvf[:, 1032:1040, :] = jnp.zeros((4, 8, 128), F32)
    da = dpre[...].astype(BF)
    gbout[...] = colsum(da.astype(F32))
    tr[...] = da.T
    for r in range(2):
        rows = pl.ds(512 * r, 512)
        dctx[rows, :] = mm(dpre[rows, :].astype(BF), w[3]).astype(BF)
    gat[3] = mm(tr[...], ctx[...]).astype(BF)
    tr[...] = tok[...].T
    for g in range(3):
        bwd_group(g, tr, w, conv, qkv, pkv, dctx, lse, kvf, None, dk, dv, dpk, dpv, dproj, gat, gconv, gbias)
    for r in range(2):
        rows = pl.ds(512 * r, 512)
        acc = dpre[rows, :]
        for g in range(3):
            acc = acc + mm_nt(dproj[g, rows, :], w[g])
        gtok[rows, :] = acc


def bwd_call(tok, w, conv, dpre, qkv, pkv, ctx, lse):
    s = jax.ShapeDtypeStruct
    return pl.pallas_call(
        bwd_kernel,
        in_specs=[VM] * 8,
        out_specs=[VM] * 5,
        out_shape=[
            s((1024, 768), F32), s((4, 768, 768), BF), s((3, 8, 512), F32), s((3, 1, 768), F32), s((1, 768), F32),
        ],
        scratch_shapes=[
            pltpu.VMEM((4, 1040, 128), F32), pltpu.VMEM((1024, 256), F32), pltpu.VMEM((1024, 256), F32),
            pltpu.VMEM((256, 256), F32), pltpu.VMEM((256, 256), F32), pltpu.VMEM((1024, 768), BF),
            pltpu.VMEM((3, 1024, 768), BF), pltpu.VMEM((768, 1024), BF),
        ],
        compiler_params=pltpu.CompilerParams(vmem_limit_bytes=64 * 1024 * 1024 - 1024*512),
        name="backward",
    )(tok, w, conv, dpre, qkv, pkv, ctx, lse)


AXES = ("dp", "fsdp")


def small_pack(qb, cv, six, ub):
    return jnp.concatenate([qb, cv.reshape(-1)] + six + [ub])


def small_unpack(rows):
    count = rows.shape[0]
    sizes = [2304 // count] + [1536 // count] * 5 + [768 // count] * 6 + [3072 // count]
    at, parts = 0, []
    for size in sizes:
        parts.append(rows[:, at:at + size].reshape(-1))
        at += size
    return parts


def by_group(v, kinds):
    return v.reshape(kinds, 3, 256).transpose(1, 0, 2).reshape(3, 1, kinds * 256)


def shards(tokens, w_qkv, b_qkv, conv_kv, w_out, b_out, gain_one, shift_one, w_up, b_up, w_down, b_down, gain_two,
           shift_two, positions, cotangent):
    rows = w_qkv.shape[0]
    count = 768 // rows
    own = jnp.concatenate([
        w_qkv.reshape(rows, 3, 3, 256).transpose(2, 0, 1, 3).reshape(3, rows, 768),
        w_out.T[None],
        w_up.reshape(rows, 4, 768).transpose(1, 0, 2),
        w_down.reshape(4, 768, rows).transpose(0, 2, 1),
    ], 0)
    w = lax.all_gather(own, AXES, axis=1, tiled=True)
    small = small_pack(b_qkv, conv_kv, [b_out, gain_one, shift_one, b_down, gain_two, shift_two], b_up)
    parts = small_unpack(lax.all_gather(small[None], AXES, axis=0, tiled=True).astype(F32))
    bqkv = by_group(parts[0], 3)
    conv = jnp.concatenate([by_group(p, 2) for p in parts[1:6]] + [jnp.zeros((3, 3, 512), F32)], 1)
    vec = jnp.stack(parts[6:12] + [jnp.zeros((768,), F32)] * 2)
    bup = parts[12].reshape(4, 1, 768)
    out, dpre, gff, gsm, gbup, qkv, pkv, ctx, lse = fwd_call(tokens[0], w, bqkv, conv, vec, bup, positions, cotangent[0])
    gff = lax.psum_scatter(gff, AXES, scatter_dimension=1, tiled=True).astype(F32)
    gtok, gat, gconv, gbias, gbout = bwd_call(tokens[0], w, conv, dpre, qkv, pkv, ctx, lse)
    gat = lax.psum_scatter(gat, AXES, scatter_dimension=1, tiled=True).astype(F32)
    flat = [gbias.reshape(3, 3, 256).transpose(1, 0, 2).reshape(count, -1)]
    flat += [gconv[:, t].reshape(3, 2, 256).transpose(1, 0, 2).reshape(count, -1) for t in range(5)]
    flat += [gbout[0].reshape(count, -1)] + [gsm[i].reshape(count, -1) for i in range(5)] + [gbup.reshape(count, -1)]
    flat = lax.psum_scatter(jnp.concatenate(flat, 1), AXES, scatter_dimension=0, tiled=True)
    s = [p for p in small_unpack_own(flat, count)]
    return (
        out[None], gtok[None],
        gat[:3].reshape(3, rows, 3, 256).transpose(1, 2, 0, 3).reshape(rows, 2304),
        s[0], jnp.stack(s[1:6]), gat[3].T, s[6], s[7], s[8],
        gff[:4].transpose(1, 0, 2).reshape(rows, 3072), s[12],
        gff[4:].transpose(0, 2, 1).reshape(3072, rows), s[9], s[10], s[11],
    )


def small_unpack_own(row, count):
    sizes = [2304 // count] + [1536 // count] * 5 + [768 // count] * 6 + [3072 // count]
    at = 0
    for size in sizes:
        yield row[0, at:at + size]
        at += size


def solution(mesh):
    rows, cols, flat, item = P(AXES, None), P(None, AXES), P(AXES), P(AXES, None, None)
    return jax.shard_map(
        shards,
        mesh=mesh,
        in_specs=(item, rows, flat, cols, cols, flat, flat, flat, rows, flat, cols, flat, flat, flat, rows, item),
        out_specs=(item, item, rows, flat, cols, cols, flat, flat, flat, rows, flat, cols, flat, flat, flat),
        check_vma=False,
    )
```

time: 1090 us -> 643 us (0.59)
  matrix products: 219 us -> 0 us
  other arithmetic: 146 us -> 3.15 us
  Pallas kernels: 0 us -> 131 us
  blocking collectives: 149 us -> 43.4 us
  local copies, waits for them, and re-layouts: 128 us -> 44.4 us
  waiting for transfers between devices: 422 us -> 400 us
    reduce_scatter x3 -> x0, waiting for transfers between devices: 294 us -> none  [the longest x1 142 us: shards(): lax.psum_scatter(feed_grads[2], ('dp', 'fsdp'), scatter_dimension=1, tile...]
    unnamed x11 -> x7, waiting for transfers between devices: 128 us -> 347 us
    dot_general x24 -> x0, matrix products: 219 us -> none  [the longest x2 32.7 us: shards(): jnp.einsum('qhd,khd->hqk', block_dc, values_all, preferred_element_type=j...]
    pallas_call x0 -> x2, Pallas kernels: none -> 131 us  [the longest x1 79.2 us: fwd_call(): pl.pallas_call(fwd_kernel, in_specs=[VM] * 8, out_specs=[VM] * 2 + [pl.Bl...]
    all_gather x1 -> x0, blocking collectives: 66.8 us -> none  [shards(): lax.all_gather(conv_kv, ('dp', 'fsdp'), axis=1, tiled=True)]
    all_gather x4 -> x1, waiting for transfers between devices: 0.03 us -> 53.1 us  [shards(): w = lax.all_gather(own, AXES, axis=1, tiled=True)]
    scatter-add x8 -> x0, other arithmetic: 51 us -> none  [the longest x5 41.8 us: shards(): grad_padded.at[tap_index:tap_index + STRIDE * pool_count:STRIDE]]
    slice x13 -> x8, local copies, waits for them, and re-layouts: 48.1 us -> 2.32 us  [the longest x1 1.1 us: shards(): gconv[:, t].reshape(3, 2, 256).transpose(1, 0, 2).reshape(count, -1)]
  transfers between devices with their start and end apart: 9 -> 4, of which waited for: 4 -> 4; matrix products, arithmetic and copies ran while one was open for 28% -> 6% of each run, Pallas kernels for 0% -> 0%
where the time goes in v1:
time: 643 us; the launch traced here: 637 us
  waiting for transfers between devices  400 us (62%)
  Pallas kernels  131 us (20%)
  local copies, waits for them, and re-layouts  44.4 us (7%)
  blocking collectives  43.4 us (7%)
  between operations  14.5 us (2%)
    unnamed x7, waiting for transfers between devices  347 us
    pallas_call x1, Pallas kernels, fwd_call(): pl.pallas_call(fwd_kernel, in_specs=[VM] * 8, out_specs=[VM] * 2 + [pl.Bl...  79.2 us
    all_gather x1, waiting for transfers between devices, shards(): w = lax.all_gather(own, AXES, axis=1, tiled=True)  53.1 us
    pallas_call x1, Pallas kernels, bwd_call(): pl.pallas_call(bwd_kernel, in_specs=[VM] * 8, out_specs=[VM] * 5, out_sha...  51.5 us
    unnamed x1, blocking collectives  43.4 us
    unnamed x12, local copies, waits for them, and re-layouts  20.2 us
  transfers between devices with their start and end apart: 4, of which 4 were waited for; matrix products, arithmetic and copies ran while one was open for 6% of the time, Pallas kernels for 0%

profile of v1, /device:TPU:0, one launch (start us, length us, event | category | flops | bytes accessed | tf_op | source)
XLA Modules:
  0.0 636.7 jit_solution(13565623041569354180)
XLA Ops:
  7.2 0.9 reshape.99
  8.4 1.0 bitcast_bitcast_fusion
  9.4 1.6 pad_maximum_fusion
  11.0 0.8 reshape.103
  11.8 5.4 concatenate.13
  17.5 43.4 %all-reduce = bf16[17664]{0:T(1024)(128)(2,1)S(1)} all-reduce(bf16[17664]{0:T(1024)(128)(2,1)S(1)} %dynamic-update-slice), channel_id=2, replica_groups=mesh['dp'=8,'fsdp'=4] {'dp','fsdp'}, use_global_device_ids=true, to_apply=%add | all-reduce | flops 17664 | bytes 70656
  65.2 53.1 %all-gather.3.cloned.1.call-done.w = bf16[12,768,768]{2,1,0:T(8,128)(2,1)} async-done(((bf16[12,24,768]{2,1,0:T(8,128)(2,1)}), bf16[12,768,768]{2,1,0:T(8,128)(2,1)}) %all-gather.3.cloned.1.call-update) | async-done | bytes 14155792 | tf_op jit(solution)/shard_map/all_gather | solution.py:335
  118.3 79.2 %forward.1 = (bf16[1024,768]{1,0:T(8,128)(2,1)}, f32[1024,768]{1,0:T(8,128)}, bf16[8,768,768]{2,1,0:T(8,128)(2,1)}, f32[8,768]{1,0:T(8,128)}, f32[4,1,768]{2,1,0...) custom-call(bf16[1024,768]{1,0:T(8,128)(2,1)} %bitcast.87, ...), custom_call_target="tpu_custom_call" | custom-call | tf_op jit(solution)/shard_map/forward/pallas_call | solution.py:185
  197.5 51.5 %backward.1 = (f32[1024,768]{1,0:T(8,128)}, bf16[4,768,768]{2,1,0:T(8,128)(2,1)}, f32[3,8,512]{2,1,0:T(8,128)}, f32[3,1,768]{2,1,0:T(1,128)}, f32[1,768]{1,0:T(1,128)}) custom-call(bf16[1024,768]{1,0:T(8,128)(2,1)} %bitcast.88, bf16[12,768,768]{2,1,0:T(8,128)(2,1)} %all-gather.3.cloned.1.call-done.w, f32[3,8,512]{2,1,0:T(8,128)} %concatenate.14.conv, ...), custom_call_target="tpu_custom_call" | custom-call | tf_op jit(solution)/shard_map/backward/pallas_call | solution.py:287
  248.9 1.1 slice_reduce_fusion
  252.7 0.8 concatenate.15
  253.6 6.0 copy.76
  259.5 3.3 copy.84
  262.9 8.6 %copy.85 = bf16[96,8,8,768]{3,1,2,0:T(8,128)(2,1)} copy(bf16[96,8,8,768]{3,1,0,2:T(8,128)(2,1)} %bitcast.86) | data formatting | bytes 18874368
  271.6 99.7 %all-reduce.4.cloned.1.call-done = f32[32,552]{1,0:T(8,128)} async-done(((f32[32,552]{1,0:T(8,128)}), f32[32,552]{1,0:T(8,128)}) %all-reduce.4.cloned.1.call-update) | async-done | bytes 70672
  371.3 0.9 fusion
  372.8 1.2 dynamic-slice_bitcast_fusion.7
  374.0 1.3 dynamic-slice_bitcast_fusion.3
  375.3 1.5 dynamic-slice_bitcast_fusion
  376.8 108.9 %reduce-scatter.7.cloned.1.call-done = bf16[24,3072]{1,0:T(8,128)(2,1)} async-done(((bf16[768,3072]{1,0:T(8,128)(2,1)}), bf16[24,3072]{1,0:T(8,128)(2,1)}) %reduce-scatter.7.cloned.1.call-update) | async-done | bytes 147472
  485.7 1.0 reshape.127
  487.1 0.8 reshape.111
  488.6 138.5 %reduce-scatter.9.cloned.1.call-done = bf16[24,6144]{1,0:T(8,128)(2,1)} async-done(((bf16[768,6144]{1,0:T(8,128)(2,1)}), bf16[24,6144]{1,0:T(8,128)(2,1)}) %reduce-scatter.9.cloned.1.call-update) | async-done | bytes 294928
  627.1 1.0 copy.86
  (79 shorter events, 10.6 us)
Async XLA Ops:
  7.2 111.1 %all-gather.3.cloned.1.call-start = ((), (), s32[]{:S(2)}) async-start(), calls=%async_computation.2 | async-start | bytes 14598144 | tf_op jit(solution)/shard_map/all_gather | solution.py:335
  11.0 360.3 %all-reduce.4.cloned.1.call-start = ((), (), s32[]{:S(2)}) async-start(), calls=%async_computation.5 | async-start | bytes 163840
  197.5 54.7 %copy-start.1 = (f32[8,768]{1,0:T(8,128)S(1)}, f32[8,768]{1,0:T(8,128)}, u32[]{:S(2)}) copy-start(f32[8,768]{1,0:T(8,128)} %get-tuple-element.40) | copy-start | bytes 73732
  197.5 55.1 %copy-start = (f32[4,1,768]{2,1,0:T(1,128)S(1)}, f32[4,1,768]{2,1,0:T(1,128)}, u32[]{:S(2)}) copy-start(f32[4,1,768]{2,1,0:T(1,128)} %get-tuple-element.41) | copy-start | bytes 36868
  253.5 232.2 %reduce-scatter.7.cloned.1.call-start = ((), (), s32[]{:S(2)}) async-start(), calls=%async_computation.3 | async-start | bytes 4866048
  262.9 364.2 %reduce-scatter.9.cloned.1.call-start = ((), (), s32[]{:S(2)}) async-start(), calls=%async_computation.4 | async-start | bytes 9732096
Sparse Core Ops, SparseCore 0:
  11.7 106.5 all-gather.2
  253.6 117.5 all-reduce.3
  376.8 108.9 reduce-scatter.6
  492.5 134.5 reduce-scatter.8

commit v2 on v1

v2 whole, which is shorter than its diff:
```python
import functools
import jax
import jax.numpy as jnp
from jax import lax
from jax.experimental import pallas as pl
from jax.experimental.pallas import tpu as pltpu
from jax.sharding import PartitionSpec as P

F32 = jnp.float32
BF = jnp.bfloat16
EPS = 1e-5
NT = (((1,), (1,)), ((), ()))
TN = (((0,), (0,)), ((), ()))
AXES = ("dp", "fsdp")
VM = pl.BlockSpec(memory_space=pltpu.VMEM)
ANY = pl.BlockSpec(memory_space=pl.ANY)
LIMIT = 64 * 1024 * 1024 - 512 * 1024
DMA = pltpu.SemaphoreType.DMA
struct = jax.ShapeDtypeStruct


def mm(a, b):
    return jnp.dot(a, b, preferred_element_type=F32)


def mm_nt(a, b):
    return lax.dot_general(a, b, NT, preferred_element_type=F32)


def mm_tn(a, b):
    return lax.dot_general(a, b, TN, preferred_element_type=F32)


def norm_stats(values):
    average = jnp.mean(values, axis=-1, keepdims=True)
    centred = values - average
    variance = jnp.mean(centred * centred, axis=-1, keepdims=True)
    rate = lax.rsqrt(variance + EPS)
    return centred * rate, rate


def norm_back(xhat, rate, gain, dy):
    e = dy * gain
    mean_e = jnp.mean(e, axis=-1, keepdims=True)
    mean_ex = jnp.mean(e * xhat, axis=-1, keepdims=True)
    return rate * (e - mean_e - xhat * mean_ex)


def colsum(v):
    return jnp.sum(v, axis=0, keepdims=True)


def gelu_both(u):
    c = 0.7978845608028654
    u2 = u * u
    t = jnp.tanh(u * (c + (c * 0.044715) * u2))
    half = 0.5 + 0.5 * t
    value = u * half
    slope = half + (0.5 * u) * (1.0 - t * t) * (c + (3.0 * c * 0.044715) * u2)
    return value, slope


def head_split(x, scale):
    lane = lax.broadcasted_iota(jnp.int32, x.shape, 1)
    low = jnp.where(lane < 64, scale, 0.0).astype(BF)
    high = jnp.where(lane < 64, 0.0, scale).astype(BF)
    return jnp.concatenate([x * low, x * high], axis=0)


def head_join(r):
    return jnp.concatenate([r[:64, :128], r[64:, 128:]], axis=0)


def window(b):
    ns = pl.multiple_of(jnp.clip(b * 128 - 64, 0, 1024 - 256), 64)
    ps = pl.multiple_of(jnp.clip(b * 32 - 64, 0, 256 - 160), 32)
    col = b * 128 + (lax.broadcasted_iota(jnp.int32, (256, 256), 1) & 127)
    row = ns + lax.broadcasted_iota(jnp.int32, (256, 256), 0)
    near = jnp.abs(row - col) <= 64
    colp = b * 128 + (lax.broadcasted_iota(jnp.int32, (160, 256), 1) & 127)
    rowp = 4 * (ps + lax.broadcasted_iota(jnp.int32, (160, 256), 0))
    far = jnp.abs(rowp - colp) <= 256
    return ns, ps, near, far


class Place:
    def __init__(self):
        d = lax.axis_index("dp")
        self.d, self.z = d, lax.axis_index("fsdp")
        self.k, self.x, self.y = lax.rem(d, 2), lax.rem(lax.div(d, 2), 2), lax.div(d, 4)
        self.sib = d + 1 - 2 * self.k
        self.xn = d + 2 - 4 * self.x
        self.yn = d + 4 - 8 * self.y
        self.diag = self.xn + 4 - 8 * self.y

    def up(self, dz):
        return lax.rem(self.z + dz, 4)

    def copy(self, src, dst, send, recv, dp=None, z=None):
        return pltpu.make_async_remote_copy(
            src_ref=src, dst_ref=dst, send_sem=send, recv_sem=recv,
            device_id={"dp": self.d if dp is None else dp, "fsdp": self.z if z is None else z},
            device_id_type=pl.DeviceIdType.MESH)

    def greet(self):
        barrier = pltpu.get_barrier_semaphore()
        for dp in (self.sib, self.xn, self.yn, self.diag):
            pl.semaphore_signal(barrier, inc=1, device_id={"dp": dp, "fsdp": self.z},
                                device_id_type=pl.DeviceIdType.MESH)
        for dz in (1, 2, 3):
            pl.semaphore_signal(barrier, inc=1, device_id={"dp": self.d, "fsdp": self.up(dz)},
                                device_id_type=pl.DeviceIdType.MESH)
        pl.semaphore_wait(barrier, 7)


def slab_of(rows):
    last = jnp.concatenate([rows[..., 16:, :384], rows[..., 16:, 384:]], axis=-2)
    return jnp.concatenate([rows[..., :16, :], last], axis=-1).astype(BF)


def rows_of(slab):
    v = slab.astype(F32)
    last = jnp.concatenate([v[..., :8, 768:], v[..., 8:, 768:]], axis=-1)
    return jnp.concatenate([v[..., :768], last], axis=-2)


class Gather:
    def __init__(self, p, slab, dense, sems):
        self.p, self.slab, self.dense = p, slab, dense
        self.zs, self.zr, self.xs, self.xr, self.ks, self.kr = sems

    def along_z(self, c, dz, arriving=False):
        p = self.p
        slot = p.up(4 - dz) if arriving else p.z
        return p.copy(self.slab.at[c, p.z], self.slab.at[c, slot], self.zs.at[c, dz - 1], self.zr.at[c, dz - 1],
                      z=p.up(dz))

    def first(self, c, arriving=False):
        p, w = self.p, self.dense
        ya = 1 - p.y if arriving else p.y
        xa = 1 - p.x if arriving else p.x
        a, b = pl.ds(0, 384), pl.ds(384, 384)
        return (
            p.copy(w.at[c, p.y, p.x, p.k, :, a], w.at[c, p.y, xa, p.k, :, a], self.xs.at[c, 0], self.xr.at[c, 0], dp=p.xn),
            p.copy(w.at[c, p.y, p.x, p.k, :, b], w.at[c, ya, p.x, p.k, :, b], self.xs.at[c, 1], self.xr.at[c, 1], dp=p.yn),
        )

    def second(self, c, arriving=False):
        p, w = self.p, self.dense
        ya = 1 - p.y if arriving else p.y
        xa = 1 - p.x if arriving else p.x
        a, b = pl.ds(0, 384), pl.ds(384, 384)
        return (
            p.copy(w.at[c, p.y, :, p.k, :, a], w.at[c, ya, :, p.k, :, a], self.xs.at[c, 2], self.xr.at[c, 2], dp=p.yn),
            p.copy(w.at[c, :, p.x, p.k, :, b], w.at[c, :, xa, p.k, :, b], self.xs.at[c, 3], self.xr.at[c, 3], dp=p.xn),
        )

    def across(self, c, arriving=False):
        p, w = self.p, self.dense
        k = 1 - p.k if arriving else p.k
        return p.copy(w.at[c, :, :, p.k], w.at[c, :, :, k], self.ks.at[c], self.kr.at[c], dp=p.sib)

    def s1(self, c):
        for dz in (1, 2, 3):
            self.along_z(c, dz).start()

    def s2(self, c):
        p = self.p
        for dz in (1, 2, 3):
            self.along_z(c, dz, True).wait_recv()
        self.dense[c, p.y, p.x, p.k] = rows_of(self.slab[c]).reshape(96, 768).astype(BF)
        for copy in self.first(c):
            copy.start()

    def s3(self, c):
        for copy in self.first(c, True):
            copy.wait_recv()
        for copy in self.second(c):
            copy.start()

    def s4(self, c):
        for copy in self.second(c, True):
            copy.wait_recv()
        self.across(c).start()

    def s5(self, c):
        self.across(c, True).wait_recv()

    def sent(self, count):
        def one(c, carry):
            for dz in (1, 2, 3):
                self.along_z(c, dz).wait_send()
            for copy in self.first(c) + self.second(c) + (self.across(c),):
                copy.wait_send()
            return carry
        lax.fori_loop(0, count, one, 0)


class SmallGather:
    def __init__(self, p, slab, dense, send, recv):
        self.p, self.slab, self.dense, self.send, self.recv = p, slab, dense, send, recv

    def along_z(self, dz, arriving=False):
        p = self.p
        slot = p.up(4 - dz) if arriving else p.z
        return p.copy(self.slab.at[p.z], self.slab.at[slot], self.send.at[dz - 1], self.recv.at[dz - 1], z=p.up(dz))

    def plane(self, arriving=False):
        p, w = self.p, self.dense
        out = []
        for n, (dp, y, x) in enumerate(((p.xn, p.y, 1 - p.x), (p.yn, 1 - p.y, p.x), (p.diag, 1 - p.y, 1 - p.x))):
            dst = w.at[y, x, p.k] if arriving else w.at[p.y, p.x, p.k]
            out.append(p.copy(w.at[p.y, p.x, p.k], dst, self.send.at[3 + n], self.recv.at[3 + n], dp=dp))
        return out

    def across(self, arriving=False):
        p, w = self.p, self.dense
        k = 1 - p.k if arriving else p.k
        return p.copy(w.at[:, :, p.k], w.at[:, :, k], self.send.at[6], self.recv.at[6], dp=p.sib)

    def s1(self):
        for dz in (1, 2, 3):
            self.along_z(dz).start()

    def s2(self):
        p = self.p
        for dz in (1, 2, 3):
            self.along_z(dz, True).wait_recv()
        self.dense[p.y, p.x, p.k] = self.slab[...]
        for copy in self.plane():
            copy.start()

    def s3(self):
        for copy in self.plane(True):
            copy.wait_recv()
        self.across().start()

    def s4(self):
        self.across(True).wait_recv()

    def sent(self):
        for dz in (1, 2, 3):
            self.along_z(dz).wait_send()
        for copy in self.plane() + [self.across()]:
            copy.wait_send()


class Scatter:
    def __init__(self, p, r0, r1a, r1b, r2, v, r3, fin, sems):
        self.p, self.r0, self.r1a, self.r1b, self.r2, self.v, self.r3, self.fin = p, r0, r1a, r1b, r2, v, r3, fin
        self.ks, self.kr, self.xs, self.xr, self.zs, self.zr = sems

    def across(self, c, src):
        p = self.p
        return p.copy(src.at[:, :, 1 - p.k], self.r0.at[c], self.ks.at[c], self.kr.at[c], dp=p.sib)

    def first(self, c):
        p, r = self.p, self.r0
        return (
            p.copy(r.at[c, :, 1 - p.x, :, pl.ds(0, 384)], self.r1a.at[c], self.xs.at[c, 0], self.xr.at[c, 0], dp=p.xn),
            p.copy(r.at[c, 1 - p.y, :, :, pl.ds(384, 384)], self.r1b.at[c], self.xs.at[c, 1], self.xr.at[c, 1], dp=p.yn),
        )

    def second(self, c):
        p = self.p
        return (
            p.copy(self.r1a.at[c, 1 - p.y], self.r2.at[c, 0], self.xs.at[c, 2], self.xr.at[c, 2], dp=p.yn),
            p.copy(self.r1b.at[c, 1 - p.x], self.r2.at[c, 1], self.xs.at[c, 3], self.xr.at[c, 3], dp=p.xn),
        )

    def along_z(self, c, dz):
        p = self.p
        return p.copy(self.v.at[c, p.up(dz)], self.r3.at[c, dz - 1], self.zs.at[c, dz - 1], self.zr.at[c, dz - 1],
                      z=p.up(dz))

    def s1(self, c, src, own):
        self.across(c, src).wait_recv()
        for a in range(2):
            for b in range(2):
                self.r0[c, a, b] = (self.r0[c, a, b].astype(F32) + own(a, b).astype(F32)).astype(BF)
        for copy in self.first(c):
            copy.start()

    def s2(self, c):
        p = self.p
        for copy in self.first(c):
            copy.wait_recv()
        for a in range(2):
            self.r1a[c, a] = (self.r1a[c, a].astype(F32) + self.r0[c, a, p.x, :, :384].astype(F32)).astype(BF)
            self.r1b[c, a] = (self.r1b[c, a].astype(F32) + self.r0[c, p.y, a, :, 384:].astype(F32)).astype(BF)
        for copy in self.second(c):
            copy.start()

    def s3(self, c):
        p = self.p
        for copy in self.second(c):
            copy.wait_recv()
        left = self.r1a[c, p.y].astype(F32) + self.r2[c, 0].astype(F32)
        right = self.r1b[c, p.x].astype(F32) + self.r2[c, 1].astype(F32)
        self.v[c] = slab_of(jnp.concatenate([left, right], axis=1).reshape(4, 24, 768))
        for dz in (1, 2, 3):
            self.along_z(c, dz).start()

    def s4(self, c):
        for dz in (1, 2, 3):
            self.along_z(c, dz).wait_recv()
        total = rows_of(self.v[c, self.p.z])
        for dz in range(3):
            total = total + rows_of(self.r3[c, dz])
        self.fin[c] = total

    def sent(self, c, src):
        for copy in (self.across(c, src),) + self.first(c) + self.second(c):
            copy.wait_send()
        for dz in (1, 2, 3):
            self.along_z(c, dz).wait_send()


class SmallScatter:
    def __init__(self, p, src, r0, r1, r2, send, recv):
        self.p, self.src, self.r0, self.r1, self.r2, self.send, self.recv = p, src, r0, r1, r2, send, recv

    def across(self):
        p = self.p
        return p.copy(self.src.at[:, :, 1 - p.k], self.r0, self.send.at[0], self.recv.at[0], dp=p.sib)

    def plane(self):
        p = self.p
        return [p.copy(self.r0.at[y, x], self.r1.at[n], self.send.at[1 + n], self.recv.at[1 + n], dp=dp)
                for n, (dp, y, x) in enumerate(((p.xn, p.y, 1 - p.x), (p.yn, 1 - p.y, p.x), (p.diag, 1 - p.y, 1 - p.x)))]

    def along_z(self, dz):
        p = self.p
        return p.copy(self.r0.at[p.y, p.x, pl.ds(pl.multiple_of(24 * p.up(dz), 8), 24)], self.r2.at[dz - 1],
                      self.send.at[3 + dz], self.recv.at[3 + dz], z=p.up(dz))

    def s0(self):
        self.across().start()

    def s1(self):
        p = self.p
        self.across().wait_recv()
        for a in range(2):
            for b in range(2):
                self.r0[a, b] = self.r0[a, b] + self.src[a, b, p.k]
        for copy in self.plane():
            copy.start()

    def s2(self):
        p = self.p
        for copy in self.plane():
            copy.wait_recv()
        self.r0[p.y, p.x] = self.r0[p.y, p.x] + self.r1[0] + self.r1[1] + self.r1[2]
        for dz in (1, 2, 3):
            self.along_z(dz).start()

    def s3(self):
        p = self.p
        for dz in (1, 2, 3):
            self.along_z(dz).wait_recv()
        own = self.r0[p.y, p.x, pl.ds(pl.multiple_of(24 * p.z, 8), 24), :]
        return own + self.r2[0] + self.r2[1] + self.r2[2]

    def sent(self):
        for copy in [self.across()] + self.plane() + [self.along_z(dz) for dz in (1, 2, 3)]:
            copy.wait_send()


def piece_masks(width, total, count):
    lane = lax.broadcasted_iota(jnp.int32, (1, total), 1)
    inside = lax.rem(lane, width)
    place = lax.broadcasted_iota(jnp.int32, (128, total), 0) == inside
    owner = lax.broadcasted_iota(jnp.int32, (count, total), 0) * width == lane - inside
    return place, owner


def unpack_small(pieces, first, number, width, total):
    place, owner = piece_masks(width, total, 32)
    place = place.astype(BF)
    out = []
    for n in range(number):
        spread = mm(pieces[:, first + n, :].astype(BF), place)
        out.append(jnp.sum(jnp.where(owner, spread, 0.0), axis=0, keepdims=True))
    return out


def pack_small(pieces, first, vectors, width, total):
    place, owner = piece_masks(width, total, 32)
    place = place.astype(F32)
    for n, vector in enumerate(vectors):
        spread = jnp.where(owner, vector, 0.0)
        pieces[:, first + n, :] = lax.dot_general(spread, place, NT, precision=lax.Precision.HIGHEST,
                                                  preferred_element_type=F32)


def weight(w, c):
    return w[c].reshape(768, 768)


def lane_block(start):
    return pl.ds(pl.multiple_of(start, 128), 128)


def project_group(g, tok, w, bqkv, conv, qkv, pkv, kvf):
    for r in range(2):
        rows = pl.ds(512 * r, 512)
        low = (mm(tok[rows, :], weight(w, g)) + bqkv[g]).astype(BF)
        qkv[g, rows, :] = low
        for part in range(4):
            kvf[part, pl.ds(8 + 512 * r, 512), :] = low[:, 256 + 128 * part:384 + 128 * part].astype(F32)
    for part in range(4):
        cols = pl.ds(128 * part, 128)
        total = jnp.zeros((256, 128), F32)
        for t in range(5):
            total = total + conv[g, pl.ds(t, 1), cols] * kvf[part, pl.ds(6 + t, 256, stride=4), :]
        pkv[g, :, cols] = total.astype(BF)


def attend_block(g, b, qkv, pkv, ctx, lse):
    ns, ps, near, far = window(b)
    rows = pl.ds(pl.multiple_of(b * 128, 128), 128)
    for pr in range(2):
        qm = head_split(qkv[g, rows, 128 * pr:128 * pr + 128], 0.125)
        kn = qkv[g, pl.ds(ns, 256), 256 + 128 * pr:384 + 128 * pr]
        kp = pkv[g, pl.ds(ps, 160), 128 * pr:128 * pr + 128]
        sn = jnp.where(near, mm_nt(kn, qm), -1e30)
        sp = jnp.where(far, mm_nt(kp, qm), -1e30)
        peak = jnp.maximum(jnp.max(sn, axis=0, keepdims=True), jnp.max(sp, axis=0, keepdims=True))
        en = jnp.exp(sn - peak)
        ep = jnp.exp(sp - peak)
        total = jnp.sum(en, axis=0, keepdims=True) + jnp.sum(ep, axis=0, keepdims=True)
        vn = qkv[g, pl.ds(ns, 256), 512 + 128 * pr:640 + 128 * pr]
        vp = pkv[g, pl.ds(ps, 160), 256 + 128 * pr:384 + 128 * pr]
        out = mm_tn(vn, en.astype(BF)) + mm_tn(vp, ep.astype(BF))
        out = out * pl.reciprocal(total)
        ctx[rows, lane_block(256 * g + 128 * pr)] = head_join(out).T.astype(BF)
        lse[(g * 2 + pr) * 8 + b] = peak + jnp.log(total)


def clear_edges(kvf):
    kvf[:, 0:8, :] = jnp.zeros((4, 8, 128), F32)
    kvf[:, 1032:1040, :] = jnp.zeros((4, 8, 128), F32)


def forward_kernel(comm, *refs):
    if comm:
        (tok, wqkv, bq_own, cv_own, wout, *six, wup, bu_own, wdn, pos, cot,
         out, dpre, gff, gsm, gbup, qkv_out, pkv, ctx, lse, w_out, conv,
         w, buf, act, gp, acc, first, dbr, tr, kvf, stage, sems, csem,
         slab, slab_s, dense_s, pieces, bqkv, vec, bup,
         zs, zr, xs, xr, ks, kr, ss, sr) = refs
    else:
        (tok, w_in, bqkv, conv, vec, bup, pos, cot,
         out, dpre, gff, gsm, gbup, qkv_out, pkv, ctx, lse,
         w, buf, act, gp, acc, first, dbr, tr, kvf, stage, sems, csem) = refs
    pre = dpre
    qkv = buf
    clear_edges(kvf)
    gbup[...] = jnp.zeros_like(gbup)
    todo = []
    if comm:
        p = Place()
        big = Gather(p, slab, w, (zs, zr, xs, xr, ks, kr))
        tiny = SmallGather(p, slab_s, dense_s, ss, sr)
        slab_s[p.z] = jnp.zeros((24, 128), F32)
        slab_s[p.z, 0:1, 0:72] = bq_own[...].astype(F32)
        slab_s[p.z, 1:6, 0:48] = cv_own[...].astype(F32)
        for i in range(6):
            slab_s[p.z, 6 + i:7 + i, 0:24] = six[i][...].astype(F32)
        slab_s[p.z, 12:13, 0:96] = bu_own[...].astype(F32)
        p.greet()
        tiny.s1()
        for c in range(12):
            if c < 3:
                rows24 = jnp.concatenate([wqkv[:, 768 * i + 256 * c:768 * i + 256 * c + 256] for i in range(3)], axis=1)
            elif c == 3:
                rows24 = wout[...].astype(F32).T
            elif c % 2 == 0:
                rows24 = wup[:, 384 * (c - 4):384 * (c - 4) + 768]
            else:
                rows24 = wdn[384 * (c - 5):384 * (c - 5) + 768, :].astype(F32).T
            slab[c, p.z] = slab_of(rows24.astype(F32))
            big.s1(c)
        tiny.s2()
        big.s2(0)
        big.s2(1)
        tiny.s3()
        big.s3(0)
        big.s2(2)
        big.s3(1)
        big.s4(0)
        tiny.s4()
        pieces[...] = dense_s[...].reshape(32, 24, 128)
        whole = unpack_small(pieces, 0, 1, 72, 2304)[0]
        for g in range(3):
            for i in range(3):
                bqkv[g, :, 256 * i:256 * i + 256] = whole[:, 768 * i + 256 * g:768 * i + 256 * g + 256]
        taps = unpack_small(pieces, 1, 5, 48, 1536)
        for t in range(5):
            for g in range(3):
                for i in range(2):
                    conv[g, t:t + 1, 256 * i:256 * i + 256] = taps[t][:, 768 * i + 256 * g:768 * i + 256 * g + 256]
        rest = unpack_small(pieces, 6, 6, 24, 768)
        for i in range(6):
            vec[i:i + 1, :] = rest[i]
        whole = unpack_small(pieces, 12, 1, 96, 3072)[0]
        for j in range(4):
            bup[j] = whole[:, 768 * j:768 * j + 768]
        big.s5(0)
        todo = [(big.s3, 8), (big.s2, 9), (big.s4, 7), (big.s3, 9), (big.s2, 10), (big.s4, 8), (big.s3, 10), (big.s2, 11),
                (big.s4, 9), (big.s3, 11), (big.s4, 10), (big.s4, 11)]
    else:
        load = pltpu.make_async_copy(w_in, w, csem.at[0])
        load.start()
        load.wait()

    def progress(count):
        for _ in range(min(count, len(todo))):
            step, c = todo.pop(0)
            step(c)

    def group(g, carry):
        if comm:
            @pl.when(g > 0)
            def _():
                big.s5(g)
        project_group(g, tok, w, bqkv, conv, qkv, pkv, kvf)

        def block(b, inner):
            attend_block(g, b, qkv, pkv, ctx, lse)
            if comm:
                i = 8 * g + b

                @pl.when(lax.rem(i, 4) == 0)
                def _():
                    n = lax.div(i, 4)
                    big.s3(2 + n)
                    big.s2(3 + n)

                @pl.when(lax.rem(i, 4) == 2)
                def _():
                    big.s4(1 + lax.div(i, 4))
            return inner

        return lax.fori_loop(0, 8, block, carry)

    lax.fori_loop(0, 3, group, 0)
    keep = pltpu.make_async_copy(qkv.at[pl.ds(0, 3)], qkv_out, csem.at[0])
    keep.start()
    if comm:
        big.s5(3)
        keep_w = pltpu.make_async_copy(w.at[pl.ds(0, 4)], w_out, csem.at[1])
        keep_w.start()
    b_out, gain1, shift1, b_down, gain2, shift2 = [vec[pl.ds(i, 1), :] for i in range(6)]
    sums = [jnp.zeros((1, 768), F32) for _ in range(5)]
    tiles = [pl.ds(512 * r, 512) for r in range(2)]
    for rows in tiles:
        pre_one = tok[rows, :].astype(F32) + mm_nt(ctx[rows, :], weight(w, 3)) + b_out
        pre[rows, :] = pre_one
        xhat, rate = norm_stats(pre_one)
        low = (xhat * gain1 + shift1).astype(BF)
        first[rows, :] = low
        acc[rows, :] = low.astype(F32) + b_down
        progress(1)
    for j in range(4):
        if comm:
            big.s5(4 + 2 * j)
            big.s5(5 + 2 * j)
        for rows in tiles:
            value, slope = gelu_both(mm(first[rows, :], weight(w, 4 + 2 * j)) + bup[j])
            low = value.astype(BF)
            act[j, rows, :] = low
            gp[j, rows, :] = slope.astype(BF)
            acc[rows, :] += mm_nt(low, weight(w, 5 + 2 * j))
            progress(3 if j < 3 else 12)
    for r, rows in enumerate(tiles):
        xhat, rate = norm_stats(acc[rows, :])
        out[rows, :] = (xhat * gain2 + shift2).astype(BF)
        row = 512 * r + lax.broadcasted_iota(jnp.int32, (512, 160), 0)
        dy = mm((row == pos[...]).astype(BF), cot[...])
        sums[3] = sums[3] + colsum(dy * xhat)
        sums[4] = sums[4] + colsum(dy)
        dacc = norm_back(xhat, rate, gain2, dy)
        low = dacc.astype(BF)
        dbr[rows, :] = low
        acc[rows, :] = dacc
        sums[2] = sums[2] + colsum(low.astype(F32))
    keep.wait()
    dh = buf
    sent = []

    def emit(n, left, right):
        if n >= 2:
            sent[n - 2].wait()
        stage[n % 2] = mm(left[...], right).astype(BF).reshape(2, 2, 2, 96, 768)
        sent.append(pltpu.make_async_copy(stage.at[n % 2], gff.at[n], sems.at[n % 2]))
        sent[n].start()

    tr[...] = dbr[...].T
    for j in range(4):
        emit(j, tr, act[j])
    tr[...] = first[...].T
    for j in range(4):
        for rows in tiles:
            low = (mm(dbr[rows, :], weight(w, 5 + 2 * j)) * gp[j, rows, :].astype(F32)).astype(BF)
            dh[j, rows, :] = low
            gbup[j] += colsum(low.astype(F32))
            acc[rows, :] += mm_nt(low, weight(w, 4 + 2 * j))
        emit(4 + j, tr, dh[j])
    for rows in tiles:
        xhat, rate = norm_stats(pre[rows, :])
        dacc = acc[rows, :]
        sums[0] = sums[0] + colsum(dacc * xhat)
        sums[1] = sums[1] + colsum(dacc)
        dpre[rows, :] = norm_back(xhat, rate, gain1, dacc)
    for i in range(5):
        gsm[pl.ds(i, 1), :] = sums[i]
    sent[6].wait()
    sent[7].wait()
    if comm:
        keep_w.wait()
        big.sent(12)
        tiny.sent()


def forward_call(comm, *args):
    outs = [
        (struct((1024, 768), BF), VM), (struct((1024, 768), F32), VM), (struct((8, 2, 2, 2, 96, 768), BF), ANY),
        (struct((8, 768), F32), VM), (struct((4, 1, 768), F32), VM), (struct((3, 1024, 768), BF), ANY),
        (struct((3, 256, 512), BF), VM), (struct((1024, 768), BF), VM), (struct((48, 1, 256), F32), VM),
    ]
    scratch = [
        pltpu.VMEM((12, 2, 2, 2, 96, 768), BF), pltpu.VMEM((4, 1024, 768), BF), pltpu.VMEM((4, 1024, 768), BF),
        pltpu.VMEM((4, 1024, 768), BF), pltpu.VMEM((1024, 768), F32), pltpu.VMEM((1024, 768), BF),
        pltpu.VMEM((1024, 768), BF), pltpu.VMEM((768, 1024), BF), pltpu.VMEM((4, 1040, 128), F32),
        pltpu.VMEM((2, 2, 2, 2, 96, 768), BF), DMA((2,)), DMA((2,)),
    ]
    if comm:
        outs += [(struct((4, 2, 2, 2, 96, 768), BF), ANY), (struct((3, 8, 512), F32), VM)]
        scratch += [
            pltpu.VMEM((12, 4, 16, 1152), BF), pltpu.VMEM((4, 24, 128), F32), pltpu.VMEM((2, 2, 2, 4, 24, 128), F32),
            pltpu.VMEM((32, 24, 128), F32), pltpu.VMEM((3, 1, 768), F32), pltpu.VMEM((8, 768), F32),
            pltpu.VMEM((4, 1, 768), F32),
            DMA((12, 3)), DMA((12, 3)), DMA((12, 4)), DMA((12, 4)), DMA((12,)), DMA((12,)), DMA((7,)), DMA((7,)),
        ]
        params = pltpu.CompilerParams(vmem_limit_bytes=LIMIT, collective_id=1, has_side_effects=True)
    else:
        params = pltpu.CompilerParams(vmem_limit_bytes=LIMIT)
    ins = [VM] * len(args)
    if not comm:
        ins[1] = ANY
    return pl.pallas_call(
        functools.partial(forward_kernel, comm), in_specs=ins, out_specs=[o[1] for o in outs],
        out_shape=[o[0] for o in outs], scratch_shapes=scratch, compiler_params=params, name="forward")(*args)


def back_block(g, b, qkv, pkv, dctx, lse, dk, dv, dpk, dpv, dproj):
    ns, ps, near, far = window(b)
    rows = pl.ds(pl.multiple_of(b * 128, 128), 128)
    nr, prow = pl.ds(ns, 256), pl.ds(ps, 160)
    for pr in range(2):
        ln = pl.ds(128 * pr, 128)
        qm = head_split(qkv[g, rows, 128 * pr:128 * pr + 128], 0.125)
        dm = head_split(dctx[rows, lane_block(256 * g + 128 * pr)], 1.0)
        kn = qkv[g, nr, 256 + 128 * pr:384 + 128 * pr]
        kp = pkv[g, prow, 128 * pr:128 * pr + 128]
        vn = qkv[g, nr, 512 + 128 * pr:640 + 128 * pr]
        vp = pkv[g, prow, 256 + 128 * pr:384 + 128 * pr]
        ls = lse[(g * 2 + pr) * 8 + b]
        pn = jnp.exp(jnp.where(near, mm_nt(kn, qm), -1e30) - ls)
        pp = jnp.exp(jnp.where(far, mm_nt(kp, qm), -1e30) - ls)
        dn = mm_nt(vn, dm)
        dp = mm_nt(vp, dm)
        rd = jnp.sum(pn * dn, axis=0, keepdims=True) + jnp.sum(pp * dp, axis=0, keepdims=True)
        sn = (pn * (dn - rd)).astype(BF)
        sp = (pp * (dp - rd)).astype(BF)
        dk[nr, ln] += mm(sn, qm)
        dpk[prow, ln] += mm(sp, qm)
        dv[nr, ln] += mm(pn.astype(BF), dm)
        dpv[prow, ln] += mm(pp.astype(BF), dm)
        r = mm_tn(kn, sn) + mm_tn(kp, sp)
        dproj[g, rows, ln] = (head_join(r).T * 0.125).astype(BF)


def pool_back(g, conv, qkv, kvf, dk, dv, dpk, dpv, dproj, gconv):
    for part in range(4):
        kvf[part, 8:1032, :] = qkv[g, :, 256 + 128 * part:384 + 128 * part].astype(F32)
    for part in range(4):
        cols = pl.ds(128 * part, 128)
        src, dst = (dpk, dk) if part < 2 else (dpv, dv)
        half = pl.ds(128 * (part % 2), 128)
        dpool = src[:, half]
        for t in range(5):
            gconv[g, pl.ds(t, 1), cols] = colsum(dpool * kvf[part, pl.ds(6 + t, 256, stride=4), :])
        kvf[part, 8:1032, :] = dst[:, half]
        for t in range(5):
            at = pl.ds(6 + t, 256, stride=4)
            kvf[part, at, :] += conv[g, pl.ds(t, 1), cols] * dpool
        dproj[g, :, 256 + 128 * part:384 + 128 * part] = kvf[part, 8:1032, :].astype(BF)
        kvf[part, 0:8, :] = jnp.zeros((8, 128), F32)
        kvf[part, 1032:1040, :] = jnp.zeros((8, 128), F32)


def backward_kernel(comm, *refs):
    tok, w, conv, dpre, qkv, pkv, ctx, lse = refs[:8]
    if comm:
        (gff, gsm, gbup, gtok, gqkv, gqb, gcv, gwo, gbo, gg1, gs1, gwu, gbu, gwd, gbd, gg2, gs2,
         kvf, dk, dv, dpk, dpv, dctx, dproj, tr,
         gat, gconv, gbias, gbout, r0, r1a, r1b, r2, v, r3, fin, own, pieces, small, t0, t1, t2,
         ks, kr, xs, xr, zs, zr, ls, ss, sr) = refs[8:]
    else:
        (gtok, gat, gconv, gbias, gbout, kvf, dk, dv, dpk, dpv, dctx, dproj, tr) = refs[8:]
    clear_edges(kvf)
    if comm:
        p = Place()
        big = Scatter(p, r0, r1a, r1b, r2, v, r3, fin, (ks, kr, xs, xr, zs, zr))
        tiny = SmallScatter(p, small, t0, t1, t2, ss, sr)
        p.greet()

        def fetch_ff(c):
            return pltpu.make_async_copy(gff.at[c, :, :, p.k], own.at[lax.rem(c, 2)], ls.at[lax.rem(c, 2)])

        def fetch(c):
            @pl.when(c < 8)
            def _():
                fetch_ff(c).start()

            @pl.when(c == 8)
            def _():
                pltpu.make_async_copy(gat.at[3, :, :, p.k], own.at[lax.rem(c, 2)], ls.at[lax.rem(c, 2)]).start()

            @pl.when(c > 8)
            def _():
                pltpu.make_async_copy(gat.at[lax.max(c - 9, 0), :, :, p.k], own.at[lax.rem(c, 2)], ls.at[lax.rem(c, 2)]).start()

        def start_ff(c, carry):
            big.across(c, gff.at[c]).start()
            return carry

        lax.fori_loop(0, 8, start_ff, 0)
        fetch_ff(0).start()
        fetch_ff(1).start()
    da = dpre[...].astype(BF)
    gbout[...] = colsum(da.astype(F32))
    tr[...] = da.T
    for r in range(2):
        rows = pl.ds(512 * r, 512)
        dctx[rows, :] = mm(dpre[rows, :].astype(BF), weight(w, 3)).astype(BF)
    gat[3] = mm(tr[...], ctx[...]).astype(BF).reshape(2, 2, 2, 96, 768)
    if comm:
        big.across(8, gat.at[3]).start()
    tr[...] = tok[...].T

    def group(g, carry):
        dk[...] = jnp.zeros_like(dk)
        dv[...] = jnp.zeros_like(dv)
        dpk[...] = jnp.zeros_like(dpk)
        dpv[...] = jnp.zeros_like(dpv)

        def block(b, inner):
            if comm:
                i = 8 * g + b
                n = lax.div(i, 2)

                @pl.when((lax.rem(i, 2) == 0) & (n < 11))
                def _():
                    pltpu.make_async_copy(gff.at[0, :, :, p.k], own.at[lax.rem(n, 2)], ls.at[lax.rem(n, 2)]).wait()
                    big.s1(n, gff.at[0], lambda a, b2: own[lax.rem(n, 2), a, b2])
                    pl.when(n < 9)(lambda: fetch(n + 2))

                @pl.when((lax.rem(i, 2) == 1) & (i >= 3))
                def _():
                    big.s2(n - 1)

                @pl.when((lax.rem(i, 2) == 1) & (i >= 5))
                def _():
                    big.s3(n - 2)

                @pl.when((lax.rem(i, 2) == 0) & (i >= 8))
                def _():
                    big.s4(n - 4)
            back_block(g, b, qkv, pkv, dctx, lse, dk, dv, dpk, dpv, dproj)
            return inner

        lax.fori_loop(0, 8, block, 0)
        pool_back(g, conv, qkv, kvf, dk, dv, dpk, dpv, dproj, gconv)
        gat[g] = mm(tr[...], dproj[g]).astype(BF).reshape(2, 2, 2, 96, 768)
        gbias[g] = colsum(dproj[g].astype(F32))
        if comm:
            big.across(9 + g, gat.at[g]).start()
        return carry

    lax.fori_loop(0, 3, group, 0)

    def token_part(n):
        rows = pl.ds(256 * n, 256)
        acc = dpre[rows, :]
        for g in range(3):
            acc = acc + mm_nt(dproj[g, rows, :], weight(w, g))
        gtok[rows, :] = acc

    if not comm:
        for n in range(4):
            token_part(n)
        return

    pieces[...] = jnp.zeros_like(pieces)
    kinds = [jnp.concatenate([gbias[g][:, 256 * i:256 * i + 256] for i in range(3) for g in range(3)], axis=1)]
    pack_small(pieces, 0, kinds, 72, 2304)
    pack_small(pieces, 1, [
        jnp.concatenate([gconv[g, t:t + 1, 256 * i:256 * i + 256] for i in range(2) for g in range(3)], axis=1)
        for t in range(5)], 48, 1536)
    pack_small(pieces, 6, [gbout[...]] + [gsm[i:i + 1, :] for i in range(5)], 24, 768)
    pack_small(pieces, 12, [jnp.concatenate([gbup[j] for j in range(4)], axis=1)], 96, 3072)
    small[...] = pieces[...].reshape(2, 2, 2, 96, 128)
    tiny.s0()
    big.s1(11, gff.at[0], lambda a, b: gat[2, a, b, p.k])
    big.s3(10)
    token_part(0)
    big.s2(11)
    tiny.s1()
    big.s4(8)
    token_part(1)
    big.s3(11)
    tiny.s2()
    big.s4(9)
    token_part(2)
    big.s4(10)
    token_part(3)
    for j in range(4):
        gwd[768 * j:768 * j + 768, :] = fin[j].T
        gwu[:, 768 * j:768 * j + 768] = fin[4 + j]
    gwo[...] = fin[8].T
    total = tiny.s3()
    gqb[...] = total[0:1, 0:72]
    gcv[...] = total[1:6, 0:48]
    for i, ref in enumerate((gbo, gg1, gs1, gbd, gg2, gs2)):
        ref[...] = total[6 + i:7 + i, 0:24]
    gbu[...] = total[12:13, 0:96]
    big.s4(11)
    for g in range(3):
        for i in range(3):
            gqkv[:, 768 * i + 256 * g:768 * i + 256 * g + 256] = fin[9 + g, :, 256 * i:256 * i + 256]

    def drain(c, carry):
        big.sent(c, gff.at[0])
        return carry

    lax.fori_loop(0, 12, drain, 0)
    tiny.sent()


def backward_call(comm, *args):
    scratch = [
        pltpu.VMEM((4, 1040, 128), F32), pltpu.VMEM((1024, 256), F32), pltpu.VMEM((1024, 256), F32),
        pltpu.VMEM((256, 256), F32), pltpu.VMEM((256, 256), F32), pltpu.VMEM((1024, 768), BF),
        pltpu.VMEM((3, 1024, 768), BF), pltpu.VMEM((768, 1024), BF),
    ]
    ins = [VM] * len(args)
    local = [((4, 2, 2, 2, 96, 768), BF), ((3, 8, 512), F32), ((3, 1, 768), F32), ((1, 768), F32)]
    outs = [struct((1024, 768), F32)]
    if comm:
        ins[8] = ANY
        outs += [struct(s, F32) for s in ((24, 2304), (1, 72), (5, 48), (768, 24), (1, 24), (1, 24), (1, 24), (24, 3072), (1, 96),
                                          (3072, 24), (1, 24), (1, 24), (1, 24))]
        scratch += [pltpu.VMEM(*s) for s in local]
        scratch += [
            pltpu.VMEM((12, 2, 2, 96, 768), BF), pltpu.VMEM((12, 2, 96, 384), BF), pltpu.VMEM((12, 2, 96, 384), BF),
            pltpu.VMEM((12, 2, 96, 384), BF), pltpu.VMEM((12, 4, 16, 1152), BF), pltpu.VMEM((12, 3, 16, 1152), BF),
            pltpu.VMEM((12, 24, 768), F32), pltpu.VMEM((2, 2, 2, 96, 768), BF), pltpu.VMEM((32, 24, 128), F32),
            pltpu.VMEM((2, 2, 2, 96, 128), F32), pltpu.VMEM((2, 2, 96, 128), F32), pltpu.VMEM((3, 96, 128), F32),
            pltpu.VMEM((3, 24, 128), F32),
            DMA((12,)), DMA((12,)), DMA((12, 4)), DMA((12, 4)), DMA((12, 3)), DMA((12, 3)), DMA((2,)), DMA((7,)), DMA((7,)),
        ]
        params = pltpu.CompilerParams(vmem_limit_bytes=LIMIT, collective_id=2, has_side_effects=True)
    else:
        outs += [struct(*s) for s in local]
        params = pltpu.CompilerParams(vmem_limit_bytes=LIMIT)
    return pl.pallas_call(
        functools.partial(backward_kernel, comm), in_specs=ins, out_specs=[VM] * len(outs), out_shape=outs,
        scratch_shapes=scratch, compiler_params=params, name="backward")(*args)


def shards_direct(tokens, w_qkv, b_qkv, conv_kv, w_out, b_out, gain_one, shift_one, w_up, b_up, w_down, b_down, gain_two,
                  shift_two, positions, cotangent):
    tok = tokens[0]
    out, dpre, gff, gsm, gbup, qkv, pkv, ctx, lse, w, conv = forward_call(
        True, tok, w_qkv, b_qkv[None], conv_kv, w_out, b_out[None], gain_one[None], shift_one[None], b_down[None],
        gain_two[None], shift_two[None], w_up, b_up[None], w_down, positions, cotangent[0])
    (gtok, gqkv, gqb, gcv, gwo, gbo, gg1, gs1, gwu, gbu, gwd, gbd, gg2, gs2) = backward_call(
        True, tok, w, conv, dpre, qkv, pkv, ctx, lse, gff, gsm, gbup)
    return (out[None], gtok[None], gqkv, gqb[0], gcv, gwo, gbo[0], gg1[0], gs1[0], gwu, gbu[0], gwd, gbd[0], gg2[0], gs2[0])


def small_sizes(count):
    return [2304 // count] + [1536 // count] * 5 + [768 // count] * 6 + [3072 // count]


def by_group(v, kinds):
    return v.reshape(kinds, 3, 256).transpose(1, 0, 2).reshape(3, 1, kinds * 256)


def shards_general(tokens, w_qkv, b_qkv, conv_kv, w_out, b_out, gain_one, shift_one, w_up, b_up, w_down, b_down, gain_two,
                   shift_two, positions, cotangent):
    rows = w_qkv.shape[0]
    count = 768 // rows
    blocks = (2, 2, 2, 96, 768)
    up = w_up.reshape(rows, 4, 768).transpose(1, 0, 2)
    down = w_down.reshape(4, 768, rows).transpose(0, 2, 1)
    own = jnp.concatenate([
        w_qkv.reshape(rows, 3, 3, 256).transpose(2, 0, 1, 3).reshape(3, rows, 768),
        w_out.T[None],
        jnp.stack([up, down], 1).reshape(8, rows, 768),
    ], 0)
    w = lax.all_gather(own, AXES, axis=1, tiled=True).reshape((12,) + blocks)
    small = jnp.concatenate([b_qkv, conv_kv.reshape(-1), b_out, gain_one, shift_one, b_down, gain_two, shift_two, b_up])
    small = lax.all_gather(small[None], AXES, axis=0, tiled=True).astype(F32)
    at, parts = 0, []
    for size in small_sizes(count):
        parts.append(small[:, at:at + size].reshape(-1))
        at += size
    bqkv = by_group(parts[0], 3)
    conv = jnp.concatenate([by_group(p, 2) for p in parts[1:6]] + [jnp.zeros((3, 3, 512), F32)], 1)
    vec = jnp.stack(parts[6:12] + [jnp.zeros((768,), F32)] * 2)
    bup = parts[12].reshape(4, 1, 768)
    out, dpre, gff, gsm, gbup, qkv, pkv, ctx, lse = forward_call(
        False, tokens[0], w, bqkv, conv, vec, bup, positions, cotangent[0])
    gff = lax.psum_scatter(gff.reshape(8, 768, 768), AXES, scatter_dimension=1, tiled=True).astype(F32)
    gtok, gat, gconv, gbias, gbout = backward_call(False, tokens[0], w[:4], conv, dpre, qkv, pkv, ctx, lse)
    gat = lax.psum_scatter(gat.reshape(4, 768, 768), AXES, scatter_dimension=1, tiled=True).astype(F32)
    flat = [gbias.reshape(3, 3, 256).transpose(1, 0, 2).reshape(count, -1)]
    flat += [gconv[:, t].reshape(3, 2, 256).transpose(1, 0, 2).reshape(count, -1) for t in range(5)]
    flat += [gbout[0].reshape(count, -1)] + [gsm[i].reshape(count, -1) for i in range(5)] + [gbup.reshape(count, -1)]
    flat = lax.psum_scatter(jnp.concatenate(flat, 1), AXES, scatter_dimension=0, tiled=True)
    at, s = 0, []
    for size in small_sizes(count):
        s.append(flat[0, at:at + size])
        at += size
    return (
        out[None], gtok[None],
        gat[:3].reshape(3, rows, 3, 256).transpose(1, 2, 0, 3).reshape(rows, 2304),
        s[0], jnp.stack(s[1:6]), gat[3].T, s[6], s[7], s[8],
        gff[4:].transpose(1, 0, 2).reshape(rows, 3072), s[12],
        gff[:4].transpose(0, 2, 1).reshape(3072, rows), s[9], s[10], s[11],
    )


def solution(mesh):
    rows, cols, flat, item = P(AXES, None), P(None, AXES), P(AXES), P(AXES, None, None)
    direct = mesh.shape["dp"] == 8 and mesh.shape["fsdp"] == 4
    return jax.shard_map(
        shards_direct if direct else shards_general,
        mesh=mesh,
        in_specs=(item, rows, flat, cols, cols, flat, flat, flat, rows, flat, cols, flat, flat, flat, rows, item),
        out_specs=(item, item, rows, flat, cols, cols, flat, flat, flat, rows, flat, cols, flat, flat, flat),
        check_vma=False,
    )
```

time: 643 us -> 249 us (0.39)
  waiting for transfers between devices: 400 us -> 0 us
  Pallas kernels: 131 us -> 226 us
  blocking collectives: 43.4 us -> 0 us
  local copies, waits for them, and re-layouts: 44.4 us -> 18.6 us
  between operations: 14.5 us -> 0.94 us
    unnamed x7 -> x0, waiting for transfers between devices: 347 us -> none
    pallas_call x2, Pallas kernels: 131 us -> 226 us  [the longest x1 129 us: forward_call(): pl.pallas_call(functools.partial(forward_kernel, comm), in_specs=ins, out...]
    all_gather x1 -> x0, waiting for transfers between devices: 53.1 us -> none  [shards(): w = lax.all_gather(own, AXES, axis=1, tiled=True)]
    unnamed x1 -> x0, blocking collectives: 43.4 us -> none
    concatenate x3 -> x0, local copies, waits for them, and re-layouts: 6.85 us -> none  [the longest x1 5.42 us: small_pack(): return jnp.concatenate([qb, cv.reshape(-1)] + six + [ub])]
    unnamed x12 -> x41, local copies, waits for them, and re-layouts: 20.2 us -> 18.6 us
  transfers between devices with their start and end apart: 4 -> 0, of which waited for: 4 -> 0; matrix products, arithmetic and copies ran while one was open for 6% -> 0% of each run, Pallas kernels for 0% -> 0%
where the time goes in v2:
time: 249 us; the launch traced here: 245 us
  Pallas kernels  226 us (91%)
  local copies, waits for them, and re-layouts  18.6 us (7%)
    pallas_call x1, Pallas kernels, forward_call(): pl.pallas_call(functools.partial(forward_kernel, comm), in_specs=ins, out...  129 us
    pallas_call x1, Pallas kernels, backward_call(): pl.pallas_call(functools.partial(backward_kernel, comm), in_specs=ins, ou...  96.7 us
    unnamed x41, local copies, waits for them, and re-layouts  18.6 us

profile of v2, /device:TPU:0, one launch (start us, length us, event | category | flops | bytes accessed | tf_op | source)
XLA Modules:
  0.0 245.4 jit_solution(14577360568630670797)
XLA Ops:
  0.6 1.6 copy.31.refs_4_
  2.2 2.1 copy.32.refs_13_
  4.3 129.2 %forward.1 = (bf16[1024,768]{1,0:T(8,128)(2,1)}, f32[1024,768]{1,0:T(8,128)}, bf16[8,2,2,2,96,768]{5,4,3,2,1,0:T(8,128)(2,1)}, f32[8,768]{1,0:T(8,128)}, f32[4,1...) custom-call(bf16[1024,768]{1,0:T(8,128)(2,1)} %bitcast.20, ...), custom_call_target="tpu_custom_call" | custom-call | tf_op jit(solution)/shard_map/forward/pallas_call | solution.py:652
  133.5 96.7 %backward.1 = (f32[1024,768]{1,0:T(8,128)}, f32[24,2304]{1,0:T(8,128)}, f32[1,72]{1,0:T(1,128)}, f32[5,48]{1,0:T(8,128)}, f32[768,24]{1,0:T(8,128)}, /*index=5*/...) custom-call(bf16[1024,768]{1,0:T(8,128)(2,1)} %bitcast.21, ...), custom_call_target="tpu_custom_call" | custom-call | tf_op jit(solution)/shard_map/backward/pallas_call | solution.py:879
  230.2 0.0 copy-start
  230.2 1.9 copy.33
  232.2 2.6 %copy.34 = f32[3072,24]{0,1:T(8,128)} copy(f32[3072,24]{1,0:T(8,128)} %get-tuple-element.76) | data formatting | bytes 589824
  234.7 2.7 %copy.48 = bf16[1,1024,768]{2,1,0:T(8,128)(2,1)} copy(bf16[1,1024,768]{2,1,0:T(8,128)(2,1)} %bitcast.23) | data formatting | bytes 3145728
  237.4 0.0 copy-start.10
  237.4 0.0 copy-start.9
  237.4 0.0 copy-start.8
  237.4 0.0 copy-start.1
  237.5 1.7 copy.49
  239.1 0.7 copy.50
  239.8 0.5 copy.51
  240.3 0.6 copy.52
  240.9 0.5 copy.53
  241.4 0.5 copy.54
  242.0 0.5 copy.55
  242.5 0.7 copy.56
  243.2 0.5 copy.57
  243.7 0.5 copy.58
  244.2 0.5 copy.59
  244.7 0.5 copy.60
  (19 shorter events, 0.0 us)
Async XLA Ops:
  230.2 7.1 %copy-start = (f32[1024,768]{1,0:T(8,128)S(1)}, f32[1024,768]{1,0:T(8,128)}, u32[]{:S(2)}) copy-start(f32[1024,768]{1,0:T(8,128)} %get-tuple-element.51) | copy-start | bytes 9437188
  237.4 1.8 copy-start.2
  237.4 2.4 copy-start.11
  237.4 3.0 %copy-start.3 = (f32[5,48]{1,0:T(8,128)S(1)}, f32[5,48]{1,0:T(8,128)}, u32[]{:S(2)}) copy-start(f32[5,48]{1,0:T(8,128)} %get-tuple-element.99) | copy-start | bytes 2884
  237.4 3.5 %copy-start.10 = (f32[1,24]{1,0:T(1,128)S(1)}, f32[1,24]{1,0:T(1,128)}, u32[]{:S(2)}) copy-start(f32[1,24]{1,0:T(1,128)} %get-tuple-element.56) | copy-start | bytes 292
  237.4 4.1 %copy-start.9 = (f32[1,24]{1,0:T(1,128)S(1)}, f32[1,24]{1,0:T(1,128)}, u32[]{:S(2)}) copy-start(f32[1,24]{1,0:T(1,128)} %get-tuple-element.57) | copy-start | bytes 292
  237.4 4.6 %copy-start.8 = (f32[1,24]{1,0:T(1,128)S(1)}, f32[1,24]{1,0:T(1,128)}, u32[]{:S(2)}) copy-start(f32[1,24]{1,0:T(1,128)} %get-tuple-element.58) | copy-start | bytes 292
  237.4 5.1 %copy-start.1 = (f32[24,3072]{1,0:T(8,128)S(1)}, f32[24,3072]{1,0:T(8,128)}, u32[]{:S(2)}) copy-start(f32[24,3072]{1,0:T(8,128)} %get-tuple-element.104) | copy-start | bytes 884740
  237.4 5.8 %copy-start.7 = (f32[1,96]{1,0:T(1,128)S(1)}, f32[1,96]{1,0:T(1,128)}, u32[]{:S(2)}) copy-start(f32[1,96]{1,0:T(1,128)} %get-tuple-element.60) | copy-start | bytes 1156
  237.4 6.3 %copy-start.6 = (f32[1,24]{1,0:T(1,128)S(1)}, f32[1,24]{1,0:T(1,128)}, u32[]{:S(2)}) copy-start(f32[1,24]{1,0:T(1,128)} %get-tuple-element.62) | copy-start | bytes 292
  237.4 6.8 %copy-start.5 = (f32[1,24]{1,0:T(1,128)S(1)}, f32[1,24]{1,0:T(1,128)}, u32[]{:S(2)}) copy-start(f32[1,24]{1,0:T(1,128)} %get-tuple-element.63) | copy-start | bytes 292
  237.5 7.3 %copy-start.4 = (f32[1,24]{1,0:T(1,128)S(1)}, f32[1,24]{1,0:T(1,128)}, u32[]{:S(2)}) copy-start(f32[1,24]{1,0:T(1,128)} %get-tuple-element.64) | copy-start | bytes 292

commit v3 on v2

--- a/solution.py
+++ b/solution.py
@@ -386,11 +386,13 @@
 
 def pack_small(pieces, first, vectors, width, total):
     place, owner = piece_masks(width, total, 32)
-    place = place.astype(F32)
+    place = place.astype(BF)
     for n, vector in enumerate(vectors):
-        spread = jnp.where(owner, vector, 0.0)
-        pieces[:, first + n, :] = lax.dot_general(spread, place, NT, precision=lax.Precision.HIGHEST,
-                                                  preferred_element_type=F32)
+        high = vector.astype(BF)
+        low = (vector - high.astype(F32)).astype(BF)
+        both = jnp.concatenate([jnp.where(owner, high.astype(F32), 0.0), jnp.where(owner, low.astype(F32), 0.0)], axis=0)
+        both = mm_nt(both.astype(BF), place)
+        pieces[:, first + n, :] = both[:32] + both[32:]
 
 
 def weight(w, c):
@@ -445,18 +447,22 @@
 def forward_kernel(comm, *refs):
     if comm:
         (tok, wqkv, bq_own, cv_own, wout, *six, wup, bu_own, wdn, pos, cot,
-         out, dpre, gff, gsm, gbup, qkv_out, pkv, ctx, lse, w_out, conv,
-         w, buf, act, gp, acc, first, dbr, tr, kvf, stage, sems, csem,
-         slab, slab_s, dense_s, pieces, bqkv, vec, bup,
+         out_o, pre_o, first_o, acc_o, dbr_o, gp_o, gwd_o, qkv_o, pkv_o, ctx_o, lse_o, gsm, w_o, conv, vec,
+         w, buf, act, gp, acc, pre, first, dbr, tr, ctx, pkv, lse, out, kvf, stage, sems, osem,
+         slab, slab_s, dense_s, pieces, bqkv, bup,
          zs, zr, xs, xr, ks, kr, ss, sr) = refs
     else:
         (tok, w_in, bqkv, conv, vec, bup, pos, cot,
-         out, dpre, gff, gsm, gbup, qkv_out, pkv, ctx, lse,
-         w, buf, act, gp, acc, first, dbr, tr, kvf, stage, sems, csem) = refs
-    pre = dpre
+         out_o, pre_o, first_o, acc_o, dbr_o, gp_o, gwd_o, qkv_o, pkv_o, ctx_o, lse_o, gsm,
+         w, buf, act, gp, acc, pre, first, dbr, tr, ctx, pkv, lse, out, kvf, stage, sems, osem) = refs
     qkv = buf
     clear_edges(kvf)
-    gbup[...] = jnp.zeros_like(gbup)
+    kept = []
+
+    def keep(src, dst):
+        kept.append(pltpu.make_async_copy(src, dst, osem.at[len(kept)]))
+        kept[-1].start()
+
     todo = []
     if comm:
         p = Place()
@@ -468,18 +474,17 @@
         for i in range(6):
             slab_s[p.z, 6 + i:7 + i, 0:24] = six[i][...].astype(F32)
         slab_s[p.z, 12:13, 0:96] = bu_own[...].astype(F32)
-        p.greet()
-        tiny.s1()
         for c in range(12):
             if c < 3:
                 rows24 = jnp.concatenate([wqkv[:, 768 * i + 256 * c:768 * i + 256 * c + 256] for i in range(3)], axis=1)
             elif c == 3:
-                rows24 = wout[...].astype(F32).T
-            elif c % 2 == 0:
-                rows24 = wup[:, 384 * (c - 4):384 * (c - 4) + 768]
+                rows24 = wout[...]
             else:
-                rows24 = wdn[384 * (c - 5):384 * (c - 5) + 768, :].astype(F32).T
+                rows24 = (wup if c % 2 == 0 else wdn)[:, 768 * ((c - 4) // 2):768 * ((c - 4) // 2) + 768]
             slab[c, p.z] = slab_of(rows24.astype(F32))
+            if c == 0:
+                p.greet()
+                tiny.s1()
             big.s1(c)
         tiny.s2()
         big.s2(0)
@@ -488,6 +493,7 @@
         big.s3(0)
         big.s2(2)
         big.s3(1)
+        big.s2(3)
         big.s4(0)
         tiny.s4()
         pieces[...] = dense_s[...].reshape(32, 24, 128)
@@ -507,16 +513,15 @@
         for j in range(4):
             bup[j] = whole[:, 768 * j:768 * j + 768]
         big.s5(0)
-        todo = [(big.s3, 8), (big.s2, 9), (big.s4, 7), (big.s3, 9), (big.s2, 10), (big.s4, 8), (big.s3, 10), (big.s2, 11),
-                (big.s4, 9), (big.s3, 11), (big.s4, 10), (big.s4, 11)]
+        todo = [[(big.s2, 10), (big.s3, 8)], [(big.s4, 7), (big.s2, 11)], [(big.s3, 9)], [(big.s4, 8), (big.s3, 10)],
+                [(big.s4, 9), (big.s3, 11)], [(big.s4, 10)], [(big.s4, 11)]]
     else:
-        load = pltpu.make_async_copy(w_in, w, csem.at[0])
+        load = pltpu.make_async_copy(w_in, w, sems.at[0])
         load.start()
         load.wait()
 
-    def progress(count):
-        for _ in range(min(count, len(todo))):
-            step, c = todo.pop(0)
+    def progress():
+        for step, c in todo.pop(0) if todo else ():
             step(c)
 
     def group(g, carry):
@@ -534,8 +539,8 @@
                 @pl.when(lax.rem(i, 4) == 0)
                 def _():
                     n = lax.div(i, 4)
+                    big.s2(4 + n)
                     big.s3(2 + n)
-                    big.s2(3 + n)
 
                 @pl.when(lax.rem(i, 4) == 2)
                 def _():
@@ -545,14 +550,14 @@
         return lax.fori_loop(0, 8, block, carry)
 
     lax.fori_loop(0, 3, group, 0)
-    keep = pltpu.make_async_copy(qkv.at[pl.ds(0, 3)], qkv_out, csem.at[0])
-    keep.start()
+    keep(qkv.at[pl.ds(0, 3)], qkv_o)
+    keep(pkv, pkv_o)
+    keep(ctx, ctx_o)
+    keep(lse, lse_o)
     if comm:
         big.s5(3)
-        keep_w = pltpu.make_async_copy(w.at[pl.ds(0, 4)], w_out, csem.at[1])
-        keep_w.start()
+        keep(w.at[pl.ds(0, 4)], w_o.at[pl.ds(0, 4)])
     b_out, gain1, shift1, b_down, gain2, shift2 = [vec[pl.ds(i, 1), :] for i in range(6)]
-    sums = [jnp.zeros((1, 768), F32) for _ in range(5)]
     tiles = [pl.ds(512 * r, 512) for r in range(2)]
     for rows in tiles:
         pre_one = tok[rows, :].astype(F32) + mm_nt(ctx[rows, :], weight(w, 3)) + b_out
@@ -561,86 +566,77 @@
         low = (xhat * gain1 + shift1).astype(BF)
         first[rows, :] = low
         acc[rows, :] = low.astype(F32) + b_down
-        progress(1)
+        progress()
+    keep(pre, pre_o)
+    keep(first, first_o)
     for j in range(4):
         if comm:
             big.s5(4 + 2 * j)
             big.s5(5 + 2 * j)
+            keep(w.at[pl.ds(4 + 2 * j, 2)], w_o.at[pl.ds(4 + 2 * j, 2)])
         for rows in tiles:
             value, slope = gelu_both(mm(first[rows, :], weight(w, 4 + 2 * j)) + bup[j])
             low = value.astype(BF)
             act[j, rows, :] = low
             gp[j, rows, :] = slope.astype(BF)
             acc[rows, :] += mm_nt(low, weight(w, 5 + 2 * j))
-            progress(3 if j < 3 else 12)
+            progress()
+        keep(gp.at[j], gp_o.at[j])
+    sums = [jnp.zeros((1, 768), F32) for _ in range(3)]
     for r, rows in enumerate(tiles):
         xhat, rate = norm_stats(acc[rows, :])
         out[rows, :] = (xhat * gain2 + shift2).astype(BF)
         row = 512 * r + lax.broadcasted_iota(jnp.int32, (512, 160), 0)
         dy = mm((row == pos[...]).astype(BF), cot[...])
-        sums[3] = sums[3] + colsum(dy * xhat)
-        sums[4] = sums[4] + colsum(dy)
+        sums[1] = sums[1] + colsum(dy * xhat)
+        sums[2] = sums[2] + colsum(dy)
         dacc = norm_back(xhat, rate, gain2, dy)
         low = dacc.astype(BF)
         dbr[rows, :] = low
         acc[rows, :] = dacc
-        sums[2] = sums[2] + colsum(low.astype(F32))
-    keep.wait()
-    dh = buf
+        sums[0] = sums[0] + colsum(low.astype(F32))
+    gsm[...] = jnp.zeros_like(gsm)
+    for i in range(3):
+        gsm[2 + i:3 + i, :] = sums[i]
+    keep(out, out_o)
+    keep(dbr, dbr_o)
+    keep(acc, acc_o)
+    tr[...] = dbr[...].T
     sent = []
-
-    def emit(n, left, right):
-        if n >= 2:
-            sent[n - 2].wait()
-        stage[n % 2] = mm(left[...], right).astype(BF).reshape(2, 2, 2, 96, 768)
-        sent.append(pltpu.make_async_copy(stage.at[n % 2], gff.at[n], sems.at[n % 2]))
-        sent[n].start()
-
-    tr[...] = dbr[...].T
     for j in range(4):
-        emit(j, tr, act[j])
-    tr[...] = first[...].T
-    for j in range(4):
-        for rows in tiles:
-            low = (mm(dbr[rows, :], weight(w, 5 + 2 * j)) * gp[j, rows, :].astype(F32)).astype(BF)
-            dh[j, rows, :] = low
-            gbup[j] += colsum(low.astype(F32))
-            acc[rows, :] += mm_nt(low, weight(w, 4 + 2 * j))
-        emit(4 + j, tr, dh[j])
-    for rows in tiles:
-        xhat, rate = norm_stats(pre[rows, :])
-        dacc = acc[rows, :]
-        sums[0] = sums[0] + colsum(dacc * xhat)
-        sums[1] = sums[1] + colsum(dacc)
-        dpre[rows, :] = norm_back(xhat, rate, gain1, dacc)
-    for i in range(5):
-        gsm[pl.ds(i, 1), :] = sums[i]
-    sent[6].wait()
-    sent[7].wait()
+        if j >= 2:
+            sent[j - 2].wait()
+        stage[j % 2] = mm(tr[...], act[j]).astype(BF).reshape(2, 2, 2, 96, 768)
+        sent.append(pltpu.make_async_copy(stage.at[j % 2], gwd_o.at[j], sems.at[j % 2]))
+        sent[j].start()
+    sent[2].wait()
+    sent[3].wait()
+    for copy in kept:
+        copy.wait()
     if comm:
-        keep_w.wait()
         big.sent(12)
         tiny.sent()
 
 
 def forward_call(comm, *args):
     outs = [
-        (struct((1024, 768), BF), VM), (struct((1024, 768), F32), VM), (struct((8, 2, 2, 2, 96, 768), BF), ANY),
-        (struct((8, 768), F32), VM), (struct((4, 1, 768), F32), VM), (struct((3, 1024, 768), BF), ANY),
-        (struct((3, 256, 512), BF), VM), (struct((1024, 768), BF), VM), (struct((48, 1, 256), F32), VM),
+        (struct((1024, 768), BF), ANY), (struct((1024, 768), F32), ANY), (struct((1024, 768), BF), ANY),
+        (struct((1024, 768), F32), ANY), (struct((1024, 768), BF), ANY), (struct((4, 1024, 768), BF), ANY),
+        (struct((4, 2, 2, 2, 96, 768), BF), ANY), (struct((3, 1024, 768), BF), ANY), (struct((3, 256, 512), BF), ANY),
+        (struct((1024, 768), BF), ANY), (struct((48, 1, 256), F32), ANY), (struct((8, 768), F32), VM),
     ]
     scratch = [
-        pltpu.VMEM((12, 2, 2, 2, 96, 768), BF), pltpu.VMEM((4, 1024, 768), BF), pltpu.VMEM((4, 1024, 768), BF),
-        pltpu.VMEM((4, 1024, 768), BF), pltpu.VMEM((1024, 768), F32), pltpu.VMEM((1024, 768), BF),
-        pltpu.VMEM((1024, 768), BF), pltpu.VMEM((768, 1024), BF), pltpu.VMEM((4, 1040, 128), F32),
-        pltpu.VMEM((2, 2, 2, 2, 96, 768), BF), DMA((2,)), DMA((2,)),
+        pltpu.VMEM((12, 2, 2, 2, 96, 768), BF), pltpu.VMEM((3, 1024, 768), BF), pltpu.VMEM((4, 1024, 768), BF),
+        pltpu.VMEM((4, 1024, 768), BF), pltpu.VMEM((1024, 768), F32), pltpu.VMEM((1024, 768), F32),
+        pltpu.VMEM((1024, 768), BF), pltpu.VMEM((1024, 768), BF), pltpu.VMEM((768, 1024), BF), pltpu.VMEM((1024, 768), BF),
+        pltpu.VMEM((3, 256, 512), BF), pltpu.VMEM((48, 1, 256), F32), pltpu.VMEM((1024, 768), BF),
+        pltpu.VMEM((4, 1040, 128), F32), pltpu.VMEM((2, 2, 2, 2, 96, 768), BF), DMA((2,)), DMA((20,)),
     ]
     if comm:
-        outs += [(struct((4, 2, 2, 2, 96, 768), BF), ANY), (struct((3, 8, 512), F32), VM)]
+        outs += [(struct((12, 2, 2, 2, 96, 768), BF), ANY), (struct((3, 8, 512), F32), VM), (struct((8, 768), F32), VM)]
         scratch += [
             pltpu.VMEM((12, 4, 16, 1152), BF), pltpu.VMEM((4, 24, 128), F32), pltpu.VMEM((2, 2, 2, 4, 24, 128), F32),
-            pltpu.VMEM((32, 24, 128), F32), pltpu.VMEM((3, 1, 768), F32), pltpu.VMEM((8, 768), F32),
-            pltpu.VMEM((4, 1, 768), F32),
+            pltpu.VMEM((32, 24, 128), F32), pltpu.VMEM((3, 1, 768), F32), pltpu.VMEM((4, 1, 768), F32),
             DMA((12, 3)), DMA((12, 3)), DMA((12, 4)), DMA((12, 4)), DMA((12,)), DMA((12,)), DMA((7,)), DMA((7,)),
         ]
         params = pltpu.CompilerParams(vmem_limit_bytes=LIMIT, collective_id=1, has_side_effects=True)
@@ -654,17 +650,23 @@
         out_shape=[o[0] for o in outs], scratch_shapes=scratch, compiler_params=params, name="forward")(*args)
 
 
-def back_block(g, b, qkv, pkv, dctx, lse, dk, dv, dpk, dpv, dproj):
+def qkv_rows(g, start, size):
+    return pl.ds(pl.multiple_of(3072 + 1024 * g + start, 32), size)
+
+
+def back_block(g, b, wb, pkv, buf, lse, dk, dv, dpk, dpv):
     ns, ps, near, far = window(b)
-    rows = pl.ds(pl.multiple_of(b * 128, 128), 128)
+    first_row = pl.multiple_of(b * 128, 128)
+    rows = pl.ds(first_row, 128)
     nr, prow = pl.ds(ns, 256), pl.ds(ps, 160)
+    qrows, krows = qkv_rows(g, first_row, 128), qkv_rows(g, ns, 256)
     for pr in range(2):
         ln = pl.ds(128 * pr, 128)
-        qm = head_split(qkv[g, rows, 128 * pr:128 * pr + 128], 0.125)
-        dm = head_split(dctx[rows, lane_block(256 * g + 128 * pr)], 1.0)
-        kn = qkv[g, nr, 256 + 128 * pr:384 + 128 * pr]
+        qm = head_split(wb[qrows, 128 * pr:128 * pr + 128], 0.125)
+        dm = head_split(buf[3, rows, lane_block(256 * g + 128 * pr)], 1.0)
+        kn = wb[krows, 256 + 128 * pr:384 + 128 * pr]
         kp = pkv[g, prow, 128 * pr:128 * pr + 128]
-        vn = qkv[g, nr, 512 + 128 * pr:640 + 128 * pr]
+        vn = wb[krows, 512 + 128 * pr:640 + 128 * pr]
         vp = pkv[g, prow, 256 + 128 * pr:384 + 128 * pr]
         ls = lse[(g * 2 + pr) * 8 + b]
         pn = jnp.exp(jnp.where(near, mm_nt(kn, qm), -1e30) - ls)
@@ -679,12 +681,12 @@
         dv[nr, ln] += mm(pn.astype(BF), dm)
         dpv[prow, ln] += mm(pp.astype(BF), dm)
         r = mm_tn(kn, sn) + mm_tn(kp, sp)
-        dproj[g, rows, ln] = (head_join(r).T * 0.125).astype(BF)
-
-
-def pool_back(g, conv, qkv, kvf, dk, dv, dpk, dpv, dproj, gconv):
+        buf[g, rows, ln] = (head_join(r).T * 0.125).astype(BF)
+
+
+def pool_back(g, conv, wb, kvf, dk, dv, dpk, dpv, buf, gconv):
     for part in range(4):
-        kvf[part, 8:1032, :] = qkv[g, :, 256 + 128 * part:384 + 128 * part].astype(F32)
+        kvf[part, 8:1032, :] = wb[qkv_rows(g, 0, 1024), 256 + 128 * part:384 + 128 * part].astype(F32)
     for part in range(4):
         cols = pl.ds(128 * part, 128)
         src, dst = (dpk, dk) if part < 2 else (dpv, dv)
@@ -696,60 +698,163 @@
         for t in range(5):
             at = pl.ds(6 + t, 256, stride=4)
             kvf[part, at, :] += conv[g, pl.ds(t, 1), cols] * dpool
-        dproj[g, :, 256 + 128 * part:384 + 128 * part] = kvf[part, 8:1032, :].astype(BF)
+        buf[g, :, 256 + 128 * part:384 + 128 * part] = kvf[part, 8:1032, :].astype(BF)
         kvf[part, 0:8, :] = jnp.zeros((8, 128), F32)
         kvf[part, 1032:1040, :] = jnp.zeros((8, 128), F32)
 
 
+BLOCKS = (2, 2, 2, 96, 768)
+
+
+STEPS = (
+    ((1, 0),), (), ((1, 1),), ((2, 0),), ((1, 2),), ((2, 1),), ((3, 0), (1, 3)), ((2, 2),), ((3, 1), (1, 4)),
+    ((2, 3),), ((4, 0), (3, 2), (1, 5)), ((2, 4),), ((3, 3), (4, 1), (1, 6), (2, 5)), ((4, 2), (3, 4)), ((4, 3),),
+)
+LOOP_STEPS = {
+    0: ((1, 7),), 1: ((2, 6),), 2: ((3, 5),), 3: ((1, 8),), 4: ((2, 7), (4, 4)), 5: ((3, 6),), 7: ((2, 8),),
+    8: ((3, 7), (4, 5)), 9: ((1, 9),), 11: ((3, 8), (4, 6)), 13: ((2, 9), (4, 7)), 16: ((4, 8), (3, 9)), 17: ((1, 10),),
+    20: ((2, 10),), 21: ((4, 9),), 23: ((3, 10),),
+}
+
+
 def backward_kernel(comm, *refs):
-    tok, w, conv, dpre, qkv, pkv, ctx, lse = refs[:8]
+    (tok_i, w_i, conv, vec, pre_i, first_i, acc_i, dbr_i, gp_i, qkv_i, pkv_i, ctx_i, lse_i, gsm_in) = refs[:14]
     if comm:
-        (gff, gsm, gbup, gtok, gqkv, gqb, gcv, gwo, gbo, gg1, gs1, gwu, gbu, gwd, gbd, gg2, gs2,
-         kvf, dk, dv, dpk, dpv, dctx, dproj, tr,
-         gat, gconv, gbias, gbout, r0, r1a, r1b, r2, v, r3, fin, own, pieces, small, t0, t1, t2,
-         ks, kr, xs, xr, zs, zr, ls, ss, sr) = refs[8:]
+        (gwd_i, gtok_o, fin, tot,
+         wb, buf, xb, db, tr, acc, gtok, pkv, lse, kvf, dk, dv, dpk, dpv, isem, osem,
+         gat, gconv, gbias, gbout, gsm, gbup, r0, r1a, r1b, r2, v, r3, own, pieces, small, t0, t1, t2,
+         ks, kr, xs, xr, zs, zr, ls, ss, sr) = refs[14:]
     else:
-        (gtok, gat, gconv, gbias, gbout, kvf, dk, dv, dpk, dpv, dctx, dproj, tr) = refs[8:]
-    clear_edges(kvf)
+        (gtok_o, gat, gconv, gbias, gbout, gsm, gbup,
+         wb, buf, xb, db, tr, acc, gtok, pkv, lse, kvf, dk, dv, dpk, dpv, isem, osem) = refs[14:]
+    loads = {}
+
+    def load(name, src, dst):
+        loads[name] = pltpu.make_async_copy(src, dst, isem.at[len(loads)])
+        loads[name].start()
+
+    def slot(n):
+        return wb[pl.ds(768 * n, 768), :]
+
+    def load_weight(c, n):
+        for i in range(8):
+            load(("w", c, i), w_i.at[c, i // 4, i // 2 % 2, i % 2], wb.at[pl.ds(768 * n + 96 * i, 96), :])
+
+    def have_weight(c):
+        for i in range(8):
+            loads["w", c, i].wait()
+
+    load("dbr", dbr_i, db)
+    load_weight(5, 1)
+    load(("gp", 0), gp_i.at[0], buf.at[0])
+    load_weight(4, 0)
+    load("acc", acc_i, acc)
+    load("first", first_i, xb)
     if comm:
         p = Place()
         big = Scatter(p, r0, r1a, r1b, r2, v, r3, fin, (ks, kr, xs, xr, zs, zr))
         tiny = SmallScatter(p, small, t0, t1, t2, ss, sr)
         p.greet()
 
-        def fetch_ff(c):
-            return pltpu.make_async_copy(gff.at[c, :, :, p.k], own.at[lax.rem(c, 2)], ls.at[lax.rem(c, 2)])
-
         def fetch(c):
-            @pl.when(c < 8)
-            def _():
-                fetch_ff(c).start()
-
-            @pl.when(c == 8)
-            def _():
-                pltpu.make_async_copy(gat.at[3, :, :, p.k], own.at[lax.rem(c, 2)], ls.at[lax.rem(c, 2)]).start()
-
-            @pl.when(c > 8)
-            def _():
-                pltpu.make_async_copy(gat.at[lax.max(c - 9, 0), :, :, p.k], own.at[lax.rem(c, 2)], ls.at[lax.rem(c, 2)]).start()
-
-        def start_ff(c, carry):
-            big.across(c, gff.at[c]).start()
-            return carry
-
-        lax.fori_loop(0, 8, start_ff, 0)
-        fetch_ff(0).start()
-        fetch_ff(1).start()
-    da = dpre[...].astype(BF)
-    gbout[...] = colsum(da.astype(F32))
-    tr[...] = da.T
-    for r in range(2):
-        rows = pl.ds(512 * r, 512)
-        dctx[rows, :] = mm(dpre[rows, :].astype(BF), weight(w, 3)).astype(BF)
-    gat[3] = mm(tr[...], ctx[...]).astype(BF).reshape(2, 2, 2, 96, 768)
+            return pltpu.make_async_copy(gwd_i.at[c, :, :, p.k], own.at[c % 2], ls.at[c % 2])
+
+        for c in range(4):
+            big.across(c, gwd_i.at[c]).start()
+        fetch(0).start()
+        fetch(1).start()
+
+        def take(steps):
+            for stage, c in steps:
+                if stage > 1:
+                    (big.s2, big.s3, big.s4)[stage - 2](c)
+                elif c >= 4:
+                    at = c - 4 if c < 9 else c - 9
+                    big.s1(c, gat.at[0], lambda a, b: gat[at, a, b, p.k])
+                else:
+                    fetch(c).wait()
+                    big.s1(c, gat.at[0], lambda a, b: own[c % 2, a, b])
+                    if c < 2:
+                        fetch(c + 2).start()
+
+    def run(n):
+        if comm:
+            take(STEPS[n])
+
+    for j in range(1, 4):
+        load_weight(5 + 2 * j, 1 + 2 * j)
+        load(("gp", j), gp_i.at[j], buf.at[j])
+        load_weight(4 + 2 * j, 2 * j)
+    load("pre", pre_i, gtok)
+    load("pkv", pkv_i, pkv)
+    load("lse", lse_i, lse)
+    clear_edges(kvf)
+    gbup[...] = jnp.zeros_like(gbup)
+    gsm[...] = gsm_in[...]
+    tiles = [pl.ds(512 * r, 512) for r in range(2)]
+    loads["first"].wait()
+    tr[...] = xb[...].T
+    load("tok", tok_i, xb)
+    loads["dbr"].wait()
+    for j in range(4):
+        have_weight(5 + 2 * j)
+        loads["gp", j].wait()
+        for r, rows in enumerate(tiles):
+            low = (mm(db[rows, :], slot(1 + 2 * j)) * buf[j, rows, :].astype(F32)).astype(BF)
+            buf[j, rows, :] = low
+            gbup[j] += colsum(low.astype(F32))
+            if r == 0:
+                have_weight(4 + 2 * j)
+                if j == 0:
+                    loads["acc"].wait()
+            acc[rows, :] += mm_nt(low, slot(2 * j))
+            run(3 * j + r)
+        gat[j] = mm(tr[...], buf[j]).astype(BF).reshape(BLOCKS)
+        if comm:
+            big.across(4 + j, gat.at[j]).start()
+            run(3 * j + 2)
+        if j == 1:
+            for c in range(4):
+                load_weight(c, c)
+    for g in range(3):
+        load(("qkv", g), qkv_i.at[g], wb.at[pl.ds(3072 + 1024 * g, 1024), :])
+    load("ctx", ctx_i, db)
+    loads["pre"].wait()
+    gain1 = vec[1:2, :]
+    sums = [jnp.zeros((1, 768), F32) for _ in range(3)]
+    have_weight(3)
+    for rows in tiles:
+        xhat, rate = norm_stats(gtok[rows, :])
+        dacc = acc[rows, :]
+        sums[0] = sums[0] + colsum(dacc * xhat)
+        sums[1] = sums[1] + colsum(dacc)
+        dpre = norm_back(xhat, rate, gain1, dacc)
+        gtok[rows, :] = dpre
+        da = dpre.astype(BF)
+        sums[2] = sums[2] + colsum(da.astype(F32))
+        buf[3, rows, :] = mm(da, slot(3)).astype(BF)
+        tr[:, rows] = da.T
+    gsm[0:1, :] = sums[0]
+    gsm[1:2, :] = sums[1]
+    gbout[...] = sums[2]
     if comm:
-        big.across(8, gat.at[3]).start()
-    tr[...] = tok[...].T
+        run(12)
+        pieces[...] = jnp.zeros_like(pieces)
+        pack_small(pieces, 6, [gbout[...]] + [gsm[i:i + 1, :] for i in range(5)], 24, 768)
+        pack_small(pieces, 12, [jnp.concatenate([gbup[j] for j in range(4)], axis=1)], 96, 3072)
+    loads["ctx"].wait()
+    gat[4] = mm(tr[...], db[...]).astype(BF).reshape(BLOCKS)
+    if comm:
+        big.across(8, gat.at[4]).start()
+        run(13)
+    loads["tok"].wait()
+    tr[...] = xb[...].T
+    loads["pkv"].wait()
+    loads["lse"].wait()
+    for g in range(3):
+        loads["qkv", g].wait()
+        have_weight(g)
+    run(14)
 
     def group(g, carry):
         dk[...] = jnp.zeros_like(dk)
@@ -759,137 +864,146 @@
 
         def block(b, inner):
             if comm:
-                i = 8 * g + b
-                n = lax.div(i, 2)
-
-                @pl.when((lax.rem(i, 2) == 0) & (n < 11))
-                def _():
-                    pltpu.make_async_copy(gff.at[0, :, :, p.k], own.at[lax.rem(n, 2)], ls.at[lax.rem(n, 2)]).wait()
-                    big.s1(n, gff.at[0], lambda a, b2: own[lax.rem(n, 2), a, b2])
-                    pl.when(n < 9)(lambda: fetch(n + 2))
-
-                @pl.when((lax.rem(i, 2) == 1) & (i >= 3))
-                def _():
-                    big.s2(n - 1)
-
-                @pl.when((lax.rem(i, 2) == 1) & (i >= 5))
-                def _():
-                    big.s3(n - 2)
-
-                @pl.when((lax.rem(i, 2) == 0) & (i >= 8))
-                def _():
-                    big.s4(n - 4)
-            back_block(g, b, qkv, pkv, dctx, lse, dk, dv, dpk, dpv, dproj)
+                for i, steps in LOOP_STEPS.items():
+                    pl.when(8 * g + b == i)(functools.partial(take, steps))
+            back_block(g, b, wb, pkv, buf, lse, dk, dv, dpk, dpv)
             return inner
 
         lax.fori_loop(0, 8, block, 0)
-        pool_back(g, conv, qkv, kvf, dk, dv, dpk, dpv, dproj, gconv)
-        gat[g] = mm(tr[...], dproj[g]).astype(BF).reshape(2, 2, 2, 96, 768)
-        gbias[g] = colsum(dproj[g].astype(F32))
+        pool_back(g, conv, wb, kvf, dk, dv, dpk, dpv, buf, gconv)
+        if comm:
+            big.across(4 + g, gat.at[0]).wait_send()
+        gat[g if comm else 5 + g] = mm(tr[...], buf[g]).astype(BF).reshape(BLOCKS)
         if comm:
             big.across(9 + g, gat.at[g]).start()
+        gbias[g] = colsum(buf[g].astype(F32))
         return carry
 
     lax.fori_loop(0, 3, group, 0)
+    parts = []
 
     def token_part(n):
         rows = pl.ds(256 * n, 256)
-        acc = dpre[rows, :]
+        total = gtok[rows, :]
         for g in range(3):
-            acc = acc + mm_nt(dproj[g, rows, :], weight(w, g))
-        gtok[rows, :] = acc
+            total = total + mm_nt(buf[g, rows, :], slot(g))
+        gtok[rows, :] = total
+        parts.append(pltpu.make_async_copy(gtok.at[rows, :], gtok_o.at[rows, :], osem.at[n]))
+        parts[n].start()
 
     if not comm:
         for n in range(4):
             token_part(n)
+        for copy in parts:
+            copy.wait()
         return
 
-    pieces[...] = jnp.zeros_like(pieces)
+    take(((1, 11),))
     kinds = [jnp.concatenate([gbias[g][:, 256 * i:256 * i + 256] for i in range(3) for g in range(3)], axis=1)]
     pack_small(pieces, 0, kinds, 72, 2304)
     pack_small(pieces, 1, [
         jnp.concatenate([gconv[g, t:t + 1, 256 * i:256 * i + 256] for i in range(2) for g in range(3)], axis=1)
         for t in range(5)], 48, 1536)
-    pack_small(pieces, 6, [gbout[...]] + [gsm[i:i + 1, :] for i in range(5)], 24, 768)
-    pack_small(pieces, 12, [jnp.concatenate([gbup[j] for j in range(4)], axis=1)], 96, 3072)
     small[...] = pieces[...].reshape(2, 2, 2, 96, 128)
     tiny.s0()
-    big.s1(11, gff.at[0], lambda a, b: gat[2, a, b, p.k])
-    big.s3(10)
     token_part(0)
-    big.s2(11)
     tiny.s1()
-    big.s4(8)
+    take(((2, 11),))
     token_part(1)
-    big.s3(11)
     tiny.s2()
-    big.s4(9)
+    take(((3, 11),))
     token_part(2)
-    big.s4(10)
+    take(((4, 10),))
     token_part(3)
-    for j in range(4):
-        gwd[768 * j:768 * j + 768, :] = fin[j].T
-        gwu[:, 768 * j:768 * j + 768] = fin[4 + j]
-    gwo[...] = fin[8].T
-    total = tiny.s3()
-    gqb[...] = total[0:1, 0:72]
-    gcv[...] = total[1:6, 0:48]
-    for i, ref in enumerate((gbo, gg1, gs1, gbd, gg2, gs2)):
-        ref[...] = total[6 + i:7 + i, 0:24]
-    gbu[...] = total[12:13, 0:96]
-    big.s4(11)
-    for g in range(3):
-        for i in range(3):
-            gqkv[:, 768 * i + 256 * g:768 * i + 256 * g + 256] = fin[9 + g, :, 256 * i:256 * i + 256]
-
-    def drain(c, carry):
-        big.sent(c, gff.at[0])
-        return carry
-
-    lax.fori_loop(0, 12, drain, 0)
+    tot[...] = tiny.s3()
+    take(((4, 11),))
+    for c in range(12):
+        for copy in big.first(c) + big.second(c) + tuple(big.along_z(c, dz) for dz in (1, 2, 3)):
+            copy.wait_send()
+        if c not in (4, 5, 6):
+            big.across(c, gat.at[0]).wait_send()
     tiny.sent()
+    for copy in parts:
+        copy.wait()
 
 
 def backward_call(comm, *args):
     scratch = [
+        pltpu.VMEM((6144, 768), BF), pltpu.VMEM((4, 1024, 768), BF), pltpu.VMEM((1024, 768), BF), pltpu.VMEM((1024, 768), BF),
+        pltpu.VMEM((768, 1024), BF), pltpu.VMEM((1024, 768), F32), pltpu.VMEM((1024, 768), F32),
+        pltpu.VMEM((3, 256, 512), BF), pltpu.VMEM((48, 1, 256), F32),
         pltpu.VMEM((4, 1040, 128), F32), pltpu.VMEM((1024, 256), F32), pltpu.VMEM((1024, 256), F32),
-        pltpu.VMEM((256, 256), F32), pltpu.VMEM((256, 256), F32), pltpu.VMEM((1024, 768), BF),
-        pltpu.VMEM((3, 1024, 768), BF), pltpu.VMEM((768, 1024), BF),
+        pltpu.VMEM((256, 256), F32), pltpu.VMEM((256, 256), F32), DMA((120,)), DMA((4,)),
     ]
-    ins = [VM] * len(args)
-    local = [((4, 2, 2, 2, 96, 768), BF), ((3, 8, 512), F32), ((3, 1, 768), F32), ((1, 768), F32)]
-    outs = [struct((1024, 768), F32)]
+    ins = [ANY] * len(args)
+    for i in (2, 3, 13):
+        ins[i] = VM
+    local = [((5 if comm else 8,) + BLOCKS, BF), ((3, 8, 512), F32), ((3, 1, 768), F32), ((1, 768), F32), ((8, 768), F32), ((4, 1, 768), F32)]
+    outs = [(struct((1024, 768), F32), ANY)]
     if comm:
-        ins[8] = ANY
-        outs += [struct(s, F32) for s in ((24, 2304), (1, 72), (5, 48), (768, 24), (1, 24), (1, 24), (1, 24), (24, 3072), (1, 96),
-                                          (3072, 24), (1, 24), (1, 24), (1, 24))]
+        outs += [(struct((12, 24, 768), F32), VM), (struct((24, 128), F32), VM)]
         scratch += [pltpu.VMEM(*s) for s in local]
         scratch += [
             pltpu.VMEM((12, 2, 2, 96, 768), BF), pltpu.VMEM((12, 2, 96, 384), BF), pltpu.VMEM((12, 2, 96, 384), BF),
             pltpu.VMEM((12, 2, 96, 384), BF), pltpu.VMEM((12, 4, 16, 1152), BF), pltpu.VMEM((12, 3, 16, 1152), BF),
-            pltpu.VMEM((12, 24, 768), F32), pltpu.VMEM((2, 2, 2, 96, 768), BF), pltpu.VMEM((32, 24, 128), F32),
+            pltpu.VMEM((2, 2, 2, 96, 768), BF), pltpu.VMEM((32, 24, 128), F32),
             pltpu.VMEM((2, 2, 2, 96, 128), F32), pltpu.VMEM((2, 2, 96, 128), F32), pltpu.VMEM((3, 96, 128), F32),
             pltpu.VMEM((3, 24, 128), F32),
             DMA((12,)), DMA((12,)), DMA((12, 4)), DMA((12, 4)), DMA((12, 3)), DMA((12, 3)), DMA((2,)), DMA((7,)), DMA((7,)),
         ]
         params = pltpu.CompilerParams(vmem_limit_bytes=LIMIT, collective_id=2, has_side_effects=True)
     else:
-        outs += [struct(*s) for s in local]
+        outs += [(struct(*s), VM) for s in local]
         params = pltpu.CompilerParams(vmem_limit_bytes=LIMIT)
     return pl.pallas_call(
-        functools.partial(backward_kernel, comm), in_specs=ins, out_specs=[VM] * len(outs), out_shape=outs,
+        functools.partial(backward_kernel, comm), in_specs=ins, out_specs=[o[1] for o in outs], out_shape=[o[0] for o in outs],
         scratch_shapes=scratch, compiler_params=params, name="backward")(*args)
+
+
+def finish_kernel(out_i, gtok_i, fin, tot, out, gtok, gqkv, gqb, gcv, gwo, gbo, gg1, gs1, gwu, gbu, gwd, gbd, gg2, gs2):
+    out[...] = out_i[...]
+    gtok[...] = gtok_i[...]
+
+    @pl.when(pl.program_id(0) == 0)
+    def _():
+        for j in range(4):
+            gwd[:, 768 * j:768 * j + 768] = fin[j]
+            gwu[:, 768 * j:768 * j + 768] = fin[4 + j]
+        gwo[...] = fin[8]
+        for g in range(3):
+            for i in range(3):
+                gqkv[:, 768 * i + 256 * g:768 * i + 256 * g + 256] = fin[9 + g, :, 256 * i:256 * i + 256]
+        gqb[...] = tot[0:1, 0:72]
+        gcv[...] = tot[1:6, 0:48]
+        for i, ref in enumerate((gbo, gg1, gs1, gbd, gg2, gs2)):
+            ref[...] = tot[6 + i:7 + i, 0:24]
+        gbu[...] = tot[12:13, 0:96]
+
+
+def finish_call(*args):
+    shapes = ((24, 2304), (1, 72), (5, 48), (24, 768), (1, 24), (1, 24), (1, 24), (24, 3072), (1, 96),
+              (24, 3072), (1, 24), (1, 24), (1, 24))
+    part = pl.BlockSpec((256, 768), lambda n: (n, 0))
+
+    def full(shape):
+        return pl.BlockSpec(shape, lambda n: (0,) * len(shape))
+
+    return pl.pallas_call(
+        finish_kernel, grid=(4,), in_specs=[part, part, full((12, 24, 768)), full((24, 128))],
+        out_specs=[part, part] + [full(s) for s in shapes],
+        out_shape=[struct((1024, 768), BF), struct((1024, 768), F32)] + [struct(s, F32) for s in shapes],
+        name="finish")(*args)
 
 
 def shards_direct(tokens, w_qkv, b_qkv, conv_kv, w_out, b_out, gain_one, shift_one, w_up, b_up, w_down, b_down, gain_two,
                   shift_two, positions, cotangent):
     tok = tokens[0]
-    out, dpre, gff, gsm, gbup, qkv, pkv, ctx, lse, w, conv = forward_call(
-        True, tok, w_qkv, b_qkv[None], conv_kv, w_out, b_out[None], gain_one[None], shift_one[None], b_down[None],
-        gain_two[None], shift_two[None], w_up, b_up[None], w_down, positions, cotangent[0])
-    (gtok, gqkv, gqb, gcv, gwo, gbo, gg1, gs1, gwu, gbu, gwd, gbd, gg2, gs2) = backward_call(
-        True, tok, w, conv, dpre, qkv, pkv, ctx, lse, gff, gsm, gbup)
-    return (out[None], gtok[None], gqkv, gqb[0], gcv, gwo, gbo[0], gg1[0], gs1[0], gwu, gbu[0], gwd, gbd[0], gg2[0], gs2[0])
+    out, pre, first, acc, dbr, gp, gwd, qkv, pkv, ctx, lse, gsm, w, conv, vec = forward_call(
+        True, tok, w_qkv, b_qkv[None], conv_kv, w_out.T, b_out[None], gain_one[None], shift_one[None], b_down[None],
+        gain_two[None], shift_two[None], w_up, b_up[None], w_down.T, positions, cotangent[0])
+    gtok, fin, tot = backward_call(True, tok, w, conv, vec, pre, first, acc, dbr, gp, qkv, pkv, ctx, lse, gsm, gwd)
+    (out, gtok, gqkv, gqb, gcv, gwo, gbo, gg1, gs1, gwu, gbu, gwd, gbd, gg2, gs2) = finish_call(out, gtok, fin, tot)
+    return (out[None], gtok[None], gqkv, gqb[0], gcv, gwo.T, gbo[0], gg1[0], gs1[0], gwu, gbu[0], gwd.T, gbd[0], gg2[0], gs2[0])
 
 
 def small_sizes(count):
@@ -923,11 +1037,12 @@
     conv = jnp.concatenate([by_group(p, 2) for p in parts[1:6]] + [jnp.zeros((3, 3, 512), F32)], 1)
     vec = jnp.stack(parts[6:12] + [jnp.zeros((768,), F32)] * 2)
     bup = parts[12].reshape(4, 1, 768)
-    out, dpre, gff, gsm, gbup, qkv, pkv, ctx, lse = forward_call(
+    out, pre, first, acc, dbr, gp, gwd, qkv, pkv, ctx, lse, gsm = forward_call(
         False, tokens[0], w, bqkv, conv, vec, bup, positions, cotangent[0])
-    gff = lax.psum_scatter(gff.reshape(8, 768, 768), AXES, scatter_dimension=1, tiled=True).astype(F32)
-    gtok, gat, gconv, gbias, gbout = backward_call(False, tokens[0], w[:4], conv, dpre, qkv, pkv, ctx, lse)
-    gat = lax.psum_scatter(gat.reshape(4, 768, 768), AXES, scatter_dimension=1, tiled=True).astype(F32)
+    gwd = lax.psum_scatter(gwd.reshape(4, 768, 768), AXES, scatter_dimension=1, tiled=True).astype(F32)
+    gtok, gat, gconv, gbias, gbout, gsm, gbup = backward_call(
+        False, tokens[0], w, conv, vec, pre, first, acc, dbr, gp, qkv, pkv, ctx, lse, gsm)
+    gat = lax.psum_scatter(gat.reshape(8, 768, 768), AXES, scatter_dimension=1, tiled=True).astype(F32)
     flat = [gbias.reshape(3, 3, 256).transpose(1, 0, 2).reshape(count, -1)]
     flat += [gconv[:, t].reshape(3, 2, 256).transpose(1, 0, 2).reshape(count, -1) for t in range(5)]
     flat += [gbout[0].reshape(count, -1)] + [gsm[i].reshape(count, -1) for i in range(5)] + [gbup.reshape(count, -1)]
@@ -938,10 +1053,10 @@
         at += size
     return (
         out[None], gtok[None],
-        gat[:3].reshape(3, rows, 3, 256).transpose(1, 2, 0, 3).reshape(rows, 2304),
-        s[0], jnp.stack(s[1:6]), gat[3].T, s[6], s[7], s[8],
-        gff[4:].transpose(1, 0, 2).reshape(rows, 3072), s[12],
-        gff[:4].transpose(0, 2, 1).reshape(3072, rows), s[9], s[10], s[11],
+        gat[5:].reshape(3, rows, 3, 256).transpose(1, 2, 0, 3).reshape(rows, 2304),
+        s[0], jnp.stack(s[1:6]), gat[4].T, s[6], s[7], s[8],
+        gat[:4].transpose(1, 0, 2).reshape(rows, 3072), s[12],
+        gwd.transpose(0, 2, 1).reshape(3072, rows), s[9], s[10], s[11],
     )
 
 

time: 249 us -> 217 us (0.87)
  local copies, waits for them, and re-layouts: 18.6 us -> 0 us
  Pallas kernels: 226 us -> 212 us
    pallas_call x1, Pallas kernels: 129 us -> 98.9 us  [forward_call(): pl.pallas_call(functools.partial(forward_kernel, comm), in_specs=ins, out...]
    unnamed x41 -> x0, local copies, waits for them, and re-layouts: 18.6 us -> none
    pallas_call x1, Pallas kernels: 96.7 us -> 108 us  [backward_call(): pl.pallas_call(functools.partial(backward_kernel, comm), in_specs=ins, ou...]
    pallas_call x0 -> x1, Pallas kernels: none -> 5.71 us  [finish_call(): pl.pallas_call(finish_kernel, grid=(4,), in_specs=[part, part, full((12,...]
where the time goes in v3:
time: 217 us; the launch traced here: 213 us
  Pallas kernels  212 us (98%)
    pallas_call x1, Pallas kernels, backward_call(): pl.pallas_call(functools.partial(backward_kernel, comm), in_specs=ins, ou...  108 us
    pallas_call x1, Pallas kernels, forward_call(): pl.pallas_call(functools.partial(forward_kernel, comm), in_specs=ins, out...  98.9 us
    pallas_call x1, Pallas kernels, finish_call(): pl.pallas_call(finish_kernel, grid=(4,), in_specs=[part, part, full((12,...  5.71 us

profile of v3, /device:TPU:0, one launch (start us, length us, event | category | flops | bytes accessed | tf_op | source)
XLA Modules:
  0.0 213.5 jit_solution(5406566048904223391)
XLA Ops:
  0.7 98.9 %forward.1 = (bf16[1024,768]{1,0:T(8,128)(2,1)}, f32[1024,768]{1,0:T(8,128)}, bf16[1024,768]{1,0:T(8,128)(2,1)}, f32[1024,768]{1,0:T(8,128)}, bf16[1024,768]{1,0...) custom-call(bf16[1024,768]{1,0:T(8,128)(2,1)} %bitcast.24, ...), custom_call_target="tpu_custom_call" | custom-call | tf_op jit(solution)/shard_map/forward/pallas_call | solution.py:648
  99.5 107.7 %backward.1 = (f32[1024,768]{1,0:T(8,128)}, f32[12,24,768]{2,1,0:T(8,128)}, f32[24,128]{1,0:T(8,128)}) custom-call(bf16[1024,768]{1,0:T(8,128)(2,1)} %bitcast.25, bf16[12,2,2,2,96,768]{5,4,3,2,1,0:T(8,128)(2,1)} %get-tuple-element.49.refs_1_, f32[3,8,512]{2,1,0:T(8,128)} %get-tuple-element.50.refs_2_, f32[8,768]{1,0:T(8,128)} %get-tuple-element.51.refs_3_, ...), custom_call_target="tpu_custom_call" | custom-call | tf_op jit(solution)/shard_map/backward/pallas_call | solution.py:958
  207.3 5.7 %finish.1 = (bf16[1024,768]{1,0:T(8,128)(2,1)}, f32[1024,768]{1,0:T(8,128)}, f32[24,2304]{1,0:T(8,128)}, f32[1,72]{1,0:T(1,128)}, f32[5,48]{1,0:T(8,128)}, /*ind...) custom-call(bf16[1024,768]{1,0:T(8,128)(2,1)} %get-tuple-element.48., ...), custom_call_target="tpu_custom_call" | custom-call | tf_op jit(solution)/shard_map/finish/pallas_call | solution.py:991

commit v4 on v3

--- a/solution.py
+++ b/solution.py
@@ -418,25 +418,35 @@
         pkv[g, :, cols] = total.astype(BF)
 
 
-def attend_block(g, b, qkv, pkv, ctx, lse):
-    ns, ps, near, far = window(b)
-    rows = pl.ds(pl.multiple_of(b * 128, 128), 128)
-    for pr in range(2):
-        qm = head_split(qkv[g, rows, 128 * pr:128 * pr + 128], 0.125)
-        kn = qkv[g, pl.ds(ns, 256), 256 + 128 * pr:384 + 128 * pr]
-        kp = pkv[g, pl.ds(ps, 160), 128 * pr:128 * pr + 128]
-        sn = jnp.where(near, mm_nt(kn, qm), -1e30)
-        sp = jnp.where(far, mm_nt(kp, qm), -1e30)
-        peak = jnp.maximum(jnp.max(sn, axis=0, keepdims=True), jnp.max(sp, axis=0, keepdims=True))
-        en = jnp.exp(sn - peak)
-        ep = jnp.exp(sp - peak)
-        total = jnp.sum(en, axis=0, keepdims=True) + jnp.sum(ep, axis=0, keepdims=True)
-        vn = qkv[g, pl.ds(ns, 256), 512 + 128 * pr:640 + 128 * pr]
-        vp = pkv[g, pl.ds(ps, 160), 256 + 128 * pr:384 + 128 * pr]
-        out = mm_tn(vn, en.astype(BF)) + mm_tn(vp, ep.astype(BF))
-        out = out * pl.reciprocal(total)
-        ctx[rows, lane_block(256 * g + 128 * pr)] = head_join(out).T.astype(BF)
-        lse[(g * 2 + pr) * 8 + b] = peak + jnp.log(total)
+def attend_blocks(g, blocks, qkv, pkv, ctx, lse):
+    parts = []
+    for b in blocks:
+        ns, ps, near, far = window(b)
+        rows = pl.ds(pl.multiple_of(b * 128, 128), 128)
+        for pr in range(2):
+            parts.append(dict(
+                near=near, far=far, rows=rows, lanes=lane_block(256 * g + 128 * pr), at=(g * 2 + pr) * 8 + b,
+                qm=head_split(qkv[g, rows, 128 * pr:128 * pr + 128], 0.125),
+                kn=qkv[g, pl.ds(ns, 256), 256 + 128 * pr:384 + 128 * pr],
+                kp=pkv[g, pl.ds(ps, 160), 128 * pr:128 * pr + 128],
+                vn=qkv[g, pl.ds(ns, 256), 512 + 128 * pr:640 + 128 * pr],
+                vp=pkv[g, pl.ds(ps, 160), 256 + 128 * pr:384 + 128 * pr]))
+    for t in parts:
+        t["sn"] = jnp.where(t["near"], mm_nt(t["kn"], t["qm"]), -1e30)
+        t["sp"] = jnp.where(t["far"], mm_nt(t["kp"], t["qm"]), -1e30)
+    for t in parts:
+        t["peak"] = jnp.maximum(jnp.max(t["sn"], axis=0, keepdims=True), jnp.max(t["sp"], axis=0, keepdims=True))
+    for t in parts:
+        t["en"] = jnp.exp(t["sn"] - t["peak"])
+        t["ep"] = jnp.exp(t["sp"] - t["peak"])
+    for t in parts:
+        t["total"] = jnp.sum(t["en"], axis=0, keepdims=True) + jnp.sum(t["ep"], axis=0, keepdims=True)
+    for t in parts:
+        out = mm_tn(t["vn"], t["en"].astype(BF)) + mm_tn(t["vp"], t["ep"].astype(BF))
+        t["out"] = head_join(out * pl.reciprocal(t["total"])).T.astype(BF)
+    for t in parts:
+        ctx[t["rows"], t["lanes"]] = t["out"]
+        lse[t["at"]] = t["peak"] + jnp.log(t["total"])
 
 
 def clear_edges(kvf):
@@ -532,22 +542,22 @@
         project_group(g, tok, w, bqkv, conv, qkv, pkv, kvf)
 
         def block(b, inner):
-            attend_block(g, b, qkv, pkv, ctx, lse)
             if comm:
-                i = 8 * g + b
-
-                @pl.when(lax.rem(i, 4) == 0)
+                i = 4 * g + b
+                n = lax.div(i, 2)
+
+                @pl.when(lax.rem(i, 2) == 0)
                 def _():
-                    n = lax.div(i, 4)
                     big.s2(4 + n)
                     big.s3(2 + n)
 
-                @pl.when(lax.rem(i, 4) == 2)
+                @pl.when(lax.rem(i, 2) == 1)
                 def _():
-                    big.s4(1 + lax.div(i, 4))
+                    big.s4(1 + n)
+            attend_blocks(g, (2 * b, 2 * b + 1), qkv, pkv, ctx, lse)
             return inner
 
-        return lax.fori_loop(0, 8, block, carry)
+        return lax.fori_loop(0, 4, block, carry)
 
     lax.fori_loop(0, 3, group, 0)
     keep(qkv.at[pl.ds(0, 3)], qkv_o)
@@ -654,34 +664,45 @@
     return pl.ds(pl.multiple_of(3072 + 1024 * g + start, 32), size)
 
 
-def back_block(g, b, wb, pkv, buf, lse, dk, dv, dpk, dpv):
-    ns, ps, near, far = window(b)
-    first_row = pl.multiple_of(b * 128, 128)
-    rows = pl.ds(first_row, 128)
-    nr, prow = pl.ds(ns, 256), pl.ds(ps, 160)
-    qrows, krows = qkv_rows(g, first_row, 128), qkv_rows(g, ns, 256)
-    for pr in range(2):
-        ln = pl.ds(128 * pr, 128)
-        qm = head_split(wb[qrows, 128 * pr:128 * pr + 128], 0.125)
-        dm = head_split(buf[3, rows, lane_block(256 * g + 128 * pr)], 1.0)
-        kn = wb[krows, 256 + 128 * pr:384 + 128 * pr]
-        kp = pkv[g, prow, 128 * pr:128 * pr + 128]
-        vn = wb[krows, 512 + 128 * pr:640 + 128 * pr]
-        vp = pkv[g, prow, 256 + 128 * pr:384 + 128 * pr]
-        ls = lse[(g * 2 + pr) * 8 + b]
-        pn = jnp.exp(jnp.where(near, mm_nt(kn, qm), -1e30) - ls)
-        pp = jnp.exp(jnp.where(far, mm_nt(kp, qm), -1e30) - ls)
-        dn = mm_nt(vn, dm)
-        dp = mm_nt(vp, dm)
-        rd = jnp.sum(pn * dn, axis=0, keepdims=True) + jnp.sum(pp * dp, axis=0, keepdims=True)
-        sn = (pn * (dn - rd)).astype(BF)
-        sp = (pp * (dp - rd)).astype(BF)
-        dk[nr, ln] += mm(sn, qm)
-        dpk[prow, ln] += mm(sp, qm)
-        dv[nr, ln] += mm(pn.astype(BF), dm)
-        dpv[prow, ln] += mm(pp.astype(BF), dm)
-        r = mm_tn(kn, sn) + mm_tn(kp, sp)
-        buf[g, rows, ln] = (head_join(r).T * 0.125).astype(BF)
+def back_blocks(g, blocks, wb, pkv, buf, lse, dk, dv, dpk, dpv):
+    parts = []
+    for b in blocks:
+        ns, ps, near, far = window(b)
+        first_row = pl.multiple_of(b * 128, 128)
+        rows, prow = pl.ds(first_row, 128), pl.ds(ps, 160)
+        qrows, krows = qkv_rows(g, first_row, 128), qkv_rows(g, ns, 256)
+        for pr in range(2):
+            parts.append(dict(
+                near=near, far=far, rows=rows, nr=pl.ds(ns, 256), prow=prow, ln=pl.ds(128 * pr, 128),
+                qm=head_split(wb[qrows, 128 * pr:128 * pr + 128], 0.125),
+                dm=head_split(buf[3, rows, lane_block(256 * g + 128 * pr)], 1.0),
+                kn=wb[krows, 256 + 128 * pr:384 + 128 * pr],
+                kp=pkv[g, prow, 128 * pr:128 * pr + 128],
+                vn=wb[krows, 512 + 128 * pr:640 + 128 * pr],
+                vp=pkv[g, prow, 256 + 128 * pr:384 + 128 * pr],
+                ls=lse[(g * 2 + pr) * 8 + b]))
+    for t in parts:
+        t["pn"] = jnp.exp(jnp.where(t["near"], mm_nt(t["kn"], t["qm"]), -1e30) - t["ls"])
+        t["pp"] = jnp.exp(jnp.where(t["far"], mm_nt(t["kp"], t["qm"]), -1e30) - t["ls"])
+    for t in parts:
+        t["dn"] = mm_nt(t["vn"], t["dm"])
+        t["dp"] = mm_nt(t["vp"], t["dm"])
+        t["gvn"] = mm(t["pn"].astype(BF), t["dm"])
+        t["gvp"] = mm(t["pp"].astype(BF), t["dm"])
+    for t in parts:
+        rd = jnp.sum(t["pn"] * t["dn"], axis=0, keepdims=True) + jnp.sum(t["pp"] * t["dp"], axis=0, keepdims=True)
+        t["sn"] = (t["pn"] * (t["dn"] - rd)).astype(BF)
+        t["sp"] = (t["pp"] * (t["dp"] - rd)).astype(BF)
+    for t in parts:
+        t["gkn"] = mm(t["sn"], t["qm"])
+        t["gkp"] = mm(t["sp"], t["qm"])
+        t["gq"] = (head_join(mm_tn(t["kn"], t["sn"]) + mm_tn(t["kp"], t["sp"])).T * 0.125).astype(BF)
+    for t in parts:
+        dk[t["nr"], t["ln"]] += t["gkn"]
+        dpk[t["prow"], t["ln"]] += t["gkp"]
+        dv[t["nr"], t["ln"]] += t["gvn"]
+        dpv[t["prow"], t["ln"]] += t["gvp"]
+        buf[g, t["rows"], t["ln"]] = t["gq"]
 
 
 def pool_back(g, conv, wb, kvf, dk, dv, dpk, dpv, buf, gconv):
@@ -711,9 +732,8 @@
     ((2, 3),), ((4, 0), (3, 2), (1, 5)), ((2, 4),), ((3, 3), (4, 1), (1, 6), (2, 5)), ((4, 2), (3, 4)), ((4, 3),),
 )
 LOOP_STEPS = {
-    0: ((1, 7),), 1: ((2, 6),), 2: ((3, 5),), 3: ((1, 8),), 4: ((2, 7), (4, 4)), 5: ((3, 6),), 7: ((2, 8),),
-    8: ((3, 7), (4, 5)), 9: ((1, 9),), 11: ((3, 8), (4, 6)), 13: ((2, 9), (4, 7)), 16: ((4, 8), (3, 9)), 17: ((1, 10),),
-    20: ((2, 10),), 21: ((4, 9),), 23: ((3, 10),),
+    0: ((1, 7),), 1: ((2, 6),), 2: ((3, 5), (4, 4)), 3: ((1, 8), (2, 7)), 4: ((3, 6),), 5: ((4, 5),), 6: ((1, 9), (2, 8), (3, 7)),
+    7: ((4, 6),), 8: ((3, 8),), 9: ((1, 10), (2, 9), (4, 7)), 11: ((2, 10), (3, 9), (4, 8)),
 }
 
 
@@ -721,12 +741,14 @@
     (tok_i, w_i, conv, vec, pre_i, first_i, acc_i, dbr_i, gp_i, qkv_i, pkv_i, ctx_i, lse_i, gsm_in) = refs[:14]
     if comm:
         (gwd_i, gtok_o, fin, tot,
-         wb, buf, xb, db, tr, acc, gtok, pkv, lse, kvf, dk, dv, dpk, dpv, isem, osem,
+         wb, buf, xb, db, tr, acc, gtok, pkv, lse, kvf, isem, osem,
          gat, gconv, gbias, gbout, gsm, gbup, r0, r1a, r1b, r2, v, r3, own, pieces, small, t0, t1, t2,
          ks, kr, xs, xr, zs, zr, ls, ss, sr) = refs[14:]
     else:
         (gtok_o, gat, gconv, gbias, gbout, gsm, gbup,
-         wb, buf, xb, db, tr, acc, gtok, pkv, lse, kvf, dk, dv, dpk, dpv, isem, osem) = refs[14:]
+         wb, buf, xb, db, tr, acc, gtok, pkv, lse, kvf, isem, osem) = refs[14:]
+    dk, dv = acc.at[:, pl.ds(0, 256)], acc.at[:, pl.ds(256, 256)]
+    dpk, dpv = acc.at[pl.ds(0, 256), pl.ds(512, 256)], acc.at[pl.ds(256, 256), pl.ds(512, 256)]
     loads = {}
 
     def load(name, src, dst):
@@ -857,19 +879,16 @@
     run(14)
 
     def group(g, carry):
-        dk[...] = jnp.zeros_like(dk)
-        dv[...] = jnp.zeros_like(dv)
-        dpk[...] = jnp.zeros_like(dpk)
-        dpv[...] = jnp.zeros_like(dpv)
+        acc[...] = jnp.zeros_like(acc)
 
         def block(b, inner):
             if comm:
                 for i, steps in LOOP_STEPS.items():
-                    pl.when(8 * g + b == i)(functools.partial(take, steps))
-            back_block(g, b, wb, pkv, buf, lse, dk, dv, dpk, dpv)
+                    pl.when(4 * g + b == i)(functools.partial(take, steps))
+            back_blocks(g, (2 * b, 2 * b + 1), wb, pkv, buf, lse, dk, dv, dpk, dpv)
             return inner
 
-        lax.fori_loop(0, 8, block, 0)
+        lax.fori_loop(0, 4, block, 0)
         pool_back(g, conv, wb, kvf, dk, dv, dpk, dpv, buf, gconv)
         if comm:
             big.across(4 + g, gat.at[0]).wait_send()
@@ -906,12 +925,13 @@
         for t in range(5)], 48, 1536)
     small[...] = pieces[...].reshape(2, 2, 2, 96, 128)
     tiny.s0()
+    take(((3, 10),))
     token_part(0)
     tiny.s1()
     take(((2, 11),))
     token_part(1)
     tiny.s2()
-    take(((3, 11),))
+    take(((4, 9), (3, 11)))
     token_part(2)
     take(((4, 10),))
     token_part(3)
@@ -932,8 +952,7 @@
         pltpu.VMEM((6144, 768), BF), pltpu.VMEM((4, 1024, 768), BF), pltpu.VMEM((1024, 768), BF), pltpu.VMEM((1024, 768), BF),
         pltpu.VMEM((768, 1024), BF), pltpu.VMEM((1024, 768), F32), pltpu.VMEM((1024, 768), F32),
         pltpu.VMEM((3, 256, 512), BF), pltpu.VMEM((48, 1, 256), F32),
-        pltpu.VMEM((4, 1040, 128), F32), pltpu.VMEM((1024, 256), F32), pltpu.VMEM((1024, 256), F32),
-        pltpu.VMEM((256, 256), F32), pltpu.VMEM((256, 256), F32), DMA((120,)), DMA((4,)),
+        pltpu.VMEM((4, 1040, 128), F32), DMA((120,)), DMA((4,)),
     ]
     ins = [ANY] * len(args)
     for i in (2, 3, 13):

time: 217 us -> 204 us (0.940)
  Pallas kernels: 212 us -> 199 us
    pallas_call x1, Pallas kernels: 108 us -> 95.9 us  [backward_call(): pl.pallas_call(functools.partial(backward_kernel, comm), in_specs=ins, ou...]
where the time goes in v4:
time: 204 us; the launch traced here: 200 us
  Pallas kernels  199 us (98%)
    pallas_call x1, Pallas kernels, forward_call(): pl.pallas_call(functools.partial(forward_kernel, comm), in_specs=ins, out...  97.4 us
    pallas_call x1, Pallas kernels, backward_call(): pl.pallas_call(functools.partial(backward_kernel, comm), in_specs=ins, ou...  95.9 us
    pallas_call x1, Pallas kernels, finish_call(): pl.pallas_call(finish_kernel, grid=(4,), in_specs=[part, part, full((12,...  5.71 us

profile of v4, /device:TPU:0, one launch (start us, length us, event | category | flops | bytes accessed | tf_op | source)
XLA Modules:
  0.0 200.2 jit_solution(10974159129210628564)
XLA Ops:
  0.7 97.4 %forward.1 = (bf16[1024,768]{1,0:T(8,128)(2,1)}, f32[1024,768]{1,0:T(8,128)}, bf16[1024,768]{1,0:T(8,128)(2,1)}, f32[1024,768]{1,0:T(8,128)}, bf16[1024,768]{1,0...) custom-call(bf16[1024,768]{1,0:T(8,128)(2,1)} %bitcast.24, ...), custom_call_target="tpu_custom_call" | custom-call | tf_op jit(solution)/shard_map/forward/pallas_call | solution.py:658
  98.0 95.9 %backward.1 = (f32[1024,768]{1,0:T(8,128)}, f32[12,24,768]{2,1,0:T(8,128)}, f32[24,128]{1,0:T(8,128)}) custom-call(bf16[1024,768]{1,0:T(8,128)(2,1)} %bitcast.25, bf16[12,2,2,2,96,768]{5,4,3,2,1,0:T(8,128)(2,1)} %get-tuple-element.49.refs_1_, f32[3,8,512]{2,1,0:T(8,128)} %get-tuple-element.50.refs_2_, f32[8,768]{1,0:T(8,128)} %get-tuple-element.51.refs_3_, ...), custom_call_target="tpu_custom_call" | custom-call | tf_op jit(solution)/shard_map/backward/pallas_call | solution.py:977
  194.0 5.7 %finish.1 = (bf16[1024,768]{1,0:T(8,128)(2,1)}, f32[1024,768]{1,0:T(8,128)}, f32[24,2304]{1,0:T(8,128)}, f32[1,72]{1,0:T(1,128)}, f32[5,48]{1,0:T(8,128)}, /*ind...) custom-call(bf16[1024,768]{1,0:T(8,128)(2,1)} %get-tuple-element.48., ...), custom_call_target="tpu_custom_call" | custom-call | tf_op jit(solution)/shard_map/finish/pallas_call | solution.py:1010

commit v5 on v4

--- a/solution.py
+++ b/solution.py
@@ -186,14 +186,51 @@
     def s5(self, c):
         self.across(c, True).wait_recv()
 
-    def sent(self, count):
-        def one(c, carry):
-            for dz in (1, 2, 3):
-                self.along_z(c, dz).wait_send()
-            for copy in self.first(c) + self.second(c) + (self.across(c),):
-                copy.wait_send()
-            return carry
-        lax.fori_loop(0, count, one, 0)
+    def sent(self, c):
+        for dz in (1, 2, 3):
+            self.along_z(c, dz).wait_send()
+        for copy in self.first(c) + self.second(c) + (self.across(c),):
+            copy.wait_send()
+
+
+class PlaneFirst:
+    def __init__(self, gather, c, group, sems):
+        self.g, self.p, self.c, self.group = gather, gather.p, c, group
+        self.ps, self.pr, self.zs, self.zr = sems
+
+    def plane(self, arriving=False):
+        p, me, out = self.p, 2 * self.p.y + self.p.x, []
+        for n, (dp, other) in enumerate(((p.xn, me + 1 - 2 * p.x), (p.yn, me + 2 - 4 * p.y), (p.diag, 3 - me))):
+            out.append(p.copy(self.group.at[p.z, me], self.group.at[p.z, other if arriving else me], self.ps.at[n], self.pr.at[n],
+                              dp=dp))
+        return out
+
+    def along_z(self, arriving=False):
+        p = self.p
+        return [p.copy(self.group.at[p.z], self.group.at[p.up(4 - dz) if arriving else p.z], self.zs.at[dz - 1],
+                       self.zr.at[dz - 1], z=p.up(dz)) for dz in (1, 2, 3)]
+
+    def s1(self, slab):
+        self.group[self.p.z, 2 * self.p.y + self.p.x] = slab
+        for copy in self.plane():
+            copy.start()
+
+    def s2(self):
+        for copy in self.plane(True):
+            copy.wait_recv()
+        for copy in self.along_z():
+            copy.start()
+
+    def s3(self):
+        for copy in self.along_z(True):
+            copy.wait_recv()
+        for n in range(4):
+            self.g.dense[self.c, n // 2, n % 2, self.p.k] = rows_of(self.group[:, n]).reshape(96, 768).astype(BF)
+        self.g.across(self.c).start()
+
+    def sent(self):
+        for copy in self.plane() + self.along_z() + [self.g.across(self.c)]:
+            copy.wait_send()
 
 
 class SmallGather:
@@ -457,20 +494,20 @@
 def forward_kernel(comm, *refs):
     if comm:
         (tok, wqkv, bq_own, cv_own, wout, *six, wup, bu_own, wdn, pos, cot,
-         out_o, pre_o, first_o, acc_o, dbr_o, gp_o, gwd_o, qkv_o, pkv_o, ctx_o, lse_o, gsm, w_o, conv, vec,
-         w, buf, act, gp, acc, pre, first, dbr, tr, ctx, pkv, lse, out, kvf, stage, sems, osem,
-         slab, slab_s, dense_s, pieces, bqkv, bup,
-         zs, zr, xs, xr, ks, kr, ss, sr) = refs
+         out_o, pre_o, tokt_o, firstt_o, acc_o, dbr_o, gp_o, gwd_o, qkv_o, pkv_o, ctx_o, lse_o, gsm, w_o, conv, vec,
+         w, buf, act, gp, acc, pre, first, dbr, tr, tokt, ctx, pkv, lse, out, kvf, stage, sems, osem,
+         slab, slab_s, dense_s, pieces, bqkv, bup, plane,
+         zs, zr, xs, xr, ks, kr, ss, sr, ps0, ps1, ps2, ps3) = refs
     else:
         (tok, w_in, bqkv, conv, vec, bup, pos, cot,
-         out_o, pre_o, first_o, acc_o, dbr_o, gp_o, gwd_o, qkv_o, pkv_o, ctx_o, lse_o, gsm,
-         w, buf, act, gp, acc, pre, first, dbr, tr, ctx, pkv, lse, out, kvf, stage, sems, osem) = refs
+         out_o, pre_o, tokt_o, firstt_o, acc_o, dbr_o, gp_o, gwd_o, qkv_o, pkv_o, ctx_o, lse_o, gsm,
+         w, buf, act, gp, acc, pre, first, dbr, tr, tokt, ctx, pkv, lse, out, kvf, stage, sems, osem) = refs
     qkv = buf
     clear_edges(kvf)
-    kept = []
+    kept, number = [], iter(range(20))
 
     def keep(src, dst):
-        kept.append(pltpu.make_async_copy(src, dst, osem.at[len(kept)]))
+        kept.append(pltpu.make_async_copy(src, dst, osem.at[next(number)]))
         kept[-1].start()
 
     todo = []
@@ -478,31 +515,40 @@
         p = Place()
         big = Gather(p, slab, w, (zs, zr, xs, xr, ks, kr))
         tiny = SmallGather(p, slab_s, dense_s, ss, sr)
+        turned = PlaneFirst(big, 10, plane, (ps0, ps1, ps2, ps3))
         slab_s[p.z] = jnp.zeros((24, 128), F32)
         slab_s[p.z, 0:1, 0:72] = bq_own[...].astype(F32)
         slab_s[p.z, 1:6, 0:48] = cv_own[...].astype(F32)
         for i in range(6):
             slab_s[p.z, 6 + i:7 + i, 0:24] = six[i][...].astype(F32)
         slab_s[p.z, 12:13, 0:96] = bu_own[...].astype(F32)
-        for c in range(12):
+        p.greet()
+        tiny.s1()
+        for c in (0, 10, 1, 2, 3, 4, 5, 6, 7, 8, 9, 11):
             if c < 3:
                 rows24 = jnp.concatenate([wqkv[:, 768 * i + 256 * c:768 * i + 256 * c + 256] for i in range(3)], axis=1)
             elif c == 3:
                 rows24 = wout[...]
             else:
                 rows24 = (wup if c % 2 == 0 else wdn)[:, 768 * ((c - 4) // 2):768 * ((c - 4) // 2) + 768]
+            if c == 10:
+                turned.s1(slab_of(rows24.astype(F32)))
+                continue
             slab[c, p.z] = slab_of(rows24.astype(F32))
-            if c == 0:
-                p.greet()
-                tiny.s1()
-            big.s1(c)
+            if c < 3:
+                big.s1(c)
+        tokt[...] = tok[...].T
         tiny.s2()
+        big.s1(3)
         big.s2(0)
+        big.s1(4)
         big.s2(1)
         tiny.s3()
         big.s3(0)
+        big.s1(5)
         big.s2(2)
         big.s3(1)
+        big.s1(6)
         big.s2(3)
         big.s4(0)
         tiny.s4()
@@ -523,9 +569,12 @@
         for j in range(4):
             bup[j] = whole[:, 768 * j:768 * j + 768]
         big.s5(0)
-        todo = [[(big.s2, 10), (big.s3, 8)], [(big.s4, 7), (big.s2, 11)], [(big.s3, 9)], [(big.s4, 8), (big.s3, 10)],
-                [(big.s4, 9), (big.s3, 11)], [(big.s4, 10)], [(big.s4, 11)]]
+        todo = [[(big.s2, 8), (big.s3, 6)], [(big.s4, 5), (big.s2, 9)],
+                [(big.s3, 7)], [(big.s4, 6), (big.s2, 11)], [(big.s3, 8)], [(big.s4, 7)],
+                [(big.s3, 9)], [(big.s4, 8)], [(big.s3, 11)], [(big.s4, 9)],
+                [], [(lambda c: turned.s3(), 10)], [(big.s4, 11)]]
     else:
+        tokt[...] = tok[...].T
         load = pltpu.make_async_copy(w_in, w, sems.at[0])
         load.start()
         load.wait()
@@ -544,22 +593,28 @@
         def block(b, inner):
             if comm:
                 i = 4 * g + b
-                n = lax.div(i, 2)
-
-                @pl.when(lax.rem(i, 2) == 0)
+                n = lax.div(i, 3)
+
+                @pl.when(lax.rem(i, 3) == 0)
                 def _():
+                    big.s1(7 + n + lax.div(n, 3))
                     big.s2(4 + n)
                     big.s3(2 + n)
 
-                @pl.when(lax.rem(i, 2) == 1)
+                @pl.when(lax.rem(i, 3) == 2)
                 def _():
                     big.s4(1 + n)
+
+                @pl.when(i == 10)
+                def _():
+                    turned.s2()
             attend_blocks(g, (2 * b, 2 * b + 1), qkv, pkv, ctx, lse)
             return inner
 
         return lax.fori_loop(0, 4, block, carry)
 
     lax.fori_loop(0, 3, group, 0)
+    keep(tokt, tokt_o)
     keep(qkv.at[pl.ds(0, 3)], qkv_o)
     keep(pkv, pkv_o)
     keep(ctx, ctx_o)
@@ -578,18 +633,22 @@
         acc[rows, :] = low.astype(F32) + b_down
         progress()
     keep(pre, pre_o)
-    keep(first, first_o)
+    tr[...] = first[...].T
+    keep(tr, firstt_o)
+    first_kept = len(kept) - 1
     for j in range(4):
         if comm:
             big.s5(4 + 2 * j)
+        for rows in tiles:
+            value, slope = gelu_both(mm(first[rows, :], weight(w, 4 + 2 * j)) + bup[j])
+            act[j, rows, :] = value.astype(BF)
+            gp[j, rows, :] = slope.astype(BF)
+            progress()
+        if comm:
             big.s5(5 + 2 * j)
             keep(w.at[pl.ds(4 + 2 * j, 2)], w_o.at[pl.ds(4 + 2 * j, 2)])
         for rows in tiles:
-            value, slope = gelu_both(mm(first[rows, :], weight(w, 4 + 2 * j)) + bup[j])
-            low = value.astype(BF)
-            act[j, rows, :] = low
-            gp[j, rows, :] = slope.astype(BF)
-            acc[rows, :] += mm_nt(low, weight(w, 5 + 2 * j))
+            acc[rows, :] += mm_nt(act[j, rows, :], weight(w, 5 + 2 * j))
             progress()
         keep(gp.at[j], gp_o.at[j])
     sums = [jnp.zeros((1, 768), F32) for _ in range(3)]
@@ -611,6 +670,7 @@
     keep(out, out_o)
     keep(dbr, dbr_o)
     keep(acc, acc_o)
+    kept.pop(first_kept).wait()
     tr[...] = dbr[...].T
     sent = []
     for j in range(4):
@@ -624,13 +684,15 @@
     for copy in kept:
         copy.wait()
     if comm:
-        big.sent(12)
+        for c in range(12):
+            (turned.sent() if c == 10 else big.sent(c))
         tiny.sent()
 
 
 def forward_call(comm, *args):
     outs = [
-        (struct((1024, 768), BF), ANY), (struct((1024, 768), F32), ANY), (struct((1024, 768), BF), ANY),
+        (struct((1024, 768), BF), ANY), (struct((1024, 768), F32), ANY), (struct((768, 1024), BF), ANY),
+        (struct((768, 1024), BF), ANY),
         (struct((1024, 768), F32), ANY), (struct((1024, 768), BF), ANY), (struct((4, 1024, 768), BF), ANY),
         (struct((4, 2, 2, 2, 96, 768), BF), ANY), (struct((3, 1024, 768), BF), ANY), (struct((3, 256, 512), BF), ANY),
         (struct((1024, 768), BF), ANY), (struct((48, 1, 256), F32), ANY), (struct((8, 768), F32), VM),
@@ -638,7 +700,8 @@
     scratch = [
         pltpu.VMEM((12, 2, 2, 2, 96, 768), BF), pltpu.VMEM((3, 1024, 768), BF), pltpu.VMEM((4, 1024, 768), BF),
         pltpu.VMEM((4, 1024, 768), BF), pltpu.VMEM((1024, 768), F32), pltpu.VMEM((1024, 768), F32),
-        pltpu.VMEM((1024, 768), BF), pltpu.VMEM((1024, 768), BF), pltpu.VMEM((768, 1024), BF), pltpu.VMEM((1024, 768), BF),
+        pltpu.VMEM((1024, 768), BF), pltpu.VMEM((1024, 768), BF), pltpu.VMEM((768, 1024), BF), pltpu.VMEM((768, 1024), BF),
+        pltpu.VMEM((1024, 768), BF),
         pltpu.VMEM((3, 256, 512), BF), pltpu.VMEM((48, 1, 256), F32), pltpu.VMEM((1024, 768), BF),
         pltpu.VMEM((4, 1040, 128), F32), pltpu.VMEM((2, 2, 2, 2, 96, 768), BF), DMA((2,)), DMA((20,)),
     ]
@@ -647,7 +710,9 @@
         scratch += [
             pltpu.VMEM((12, 4, 16, 1152), BF), pltpu.VMEM((4, 24, 128), F32), pltpu.VMEM((2, 2, 2, 4, 24, 128), F32),
             pltpu.VMEM((32, 24, 128), F32), pltpu.VMEM((3, 1, 768), F32), pltpu.VMEM((4, 1, 768), F32),
+            pltpu.VMEM((4, 4, 16, 1152), BF),
             DMA((12, 3)), DMA((12, 3)), DMA((12, 4)), DMA((12, 4)), DMA((12,)), DMA((12,)), DMA((7,)), DMA((7,)),
+            DMA((3,)), DMA((3,)), DMA((3,)), DMA((3,)),
         ]
         params = pltpu.CompilerParams(vmem_limit_bytes=LIMIT, collective_id=1, has_side_effects=True)
     else:
@@ -728,17 +793,17 @@
 
 
 STEPS = (
-    ((1, 0),), (), ((1, 1),), ((2, 0),), ((1, 2),), ((2, 1),), ((3, 0), (1, 3)), ((2, 2),), ((3, 1), (1, 4)),
-    ((2, 3),), ((4, 0), (3, 2), (1, 5)), ((2, 4),), ((3, 3), (4, 1), (1, 6), (2, 5)), ((4, 2), (3, 4)), ((4, 3),),
+    (), ((1, 0),), (), ((1, 1),), (), ((1, 2), (2, 0)), (), ((1, 3), (2, 1)), (), ((1, 4), (2, 2), (3, 0)), (),
+    ((1, 5), (2, 3), (3, 1)), (), ((1, 6), (2, 4), (3, 2), (4, 0)), ((4, 1),),
 )
 LOOP_STEPS = {
-    0: ((1, 7),), 1: ((2, 6),), 2: ((3, 5), (4, 4)), 3: ((1, 8), (2, 7)), 4: ((3, 6),), 5: ((4, 5),), 6: ((1, 9), (2, 8), (3, 7)),
-    7: ((4, 6),), 8: ((3, 8),), 9: ((1, 10), (2, 9), (4, 7)), 11: ((2, 10), (3, 9), (4, 8)),
+    0: ((2, 5), (3, 3)), 1: ((1, 7), (2, 6)), 2: ((3, 4), (4, 2)), 3: ((1, 8), (3, 5), (4, 3)), 4: ((2, 7),), 5: ((3, 6), (4, 4)),
+    6: ((1, 9), (2, 8)), 7: ((4, 5),), 8: ((3, 7),), 9: ((1, 10), (2, 9), (4, 6)), 10: ((3, 8), (4, 7)), 11: ((2, 10), (3, 9), (4, 8)),
 }
 
 
 def backward_kernel(comm, *refs):
-    (tok_i, w_i, conv, vec, pre_i, first_i, acc_i, dbr_i, gp_i, qkv_i, pkv_i, ctx_i, lse_i, gsm_in) = refs[:14]
+    (tokt_i, w_i, conv, vec, pre_i, firstt_i, acc_i, dbr_i, gp_i, qkv_i, pkv_i, ctx_i, lse_i, gsm_in) = refs[:14]
     if comm:
         (gwd_i, gtok_o, fin, tot,
          wb, buf, xb, db, tr, acc, gtok, pkv, lse, kvf, isem, osem,
@@ -771,7 +836,8 @@
     load(("gp", 0), gp_i.at[0], buf.at[0])
     load_weight(4, 0)
     load("acc", acc_i, acc)
-    load("first", first_i, xb)
+    load("first", firstt_i, tr)
+    load("tok", tokt_i, xb)
     if comm:
         p = Place()
         big = Scatter(p, r0, r1a, r1b, r2, v, r3, fin, (ks, kr, xs, xr, zs, zr))
@@ -814,9 +880,6 @@
     gbup[...] = jnp.zeros_like(gbup)
     gsm[...] = gsm_in[...]
     tiles = [pl.ds(512 * r, 512) for r in range(2)]
-    loads["first"].wait()
-    tr[...] = xb[...].T
-    load("tok", tok_i, xb)
     loads["dbr"].wait()
     for j in range(4):
         have_weight(5 + 2 * j)
@@ -831,6 +894,8 @@
                     loads["acc"].wait()
             acc[rows, :] += mm_nt(low, slot(2 * j))
             run(3 * j + r)
+        if j == 0:
+            loads["first"].wait()
         gat[j] = mm(tr[...], buf[j]).astype(BF).reshape(BLOCKS)
         if comm:
             big.across(4 + j, gat.at[j]).start()
@@ -870,7 +935,6 @@
         big.across(8, gat.at[4]).start()
         run(13)
     loads["tok"].wait()
-    tr[...] = xb[...].T
     loads["pkv"].wait()
     loads["lse"].wait()
     for g in range(3):
@@ -892,7 +956,7 @@
         pool_back(g, conv, wb, kvf, dk, dv, dpk, dpv, buf, gconv)
         if comm:
             big.across(4 + g, gat.at[0]).wait_send()
-        gat[g if comm else 5 + g] = mm(tr[...], buf[g]).astype(BF).reshape(BLOCKS)
+        gat[g if comm else 5 + g] = mm(xb[...], buf[g]).astype(BF).reshape(BLOCKS)
         if comm:
             big.across(9 + g, gat.at[g]).start()
         gbias[g] = colsum(buf[g].astype(F32))
@@ -949,7 +1013,7 @@
 
 def backward_call(comm, *args):
     scratch = [
-        pltpu.VMEM((6144, 768), BF), pltpu.VMEM((4, 1024, 768), BF), pltpu.VMEM((1024, 768), BF), pltpu.VMEM((1024, 768), BF),
+        pltpu.VMEM((6144, 768), BF), pltpu.VMEM((4, 1024, 768), BF), pltpu.VMEM((768, 1024), BF), pltpu.VMEM((1024, 768), BF),
         pltpu.VMEM((768, 1024), BF), pltpu.VMEM((1024, 768), F32), pltpu.VMEM((1024, 768), F32),
         pltpu.VMEM((3, 256, 512), BF), pltpu.VMEM((48, 1, 256), F32),
         pltpu.VMEM((4, 1040, 128), F32), DMA((120,)), DMA((4,)),
@@ -1002,13 +1066,13 @@
 def finish_call(*args):
     shapes = ((24, 2304), (1, 72), (5, 48), (24, 768), (1, 24), (1, 24), (1, 24), (24, 3072), (1, 96),
               (24, 3072), (1, 24), (1, 24), (1, 24))
-    part = pl.BlockSpec((256, 768), lambda n: (n, 0))
+    part = pl.BlockSpec((512, 768), lambda n: (n, 0))
 
     def full(shape):
         return pl.BlockSpec(shape, lambda n: (0,) * len(shape))
 
     return pl.pallas_call(
-        finish_kernel, grid=(4,), in_specs=[part, part, full((12, 24, 768)), full((24, 128))],
+        finish_kernel, grid=(2,), in_specs=[part, part, full((12, 24, 768)), full((24, 128))],
         out_specs=[part, part] + [full(s) for s in shapes],
         out_shape=[struct((1024, 768), BF), struct((1024, 768), F32)] + [struct(s, F32) for s in shapes],
         name="finish")(*args)
@@ -1017,10 +1081,10 @@
 def shards_direct(tokens, w_qkv, b_qkv, conv_kv, w_out, b_out, gain_one, shift_one, w_up, b_up, w_down, b_down, gain_two,
                   shift_two, positions, cotangent):
     tok = tokens[0]
-    out, pre, first, acc, dbr, gp, gwd, qkv, pkv, ctx, lse, gsm, w, conv, vec = forward_call(
+    out, pre, tokt, firstt, acc, dbr, gp, gwd, qkv, pkv, ctx, lse, gsm, w, conv, vec = forward_call(
         True, tok, w_qkv, b_qkv[None], conv_kv, w_out.T, b_out[None], gain_one[None], shift_one[None], b_down[None],
         gain_two[None], shift_two[None], w_up, b_up[None], w_down.T, positions, cotangent[0])
-    gtok, fin, tot = backward_call(True, tok, w, conv, vec, pre, first, acc, dbr, gp, qkv, pkv, ctx, lse, gsm, gwd)
+    gtok, fin, tot = backward_call(True, tokt, w, conv, vec, pre, firstt, acc, dbr, gp, qkv, pkv, ctx, lse, gsm, gwd)
     (out, gtok, gqkv, gqb, gcv, gwo, gbo, gg1, gs1, gwu, gbu, gwd, gbd, gg2, gs2) = finish_call(out, gtok, fin, tot)
     return (out[None], gtok[None], gqkv, gqb[0], gcv, gwo.T, gbo[0], gg1[0], gs1[0], gwu, gbu[0], gwd.T, gbd[0], gg2[0], gs2[0])
 
@@ -1056,11 +1120,11 @@
     conv = jnp.concatenate([by_group(p, 2) for p in parts[1:6]] + [jnp.zeros((3, 3, 512), F32)], 1)
     vec = jnp.stack(parts[6:12] + [jnp.zeros((768,), F32)] * 2)
     bup = parts[12].reshape(4, 1, 768)
-    out, pre, first, acc, dbr, gp, gwd, qkv, pkv, ctx, lse, gsm = forward_call(
+    out, pre, tokt, firstt, acc, dbr, gp, gwd, qkv, pkv, ctx, lse, gsm = forward_call(
         False, tokens[0], w, bqkv, conv, vec, bup, positions, cotangent[0])
     gwd = lax.psum_scatter(gwd.reshape(4, 768, 768), AXES, scatter_dimension=1, tiled=True).astype(F32)
     gtok, gat, gconv, gbias, gbout, gsm, gbup = backward_call(
-        False, tokens[0], w, conv, vec, pre, first, acc, dbr, gp, qkv, pkv, ctx, lse, gsm)
+        False, tokt, w, conv, vec, pre, firstt, acc, dbr, gp, qkv, pkv, ctx, lse, gsm)
     gat = lax.psum_scatter(gat.reshape(8, 768, 768), AXES, scatter_dimension=1, tiled=True).astype(F32)
     flat = [gbias.reshape(3, 3, 256).transpose(1, 0, 2).reshape(count, -1)]
     flat += [gconv[:, t].reshape(3, 2, 256).transpose(1, 0, 2).reshape(count, -1) for t in range(5)]

time: 204 us -> 196 us (0.961)
  Pallas kernels: 199 us -> 191 us
    pallas_call x1, Pallas kernels: 97.4 us -> 91 us  [forward_call(): pl.pallas_call(functools.partial(forward_kernel, comm), in_specs=ins, out...]
where the time goes in v5:
time: 196 us; the launch traced here: 192 us
  Pallas kernels  191 us (97%)
    pallas_call x1, Pallas kernels, backward_call(): pl.pallas_call(functools.partial(backward_kernel, comm), in_specs=ins, ou...  95 us
    pallas_call x1, Pallas kernels, forward_call(): pl.pallas_call(functools.partial(forward_kernel, comm), in_specs=ins, out...  91 us
    pallas_call x1, Pallas kernels, finish_call(): pl.pallas_call(finish_kernel, grid=(2,), in_specs=[part, part, full((12,...  4.67 us

profile of v5, /device:TPU:0, one launch (start us, length us, event | category | flops | bytes accessed | tf_op | source)
XLA Modules:
  0.0 191.8 jit_solution(3843092791613207997)
XLA Ops:
  0.7 91.0 %forward.1 = (bf16[1024,768]{1,0:T(8,128)(2,1)}, f32[1024,768]{1,0:T(8,128)}, bf16[768,1024]{1,0:T(8,128)(2,1)}, bf16[768,1024]{1,0:T(8,128)(2,1)}, f32[1024,768...) custom-call(bf16[1024,768]{1,0:T(8,128)(2,1)} %bitcast.24, ...), custom_call_target="tpu_custom_call" | custom-call | tf_op jit(solution)/shard_map/forward/pallas_call | solution.py:723
  91.7 95.0 %backward.1 = (f32[1024,768]{1,0:T(8,128)}, f32[12,24,768]{2,1,0:T(8,128)}, f32[24,128]{1,0:T(8,128)}) custom-call(bf16[768,1024]{1,0:T(8,128)(2,1)} %get-tuple-element.50.refs_0_, bf16[12,2,2,2,96,768]{5,4,3,2,1,0:T(8,128)(2,1)} %get-tuple-element.51.refs_1_, f32[3,8,512]{2,1,0:T(8,128)} %get-tuple-element.52.refs_2_, f32[8,768]{1,0:T(8,128)} %get-tuple-element.53.refs_3_, ...), custom_call_target="tpu_custom_call" | custom-call | tf_op jit(solution)/shard_map/backward/pallas_call | solution.py:1041
  186.7 4.7 %finish.1 = (bf16[1024,768]{1,0:T(8,128)(2,1)}, f32[1024,768]{1,0:T(8,128)}, f32[24,2304]{1,0:T(8,128)}, f32[1,72]{1,0:T(1,128)}, f32[5,48]{1,0:T(8,128)}, /*ind...) custom-call(bf16[1024,768]{1,0:T(8,128)(2,1)} %get-tuple-element.49., ...), custom_call_target="tpu_custom_call" | custom-call | tf_op jit(solution)/shard_map/finish/pallas_call | solution.py:1074

commit v6 on v5

--- a/solution.py
+++ b/solution.py
@@ -834,10 +834,6 @@
     load("dbr", dbr_i, db)
     load_weight(5, 1)
     load(("gp", 0), gp_i.at[0], buf.at[0])
-    load_weight(4, 0)
-    load("acc", acc_i, acc)
-    load("first", firstt_i, tr)
-    load("tok", tokt_i, xb)
     if comm:
         p = Place()
         big = Scatter(p, r0, r1a, r1b, r2, v, r3, fin, (ks, kr, xs, xr, zs, zr))
@@ -847,10 +843,9 @@
         def fetch(c):
             return pltpu.make_async_copy(gwd_i.at[c, :, :, p.k], own.at[c % 2], ls.at[c % 2])
 
-        for c in range(4):
-            big.across(c, gwd_i.at[c]).start()
+        big.across(0, gwd_i.at[0]).start()
         fetch(0).start()
-        fetch(1).start()
+        big.across(1, gwd_i.at[1]).start()
 
         def take(steps):
             for stage, c in steps:
@@ -869,13 +864,27 @@
         if comm:
             take(STEPS[n])
 
-    for j in range(1, 4):
-        load_weight(5 + 2 * j, 1 + 2 * j)
-        load(("gp", j), gp_i.at[j], buf.at[j])
-        load_weight(4 + 2 * j, 2 * j)
-    load("pre", pre_i, gtok)
-    load("pkv", pkv_i, pkv)
-    load("lse", lse_i, lse)
+    load_weight(4, 0)
+    load("acc", acc_i, acc)
+
+    def load_next(j):
+        if j == 0:
+            load("first", firstt_i, tr)
+            if comm:
+                fetch(1).start()
+                big.across(2, gwd_i.at[2]).start()
+                big.across(3, gwd_i.at[3]).start()
+        if j < 3:
+            load_weight(7 + 2 * j, 3 + 2 * j)
+            load(("gp", j + 1), gp_i.at[j + 1], buf.at[j + 1])
+            load_weight(6 + 2 * j, 2 + 2 * j)
+        if j == 2:
+            load("tok", tokt_i, xb)
+        if j == 3:
+            load("pre", pre_i, gtok)
+            load("pkv", pkv_i, pkv)
+            load("lse", lse_i, lse)
+
     clear_edges(kvf)
     gbup[...] = jnp.zeros_like(gbup)
     gsm[...] = gsm_in[...]
@@ -884,6 +893,7 @@
     for j in range(4):
         have_weight(5 + 2 * j)
         loads["gp", j].wait()
+        load_next(j)
         for r, rows in enumerate(tiles):
             low = (mm(db[rows, :], slot(1 + 2 * j)) * buf[j, rows, :].astype(F32)).astype(BF)
             buf[j, rows, :] = low
@@ -981,6 +991,7 @@
             copy.wait()
         return
 
+    token_part(0)
     take(((1, 11),))
     kinds = [jnp.concatenate([gbias[g][:, 256 * i:256 * i + 256] for i in range(3) for g in range(3)], axis=1)]
     pack_small(pieces, 0, kinds, 72, 2304)
@@ -990,14 +1001,12 @@
     small[...] = pieces[...].reshape(2, 2, 2, 96, 128)
     tiny.s0()
     take(((3, 10),))
-    token_part(0)
+    token_part(1)
     tiny.s1()
-    take(((2, 11),))
-    token_part(1)
+    take(((2, 11), (4, 9)))
+    token_part(2)
     tiny.s2()
-    take(((4, 9), (3, 11)))
-    token_part(2)
-    take(((4, 10),))
+    take(((3, 11), (4, 10)))
     token_part(3)
     tot[...] = tiny.s3()
     take(((4, 11),))

time: 196 us -> 194 us (0.990)
  Pallas kernels: 191 us -> 189 us
where the time goes in v6:
time: 194 us; the launch traced here: 190 us
  Pallas kernels  189 us (97%)
    pallas_call x1, Pallas kernels, backward_call(): pl.pallas_call(functools.partial(backward_kernel, comm), in_specs=ins, ou...  93.1 us
    pallas_call x1, Pallas kernels, forward_call(): pl.pallas_call(functools.partial(forward_kernel, comm), in_specs=ins, out...  91 us
    pallas_call x1, Pallas kernels, finish_call(): pl.pallas_call(finish_kernel, grid=(2,), in_specs=[part, part, full((12,...  4.67 us

profile of v6, /device:TPU:0, one launch (start us, length us, event | category | flops | bytes accessed | tf_op | source)
XLA Modules:
  0.0 190.0 jit_solution(1188610295611821446)
XLA Ops:
  0.7 91.0 %forward.1 = (bf16[1024,768]{1,0:T(8,128)(2,1)}, f32[1024,768]{1,0:T(8,128)}, bf16[768,1024]{1,0:T(8,128)(2,1)}, bf16[768,1024]{1,0:T(8,128)(2,1)}, f32[1024,768...) custom-call(bf16[1024,768]{1,0:T(8,128)(2,1)} %bitcast.24, ...), custom_call_target="tpu_custom_call" | custom-call | tf_op jit(solution)/shard_map/forward/pallas_call | solution.py:723
  91.7 93.1 %backward.1 = (f32[1024,768]{1,0:T(8,128)}, f32[12,24,768]{2,1,0:T(8,128)}, f32[24,128]{1,0:T(8,128)}) custom-call(bf16[768,1024]{1,0:T(8,128)(2,1)} %get-tuple-element.50.refs_0_, bf16[12,2,2,2,96,768]{5,4,3,2,1,0:T(8,128)(2,1)} %get-tuple-element.51.refs_1_, f32[3,8,512]{2,1,0:T(8,128)} %get-tuple-element.52.refs_2_, f32[8,768]{1,0:T(8,128)} %get-tuple-element.53.refs_3_, ...), custom_call_target="tpu_custom_call" | custom-call | tf_op jit(solution)/shard_map/backward/pallas_call | solution.py:1050
  184.8 4.7 %finish.1 = (bf16[1024,768]{1,0:T(8,128)(2,1)}, f32[1024,768]{1,0:T(8,128)}, f32[24,2304]{1,0:T(8,128)}, f32[1,72]{1,0:T(1,128)}, f32[5,48]{1,0:T(8,128)}, /*ind...) custom-call(bf16[1024,768]{1,0:T(8,128)(2,1)} %get-tuple-element.49., ...), custom_call_target="tpu_custom_call" | custom-call | tf_op jit(solution)/shard_map/finish/pallas_call | solution.py:1083

commit v7 on v6

--- a/solution.py
+++ b/solution.py
@@ -510,6 +510,19 @@
         kept.append(pltpu.make_async_copy(src, dst, osem.at[next(number)]))
         kept[-1].start()
 
+    def early():
+        tokt[...] = tok[...].T
+        gsm[...] = jnp.zeros_like(gsm)
+
+        def part(r, carry):
+            row = 128 * r + lax.broadcasted_iota(jnp.int32, (128, 160), 0)
+            dy = mm((row == pos[...]).astype(BF), cot[...])
+            dbr[pl.ds(pl.multiple_of(128 * r, 128), 128), :] = dy.astype(BF)
+            gsm[4:5, :] += colsum(dy)
+            return carry
+
+        lax.fori_loop(0, 8, part, 0)
+
     todo = []
     if comm:
         p = Place()
@@ -537,7 +550,7 @@
             slab[c, p.z] = slab_of(rows24.astype(F32))
             if c < 3:
                 big.s1(c)
-        tokt[...] = tok[...].T
+        early()
         tiny.s2()
         big.s1(3)
         big.s2(0)
@@ -574,7 +587,7 @@
                 [(big.s3, 9)], [(big.s4, 8)], [(big.s3, 11)], [(big.s4, 9)],
                 [], [(lambda c: turned.s3(), 10)], [(big.s4, 11)]]
     else:
-        tokt[...] = tok[...].T
+        early()
         load = pltpu.make_async_copy(w_in, w, sems.at[0])
         load.start()
         load.wait()
@@ -651,22 +664,21 @@
             acc[rows, :] += mm_nt(act[j, rows, :], weight(w, 5 + 2 * j))
             progress()
         keep(gp.at[j], gp_o.at[j])
-    sums = [jnp.zeros((1, 768), F32) for _ in range(3)]
-    for r, rows in enumerate(tiles):
+
+    def last_norm(r, carry):
+        rows = pl.ds(pl.multiple_of(256 * r, 256), 256)
         xhat, rate = norm_stats(acc[rows, :])
         out[rows, :] = (xhat * gain2 + shift2).astype(BF)
-        row = 512 * r + lax.broadcasted_iota(jnp.int32, (512, 160), 0)
-        dy = mm((row == pos[...]).astype(BF), cot[...])
-        sums[1] = sums[1] + colsum(dy * xhat)
-        sums[2] = sums[2] + colsum(dy)
+        dy = dbr[rows, :].astype(F32)
+        gsm[3:4, :] += colsum(dy * xhat)
         dacc = norm_back(xhat, rate, gain2, dy)
         low = dacc.astype(BF)
         dbr[rows, :] = low
         acc[rows, :] = dacc
-        sums[0] = sums[0] + colsum(low.astype(F32))
-    gsm[...] = jnp.zeros_like(gsm)
-    for i in range(3):
-        gsm[2 + i:3 + i, :] = sums[i]
+        gsm[2:3, :] += colsum(low.astype(F32))
+        return carry
+
+    lax.fori_loop(0, 4, last_norm, 0)
     keep(out, out_o)
     keep(dbr, dbr_o)
     keep(acc, acc_o)

time: 194 us -> 194 us (level)
  no operation moved by 1% of the time
where the time goes in v7:
time: 194 us; the launch traced here: 190 us
  Pallas kernels  189 us (97%)
    pallas_call x1, Pallas kernels, backward_call(): pl.pallas_call(functools.partial(backward_kernel, comm), in_specs=ins, ou...  92.9 us
    pallas_call x1, Pallas kernels, forward_call(): pl.pallas_call(functools.partial(forward_kernel, comm), in_specs=ins, out...  91.3 us
    pallas_call x1, Pallas kernels, finish_call(): pl.pallas_call(finish_kernel, grid=(2,), in_specs=[part, part, full((12,...  4.67 us

profile of v7, /device:TPU:0, one launch (start us, length us, event | category | flops | bytes accessed | tf_op | source)
XLA Modules:
  0.0 189.8 jit_solution(18437148001972703429)
XLA Ops:
  0.7 91.3 %forward.1 = (bf16[1024,768]{1,0:T(8,128)(2,1)}, f32[1024,768]{1,0:T(8,128)}, bf16[768,1024]{1,0:T(8,128)(2,1)}, bf16[768,1024]{1,0:T(8,128)(2,1)}, f32[1024,768...) custom-call(bf16[1024,768]{1,0:T(8,128)(2,1)} %bitcast.24, ...), custom_call_target="tpu_custom_call" | custom-call | tf_op jit(solution)/shard_map/forward/pallas_call | solution.py:735
  92.0 92.9 %backward.1 = (f32[1024,768]{1,0:T(8,128)}, f32[12,24,768]{2,1,0:T(8,128)}, f32[24,128]{1,0:T(8,128)}) custom-call(bf16[768,1024]{1,0:T(8,128)(2,1)} %get-tuple-element.50.refs_0_, bf16[12,2,2,2,96,768]{5,4,3,2,1,0:T(8,128)(2,1)} %get-tuple-element.51.refs_1_, f32[3,8,512]{2,1,0:T(8,128)} %get-tuple-element.52.refs_2_, f32[8,768]{1,0:T(8,128)} %get-tuple-element.53.refs_3_, ...), custom_call_target="tpu_custom_call" | custom-call | tf_op jit(solution)/shard_map/backward/pallas_call | solution.py:1062
  184.9 4.7 %finish.1 = (bf16[1024,768]{1,0:T(8,128)(2,1)}, f32[1024,768]{1,0:T(8,128)}, f32[24,2304]{1,0:T(8,128)}, f32[1,72]{1,0:T(1,128)}, f32[5,48]{1,0:T(8,128)}, /*ind...) custom-call(bf16[1024,768]{1,0:T(8,128)(2,1)} %get-tuple-element.49., ...), custom_call_target="tpu_custom_call" | custom-call | tf_op jit(solution)/shard_map/finish/pallas_call | solution.py:1095
